TPU v7x, 128 devices: a whole 4x4x4 slice. The times are simulated.
128 devices in a mesh: dp: 8 (over x, y_hi), shard: 16 (over y_lo, z, core).
Axes of the slice: x: 4, y: 4 (y_hi: 2, y_lo: 2; y = y_hi * 2 + y_lo), z: 4, core: 2. Of those that a mesh axis runs over, the one named last changes fastest.
Arguments:
- frames: bfloat16 [256, 256, 2048], P(('dp', 'shard')), may hold values from -6 to 6
- crop_starts: int32 [256], P(('dp', 'shard')), may hold values from 0 to 128
- pairing: int32 [256], replicated, may hold values from 0 to 255, each once
- bias_table: float32 [8, 255], replicated, may hold values from -6 to 320, as said below
- input_master: float32 [2048, 3072], P('shard'), may hold values from -0.125 to 0.125
- input_moment: float32 [2048, 3072], P('shard'), may hold values from -3 to 3
- input_square: float32 [2048, 3072], P('shard'), may hold values from 0.01 to 1
- output_master: float32 [1024, 2048], P('shard'), may hold values from -0.1875 to 0.1875
- output_moment: float32 [1024, 2048], P('shard'), may hold values from -3 to 3
- output_square: float32 [1024, 2048], P('shard'), may hold values from 0.01 to 1
- gain_master: float32 [2048], P('shard'), may hold values from 0.5 to 1.5
- gain_moment: float32 [2048], P('shard'), may hold values from -3 to 3
- gain_square: float32 [2048], P('shard'), may hold values from 0.01 to 1
Outputs:
- pair_losses: float32 [256], P(('dp', 'shard'))
- input_updated: float32 [2048, 3072], P('shard')
- input_moments: float32 [2048, 3072], P('shard')
- input_squares: float32 [2048, 3072], P('shard')
- output_updated: float32 [1024, 2048], P('shard')
- output_moments: float32 [1024, 2048], P('shard')
- output_squares: float32 [1024, 2048], P('shard')
- gain_updated: float32 [2048], P('shard')
- gain_moments: float32 [2048], P('shard')
- gain_squares: float32 [2048], P('shard')
Inputs may be any that keep to these rules, and one draw needn't show every extreme that they name: `bias_table`: entry k of a head belongs to the offset k - (127) between the query's frame and the key's frame.
All inputs are finite; a program needn't handle non-finite values.
Results may differ from a plain program's by a relative error of at most 0.017.
Values may be sent and summed in bfloat16 or wider, within the bound.
A program may use at most 128 MiB of HBM per device.

v0:
```python
import jax
import jax.numpy as jnp
from jax import lax
from jax.sharding import PartitionSpec as P

D = 2048
HEADS = 8
HEAD_DIM = 128
INNER = 1024
CROP = 128


inv_tau = 20.0
norm_eps = 1e-05
embed_eps = 1e-06
beta_one = 0.9
beta_two = 0.999
adam_eps = 1e-08
learn_rate = 0.002
weight_decay = 0.1
adam_step = 1000


def band_bias(bias_table):
    span = (bias_table.shape[1] + 1) // 2
    flipped = bias_table[:, ::-1]
    tiled = jnp.tile(flipped, (1, span + 1))
    strip = tiled[:, span - 1 : span - 1 + span * (2 * span - 2)]
    return strip.reshape(bias_table.shape[0], span, 2 * span - 2)[:, :, :span]


def crop_block(segments, starts):

    def one_crop(segment, begin):
        return lax.dynamic_slice_in_dim(segment, begin, CROP, 0)

    return jax.vmap(one_crop)(segments, starts)


def adam_update(master, moment, square, gradient, decay):
    moment_new = beta_one * moment + (1.0 - beta_one) * gradient
    square_new = beta_two * square + (1.0 - beta_two) * gradient * gradient
    mean_hat = moment_new / (1.0 - beta_one**adam_step)
    square_hat = square_new / (1.0 - beta_two**adam_step)
    master_new = master - learn_rate * (
        mean_hat / (jnp.sqrt(square_hat) + adam_eps) + decay * master
    )
    return (master_new, moment_new, square_new)


def per_device(
    frames,
    crop_starts,
    pairing,
    bias_table,
    input_master,
    input_moment,
    input_square,
    output_master,
    output_moment,
    output_square,
    gain_master,
    gain_moment,
    gain_square,
):
    f32 = jnp.float32
    bf16 = jnp.bfloat16
    count_items = frames.shape[0]
    token_rows = count_items * CROP
    score_scale = HEAD_DIM ** (-0.5)
    band = band_bias(bias_table)
    input_w, output_w, gain_w = (
        lax.all_gather(input_master.astype(bf16), "shard", axis=0, tiled=True),
        lax.all_gather(output_master.astype(bf16), "shard", axis=0, tiled=True),
        lax.all_gather(gain_master.astype(bf16), "shard", axis=0, tiled=True),
    )
    crops = crop_block(frames, crop_starts)
    frames_f = crops.astype(f32)
    centred = frames_f - jnp.mean(frames_f, axis=-1, keepdims=True)
    normed = centred * lax.rsqrt(jnp.mean(centred * centred, axis=-1, keepdims=True) + norm_eps)
    hidden = (normed * gain_w.astype(f32)).astype(bf16).reshape(token_rows, D)
    packed = jnp.dot(hidden, input_w, preferred_element_type=f32).astype(bf16)
    packed = packed.reshape(count_items, CROP, 3, HEADS, HEAD_DIM)
    queries = packed[:, :, 0]
    key_heads = packed[:, :, 1]
    value_heads = packed[:, :, 2]
    scores = (
        jnp.einsum("bihd,bjhd->bhij", queries, key_heads, preferred_element_type=f32) * score_scale
        + band[None]
    )
    peak = jnp.max(scores, axis=-1, keepdims=True)
    raised = jnp.exp(scores - peak)
    probabilities = raised / jnp.sum(raised, axis=-1, keepdims=True)
    mixed_heads = jnp.einsum(
        "bhij,bjhd->bihd", probabilities.astype(bf16), value_heads, preferred_element_type=f32
    ).astype(bf16)
    attention = jnp.dot(
        mixed_heads.reshape(token_rows, INNER), output_w, preferred_element_type=f32
    )
    pooled = jnp.mean(frames_f, axis=1) + jnp.mean(attention.reshape(count_items, CROP, D), axis=1)
    norm_inv = lax.rsqrt(jnp.sum(pooled * pooled, axis=1, keepdims=True) + embed_eps)
    embedding = pooled * norm_inv
    first_item = lax.axis_index(("dp", "shard")) * count_items
    everyone = lax.all_gather(embedding, ("dp", "shard"), axis=0, tiled=True)
    total_items = everyone.shape[0]
    item_order = jnp.arange(total_items, dtype=jnp.int32)
    position = jnp.zeros((total_items,), jnp.int32).at[pairing].set(item_order)
    partner = pairing[jnp.bitwise_xor(position, 1)]
    own_partner = lax.dynamic_slice_in_dim(partner, first_item, count_items)
    target = (own_partner[:, None] == item_order[None, :]).astype(f32)
    all_sims = jnp.dot(everyone, everyone.T, precision=lax.Precision.HIGHEST) * inv_tau
    all_exponents = jnp.where(
        item_order[:, None] == item_order[None, :], 0.0, jnp.exp(all_sims - inv_tau)
    )
    column_totals = jnp.sum(all_exponents, axis=1)
    similarity = lax.dynamic_slice_in_dim(all_sims, first_item, count_items, 0)
    exponents = lax.dynamic_slice_in_dim(all_exponents, first_item, count_items, 0)
    totals = lax.dynamic_slice_in_dim(column_totals, first_item, count_items)
    pair_losses = jnp.log(totals) + inv_tau - jnp.sum(similarity * target, axis=1)
    weights = exponents / totals[:, None] + exponents / column_totals[None, :] - 2.0 * target
    grad_embedding = jnp.dot(weights, everyone, precision=lax.Precision.HIGHEST) * inv_tau
    grad_pooled = (
        grad_embedding - embedding * jnp.sum(embedding * grad_embedding, axis=1, keepdims=True)
    ) * norm_inv
    grad_frame = (grad_pooled / CROP).astype(bf16)
    mixed_sum = jnp.sum(mixed_heads, axis=1, dtype=f32).reshape(count_items, INNER)
    grad_output = jnp.dot(mixed_sum.T, grad_frame.astype(f32), precision=lax.Precision.HIGHEST)
    output_share = lax.psum_scatter(
        grad_output.astype(jnp.bfloat16), "shard", scatter_dimension=0, tiled=True
    )
    grad_mixed = lax.dot_general(
        grad_frame, output_w, (((1,), (1,)), ((), ())), preferred_element_type=f32
    ).astype(bf16)
    grad_mixed = grad_mixed.reshape(count_items, HEADS, HEAD_DIM)
    dprob = jnp.einsum("bjhd,bhd->bhj", value_heads, grad_mixed, preferred_element_type=f32)
    shifted = dprob[:, :, None, :] - jnp.sum(
        probabilities * dprob[:, :, None, :], axis=-1, keepdims=True
    )
    dscores = (probabilities * shifted * score_scale).astype(bf16)
    grad_queries = jnp.einsum(
        "bhij,bjhd->bihd", dscores, key_heads, preferred_element_type=f32
    ).astype(bf16)
    grad_keys = jnp.einsum("bhij,bihd->bjhd", dscores, queries, preferred_element_type=f32).astype(
        bf16
    )
    column_mass = jnp.transpose(jnp.sum(probabilities, axis=2), (0, 2, 1))
    grad_values = (column_mass[:, :, :, None] * grad_mixed.astype(f32)[:, None, :, :]).astype(bf16)
    grad_packed = jnp.stack([grad_queries, grad_keys, grad_values], axis=2).reshape(
        token_rows, 3 * INNER
    )
    grad_input = lax.dot_general(
        hidden, grad_packed, (((0,), (0,)), ((), ())), preferred_element_type=f32
    )
    grad_hidden = lax.dot_general(
        grad_packed, input_w, (((1,), (1,)), ((), ())), preferred_element_type=f32
    )
    grad_gain = jnp.sum(normed.reshape(token_rows, D) * grad_hidden, axis=0)
    input_share, gain_share = (
        lax.psum_scatter(
            grad_input.astype(jnp.bfloat16), "shard", scatter_dimension=0, tiled=True
        ).astype(jnp.float32),
        lax.psum_scatter(
            grad_gain.astype(jnp.bfloat16), "shard", scatter_dimension=0, tiled=True
        ).astype(jnp.float32),
    )
    input_total, output_total, gain_total = (
        lax.psum(input_share.astype(jnp.bfloat16), "dp").astype(jnp.float32),
        lax.psum(output_share, "dp").astype(jnp.float32),
        lax.psum(gain_share.astype(jnp.bfloat16), "dp").astype(jnp.float32),
    )
    input_new = adam_update(input_master, input_moment, input_square, input_total, weight_decay)
    output_new = adam_update(
        output_master, output_moment, output_square, output_total, weight_decay
    )
    gain_new = adam_update(gain_master, gain_moment, gain_square, gain_total, 0.0)
    return (
        pair_losses,
        input_new[0],
        input_new[1],
        input_new[2],
        output_new[0],
        output_new[1],
        output_new[2],
        gain_new[0],
        gain_new[1],
        gain_new[2],
    )


def solution(mesh):
    in_specs = (
        P(("dp", "shard"), None, None),
        P(("dp", "shard")),
        P(),
        P(),
        P("shard", None),
        P("shard", None),
        P("shard", None),
        P("shard", None),
        P("shard", None),
        P("shard", None),
        P("shard"),
        P("shard"),
        P("shard"),
    )
    out_specs = (
        P(("dp", "shard")),
        P("shard", None),
        P("shard", None),
        P("shard", None),
        P("shard", None),
        P("shard", None),
        P("shard", None),
        P("shard"),
        P("shard"),
        P("shard"),
    )
    return jax.shard_map(
        per_device, mesh=mesh, in_specs=in_specs, out_specs=out_specs, check_vma=False
    )
```

profile of v0, /device:TPU:1, one launch (start us, length us, event | category | flops | bytes accessed | tf_op | source)
XLA Modules:
  0.0 455.5 jit_solution(2447372812088447417)
XLA Ops:
  7.3 2.4 convert_element_type.127
  10.7 22.1 %all-gather = bf16[16,1,128]{2,1,0:T(2,128)(2,1)S(1)} all-gather(bf16[1,1,128]{2,1,0:T(2,128)(2,1)S(1)} %convert_bitcast_fusion), channel_id=1, replica_groups=mesh['dp'=8,'shard'=16] {'shard'}, dimensions={0}, use_global_device_ids=true | all-gather | bytes 4352 | tf_op jit(solution)/shard_map/all_gather | solution.py:75
  38.0 6.3 %while.1 = (s32[]{:T(128)}, bf16[2,256,2048]{2,1,0:T(8,128)(2,1)}, s32[2,3]{1,0:T(2,128)S(1)}, bf16[2,128,2048]{2,1,0:T(8,128)(2,1)S(1)}, s32[]{:T(128)}) while((s32[]{:T(128)}, bf16[2,256,2048]{2,1,0:T(8,128)(2,1)}, s32[2,3]{1,0:T(2,128)S(1)}, bf16[2,128,2048]{2,1,0:T(8,128)(2,1)S(1)}, s32[]{:T(128)}) %tuple.45), condition=%wide.while_cond, body=%wide.while_body.sunk | while | flops 2 | bytes 1048701 | solution.py:35
  38.7 2.5 dynamic-slice_dynamic-update-slice_fusion.2
  41.8 2.5 dynamic-slice_dynamic-update-slice_fusion.2
  46.8 39.1 %all-gather.6.cloned.1.call-done = bf16[2048,3072]{1,0:T(8,128)(2,1)} async-done(((bf16[128,3072]{1,0:T(8,128)(2,1)}), bf16[2048,3072]{1,0:T(8,128)(2,1)}) %all-gather.6.cloned.1.call-update) | async-done | bytes 12582928 | tf_op jit(solution)/shard_map/all_gather | solution.py:73
  85.9 8.6 %fusion.8 = bf16[32,8,24,128]{3,1,2,0:T(8,128)(2,1)S(1)} fusion(bf16[2048,3072]{1,0:T(8,128)(2,1)} %all-gather.6.cloned.1.call-done, f32[256,2048]{1,0:T(8,128)} %fusion.4, f32[2048]{0:T(1024)S(1)} %bitcast.90), kind=kOutput, calls=%fused_computation.27 | convolution fusion | flops 3223060480 | bytes 16261120 | tf_op jit(solution)/shard_map/dot_general | solution.py:82
  100.4 26.2 %all-gather.8.cloned.1.call-done = bf16[1024,2048]{1,0:T(8,128)(2,1)} async-done(((bf16[64,2048]{1,0:T(8,128)(2,1)}), bf16[1024,2048]{1,0:T(8,128)(2,1)}) %all-gather.8.cloned.1.call-update) | async-done | bytes 4194320 | tf_op jit(solution)/shard_map/all_gather | solution.py:74
  126.6 3.5 fusion.9
  132.7 1.9 gather_fusion
  134.7 61.7 %all-gather.10.cloned.1.call-done = f32[128,2,2048]{2,1,0:T(2,128)} async-done(((f32[1,2,2048]{2,1,0:T(2,128)}), f32[128,2,2048]{2,1,0:T(2,128)}) %all-gather.10.cloned.1.call-update) | async-done | bytes 2097168 | tf_op jit(solution)/shard_map/all_gather | solution.py:104
  196.4 2.7 reshape.228
  199.1 2.0 exponential_select_fusion
  203.1 5.1 %convolution_convert_fusion.2 = bf16[1024,2048]{1,0:T(8,128)(2,1)} fusion(f32[1,2,8,128]{3,2,1,0:T(8,128)S(1)} %bitcast.92, f32[2,2048]{1,0:T(2,128)S(1)} %get-tuple-element.72, f32[2,2048]{1,0:T(2,128)S(1)} %get-tuple-element.54, f32[2]{0:T(128)S(1)} %get-tuple-element.66, f32[2]{0:T(128)S(1)} %get-tuple-element.71, f32[2]{0:T(128)S(1)} %get-tuple-element.67), kind=kOutput, calls=%fused_computation.10 | convolution fusion | flops 52453376 | bytes 4235288 | tf_op jit(solution)/shard_map/dot_general | solution.py:127
  210.0 3.5 convolution_convert_fusion.6
  218.0 7.8 %convolution_convert_fusion = bf16[2048,3072]{1,0:T(8,128)(2,1)} fusion(bf16[256,2048]{1,0:T(8,128)(2,1)} %bitcast.87, bf16[256,3072]{1,0:T(8,128)(2,1)S(1)} %reshape.181), kind=kOutput, calls=%fused_computation.6 | convolution fusion | flops 3227516928 | bytes 15204352 | tf_op jit(solution)/shard_map/dot_general | solution.py:151
  227.6 40.6 %reduce-scatter.5.cloned.1.call-done = bf16[64,2048]{1,0:T(8,128)(2,1)} async-done(((bf16[1024,2048]{1,0:T(8,128)(2,1)}), bf16[64,2048]{1,0:T(8,128)(2,1)}) %reduce-scatter.5.cloned.1.call-update) | async-done | bytes 262160 | tf_op jit(solution)/shard_map/reduce_scatter | solution.py:128
  268.3 84.3 %reduce-scatter.3.cloned.1.call-done = bf16[128,3072]{1,0:T(8,128)(2,1)} async-done(((bf16[2048,3072]{1,0:T(8,128)(2,1)}), bf16[128,3072]{1,0:T(8,128)(2,1)}) %reduce-scatter.3.cloned.1.call-update) | async-done | bytes 786448 | tf_op jit(solution)/shard_map/reduce_scatter | solution.py:159
  352.7 13.6 %fusion.12 = bf16[2048]{0:T(1024)(128)(2,1)S(1)} fusion(f32[256,2048]{1,0:T(8,128)} %fusion.4, bf16[256,3072]{1,0:T(8,128)(2,1)S(1)} %reshape.181, bf16[2048,3072]{1,0:T(8,128)(2,1)} %all-gather.6.cloned.1.call-done), kind=kOutput, calls=%fused_computation.29 | convolution fusion | flops 3222272000 | bytes 16257024 | tf_op jit(solution)/shard_map/dot_general | solution.py:154
  366.3 31.4 %all-reduce.1 = bf16[2048]{0:T(1024)(128)(2,1)S(1)} all-reduce(bf16[2048]{0:T(1024)(128)(2,1)S(1)} %fusion.12), channel_id=4, replica_groups=mesh['dp'=8,'shard'=16] {'shard'}, use_global_device_ids=true, to_apply=%region_19.20.clone | all-reduce | flops 2048 | bytes 8192
  397.7 20.7 %psum.23 = bf16[128]{0:T(256)(128)(2,1)S(1)} all-reduce(bf16[128]{0:T(256)(128)(2,1)S(1)} %dynamic-slice.5), channel_id=1, replica_groups=mesh['dp'=8,'shard'=16] {'dp'}, use_global_device_ids=true, to_apply=%region_20.21 | all-reduce | flops 128 | bytes 512 | tf_op jit(solution)/shard_map/psum | solution.py:169
  419.0 22.7 %all-reduce.5.cloned.1.call-done = (bf16[128,3072]{1,0:T(8,128)(2,1)}, bf16[64,2048]{1,0:T(8,128)(2,1)}) async-done(((bf16[128,3072]{1,0:T(8,128)(2,1)}, bf16[64,2048]{1,0:T(8,128)(2,1)}), (bf16[128,3072]{1,0:T(8,128)(2,1)}, bf16[64,2048]{1,0:T(8,128)(2,1)})) %all-reduce.5.cloned.1.call-update) | async-done | bytes 1048592 | tf_op jit(solution)/shard_map/psum | solution.py:167
  441.7 2.4 multiply_subtract_fusion.1
  444.1 4.6 %multiply_subtract_fusion = (f32[128,3072]{1,0:T(8,128)}, f32[128,3072]{1,0:T(8,128)}, f32[128,3072]{1,0:T(8,128)}) fusion(f32[128,3072]{1,0:T(8,128)S(1)} %copy-done.1, bf16[128,3072]{1,0:T(8,128)(2,1)} %get-tuple-element.40, f32[128,3072]{1,0:T(8,128)S(1)} %copy-done.10, f32[128,3072]{1,0:T(8,128)} %param.18), kind=kLoop, calls=%fused_computation.25 | loop fusion | flops 5898240 | bytes 10223616 | tf_op jit(solution)/shard_map/sub | solution.py:45
  (107 shorter events, 28.2 us)
Async XLA Ops:
  7.2 2.6 copy-start.8
  7.2 3.4 copy-start.17
  7.2 3.5 copy-start.14
  7.2 25.7 %copy-start.13 = (f32[8,255]{1,0:T(8,128)S(1)}, f32[8,255]{1,0:T(8,128)}, u32[]{:S(2)}) copy-start(f32[8,255]{1,0:T(8,128)} %param.16) | copy-start | bytes 24484
  7.2 78.7 %all-gather.6.cloned.1.call-start = ((), (), s32[]{:S(2)}) async-start(), calls=%async_computation.2 | async-start | bytes 13369344 | tf_op jit(solution)/shard_map/all_gather | solution.py:73
  9.7 116.9 %all-gather.8.cloned.1.call-start = ((), (), s32[]{:S(2)}) async-start(), calls=%async_computation.3 | async-start | bytes 4456448 | tf_op jit(solution)/shard_map/all_gather | solution.py:74
  10.5 185.9 %all-gather.10.cloned.1.call-start = ((), (), s32[]{:S(2)}) async-start(), calls=%async_computation.6 | async-start | bytes 2113536 | tf_op jit(solution)/shard_map/all_gather | solution.py:104
  95.9 3.8 copy-start.3
  98.6 1.2 copy-start.6
  126.6 4.4 copy-start
  131.0 137.3 %reduce-scatter.5.cloned.1.call-start = ((), (), s32[]{:S(2)}) async-start(), calls=%async_computation.5 | async-start | bytes 4456448 | tf_op jit(solution)/shard_map/reduce_scatter | solution.py:128
  208.2 1.4 copy-start.2
  208.2 144.4 %reduce-scatter.3.cloned.1.call-start = ((), (), s32[]{:S(2)}) async-start(), calls=%async_computation.4 | async-start | bytes 13369344 | tf_op jit(solution)/shard_map/reduce_scatter | solution.py:159
  210.0 3.5 copy-start.7
  210.0 3.8 copy-start.5
  213.7 1.1 copy-start.4
  225.8 215.9 %all-reduce.5.cloned.1.call-start = ((), (), s32[]{:S(2)}) async-start(), calls=%async_computation.7 | async-start | bytes 2097152 | tf_op jit(solution)/shard_map/psum | solution.py:167
  352.6 65.8 %copy-start.15 = (f32[128]{0:T(128)S(1)}, f32[128]{0:T(128)}, u32[]{:S(2)}) copy-start(f32[128]{0:T(128)} %param.25) | copy-start | bytes 1540
  352.6 65.8 %copy-start.16 = (f32[128]{0:T(128)S(1)}, f32[128]{0:T(128)}, u32[]{:S(2)}) copy-start(f32[128]{0:T(128)} %param.24) | copy-start | bytes 1540
  352.6 89.0 %copy-start.9 = (f32[64,2048]{1,0:T(8,128)S(1)}, f32[64,2048]{1,0:T(8,128)}, u32[]{:S(2)}) copy-start(f32[64,2048]{1,0:T(8,128)} %param.20) | copy-start | bytes 1572868
  352.7 89.0 %copy-start.11 = (f32[64,2048]{1,0:T(8,128)S(1)}, f32[64,2048]{1,0:T(8,128)}, u32[]{:S(2)}) copy-start(f32[64,2048]{1,0:T(8,128)} %param.22) | copy-start | bytes 1572868
  352.7 89.0 %copy-start.12 = (f32[64,2048]{1,0:T(8,128)S(1)}, f32[64,2048]{1,0:T(8,128)}, u32[]{:S(2)}) copy-start(f32[64,2048]{1,0:T(8,128)} %param.21) | copy-start | bytes 1572868
  366.3 77.8 %copy-start.1 = (f32[128,3072]{1,0:T(8,128)S(1)}, f32[128,3072]{1,0:T(8,128)}, u32[]{:S(2)}) copy-start(f32[128,3072]{1,0:T(8,128)} %param.17) | copy-start | bytes 4718596
  441.6 2.5 copy-start.10
  (1 other events, 0.7 us)
Sparse Core Ops, SparseCore 0:
  10.3 75.5 all-gather.5
  88.2 38.3 all-gather.7
  131.1 65.3 all-gather.9
  208.3 59.9 reduce-scatter.4
  270.5 82.0 reduce-scatter.2
  355.0 86.5 all-reduce.4
where the time goes:
time: 460 us; the launch traced here: 456 us
  waiting for transfers between devices  275 us (60%)
  blocking collectives  74.2 us (16%)
  matrix products  49.4 us (11%)
  local copies, waits for them, and re-layouts  23.4 us (5%)
  other arithmetic  18.2 us (4%)
  between operations  15.2 us (3%)
    reduce_scatter x1, waiting for transfers between devices, per_device(): lax.psum_scatter(grad_input.astype(jnp.bfloat16), 'shard', scatter_dimens...  84.3 us
    all_gather x1, waiting for transfers between devices, per_device(): everyone = lax.all_gather(embedding, ('dp', 'shard'), axis=0, tiled=True)  61.7 us
    reduce_scatter x1, waiting for transfers between devices, per_device(): lax.psum_scatter(grad_output.astype(jnp.bfloat16), 'shard', scatter_dimen...  40.6 us
    all_gather x1, waiting for transfers between devices, per_device(): lax.all_gather(input_master.astype(bf16), 'shard', axis=0, tiled=True)  39.1 us
    unnamed x1, blocking collectives  31.4 us
    all_gather x1, waiting for transfers between devices, per_device(): lax.all_gather(output_master.astype(bf16), 'shard', axis=0, tiled=True)  26.2 us
    psum x1, waiting for transfers between devices, per_device(): lax.psum(input_share.astype(jnp.bfloat16), 'dp').astype(jnp.float32)  22.7 us
    all_gather x1, blocking collectives, per_device(): lax.all_gather(gain_master.astype(bf16), 'shard', axis=0, tiled=True)  22.1 us
  transfers between devices with their start and end apart: 6, of which 6 were waited for; matrix products, arithmetic and copies ran while one was open for 14% of the time, Pallas kernels for 0%

commit v1 on v0

v1 whole, which is shorter than its diff:
```python
import functools

import jax
import jax.numpy as jnp
from jax import lax
from jax.experimental import pallas as pl
from jax.experimental.pallas import tpu as pltpu
from jax.sharding import PartitionSpec as P

D = 2048
HEADS = 8
HEAD_DIM = 128
INNER = 1024
CROP = 128
QKV = 3 * HEAD_DIM
SLICE = D // 8

inv_tau = 20.0
norm_eps = 1e-05
embed_eps = 1e-06
beta_one = 0.9
beta_two = 0.999
adam_eps = 1e-08
learn_rate = 0.002
weight_decay = 0.1
adam_step = 1000
score_scale = HEAD_DIM ** (-0.5)

f32 = jnp.float32
bf16 = jnp.bfloat16
HIGHEST = lax.Precision.HIGHEST
NT = (((1,), (1,)), ((), ()))
TN = (((0,), (0,)), ((), ()))


def dot(a, b, dims=(((1,), (0,)), ((), ())), precision=None):
    return lax.dot_general(a, b, dims, precision=precision, preferred_element_type=f32)


def adam_update(master, moment, square, gradient, decay):
    moment_new = beta_one * moment + (1.0 - beta_one) * gradient
    square_new = beta_two * square + (1.0 - beta_two) * gradient * gradient
    mean_hat = moment_new / (1.0 - beta_one**adam_step)
    square_hat = square_new / (1.0 - beta_two**adam_step)
    master_new = master - learn_rate * (
        mean_hat / (jnp.sqrt(square_hat) + adam_eps) + decay * master
    )
    return (master_new, moment_new, square_new)


W, WO, MC, MM, M2, PO, GR, TO, GF, GM, RS = range(11)


def kernel(
    xn, mc, wp, wo2, bias, pair_a, pair_b,
    loss_out, s_out, o_out,
    xbuf, wbuf, wobuf, mcbuf, qkvbuf, probs, mmbuf, m2buf, pobuf, grbuf, tobuf, gfbuf,
    gmsend, gmbuf, gp, rsend, rbuf, s_fin, o_tmp, o_fin, band,
    ssem, rsem, xssem, xrsem, f_send, f_recv, f2_send, f2_recv,
):
    dp = lax.axis_index("dp")
    sh = lax.axis_index("shard")
    x, yh = dp // 2, dp % 2
    yl, z, c = sh // 8, (sh // 2) % 4, sh % 2
    base = yl * 8 + z * 2
    t = 2 * x + c
    p = yh * 8 + yl * 4 + z

    def tp_dev(m):
        return ((m // 2) * 2 + yh, base + m % 2)

    def plane_dev(q):
        return (x * 2 + q // 8, ((q // 4) % 2) * 8 + (q % 4) * 2 + c)

    def push(src, dst, send, recv, dev):
        pltpu.make_async_remote_copy(
            src_ref=src, dst_ref=dst, send_sem=send, recv_sem=recv,
            device_id=dev, device_id_type=pl.DeviceIdType.MESH,
        ).start()

    def await_bytes(ref, sem):
        pltpu.make_async_copy(ref, ref, sem).wait()

    barrier = pltpu.get_barrier_semaphore()

    def greet(k, _):
        for dev in (
            (dp, (sh + k) % 16),
            plane_dev((p + k) % 16),
        ):
            pl.semaphore_signal(barrier, inc=1, device_id=dev, device_id_type=pl.DeviceIdType.MESH)
        j = (dp * 2 + c + k) % 16
        pl.semaphore_signal(
            barrier, inc=1, device_id=(j // 2, base + j % 2), device_id_type=pl.DeviceIdType.MESH
        )
        return 0

    lax.fori_loop(1, 16, greet, 0)
    pl.semaphore_wait(barrier, 45)

    right = ((x + 1) % 4) * 2 + c
    left = ((x + 3) % 4) * 2 + c
    far = ((x + 2) % 4) * 2 + c
    sib = x * 2 + 1 - c
    other = 1 - 2 * c

    def send_item(src, slot, member):
        push(src, xbuf.at[slot], xssem, xrsem.at[slot], tp_dev(member))

    send_item(xn.at[0], 2 * t, right)
    send_item(xn.at[1], 2 * t + 1, left)
    send_item(xn.at[0], 2 * t, sib)
    send_item(xn.at[1], 2 * t + 1, sib)

    def send_w(k, _):
        s = (sh + k) % 16
        push(wp.at[s % 2], wbuf.at[sh], ssem.at[W], rsem.at[W], (dp, s))
        return 0

    lax.fori_loop(1, 16, send_w, 0)
    send_item(xn.at[1], 2 * t + 1, right)
    send_item(xn.at[0], 2 * t, left)

    def send_wo(k, _):
        s = (sh + k) % 16
        push(wo2.at[s % 2], wobuf.at[sh], ssem.at[WO], rsem.at[WO], (dp, s))
        return 0

    lax.fori_loop(1, 16, send_wo, 0)

    def send_mc(k, _):
        m = (t + k) % 8
        push(mc.at[m], mcbuf.at[t], ssem.at[MC], rsem.at[MC], tp_dev(m))
        return 0

    lax.fori_loop(1, 8, send_mc, 0)

    wbuf[sh] = wp[c]
    wobuf[sh] = wo2[c]
    mcbuf[t] = mc[t]
    xbuf[2 * t] = xn[0]
    xbuf[2 * t + 1] = xn[1]

    row = jnp.broadcast_to(bias[t], (CROP, 2 * CROP))
    shifted = pltpu.roll(row, CROP + 1, 1, stride=1, stride_axis=0)
    band[...] = shifted[:, :CROP].T

    def wait_item(slot):
        await_bytes(xbuf.at[slot], xrsem.at[slot])

    wait_item(2 * left)
    send_item(xbuf.at[2 * left], 2 * left, right)
    send_item(xbuf.at[2 * left], 2 * left, sib)
    wait_item(2 * right + 1)
    send_item(xbuf.at[2 * right + 1], 2 * right + 1, left)
    send_item(xbuf.at[2 * right + 1], 2 * right + 1, sib)
    wait_item(2 * sib)
    wait_item(2 * sib + 1)
    await_bytes(wbuf.at[pl.ds(0, 15)], rsem.at[W])

    def forward(m):
        rows = xbuf[pl.ds(2 * m, 2)].reshape(2 * CROP, D)
        packed = dot(rows, wbuf[...].reshape(D, QKV)).astype(bf16)
        qkvbuf[pl.ds(2 * m, 2)] = packed.reshape(2, CROP, QKV)
        for i in range(2):
            part = packed[i * CROP : (i + 1) * CROP]
            q, k, v = part[:, :128], part[:, 128:256], part[:, 256:]
            scores = dot(q, k, NT) * score_scale + band[...]
            raised = jnp.exp(scores - jnp.max(scores, axis=-1, keepdims=True))
            prob = raised / jnp.sum(raised, axis=-1, keepdims=True)
            probs[2 * m + i] = prob
            mixed = dot(prob.astype(bf16), v).astype(bf16).astype(f32)
            mmbuf[t, pl.ds(2 * m + i, 1), :] = jnp.sum(mixed, axis=0, keepdims=True)

    def fwd_own(k, _):
        forward(t + k * other)
        return 0

    lax.fori_loop(0, 2, fwd_own, 0)

    wait_item(2 * left + 1)
    send_item(xbuf.at[2 * left + 1], 2 * left + 1, sib)
    wait_item(2 * right)
    send_item(xbuf.at[2 * right], 2 * right, sib)

    def fwd_near(k, _):
        member = ((x + 3 + 2 * (k % 2)) % 4) * 2 + c + (k // 2) * other

        @pl.when(k >= 2)
        def _():
            wait_item(2 * member)
            wait_item(2 * member + 1)

        forward(member)
        return 0

    lax.fori_loop(0, 4, fwd_near, 0)

    wait_item(2 * far)
    send_item(xbuf.at[2 * far], 2 * far, sib)
    wait_item(2 * far + 1)
    send_item(xbuf.at[2 * far + 1], 2 * far + 1, sib)

    def fwd_far(k, _):
        member = far + k * other

        @pl.when(k >= 1)
        def _():
            wait_item(2 * member)
            wait_item(2 * member + 1)

        forward(member)
        return 0

    lax.fori_loop(0, 2, fwd_far, 0)

    def send_mm(k, _):
        push(mmbuf.at[t], mmbuf.at[t], ssem.at[MM], rsem.at[MM], tp_dev((t + k) % 8))
        return 0

    lax.fori_loop(1, 8, send_mm, 0)
    await_bytes(wobuf.at[pl.ds(0, 15)], rsem.at[WO])
    await_bytes(mcbuf.at[pl.ds(0, 7)], rsem.at[MC])
    await_bytes(mmbuf.at[pl.ds(0, 7)], rsem.at[MM])

    wo_slice = wobuf[...].reshape(INNER, SLICE)
    summed = jnp.concatenate([mmbuf[h] for h in range(8)], axis=1)
    high = summed.astype(bf16)
    low = (summed - high.astype(f32)).astype(bf16)
    product = dot(jnp.concatenate([high, low], axis=0), wo_slice)
    means = jnp.concatenate([mcbuf[m] for m in range(8)], axis=0)
    pooled = means + (product[:16] + product[16:]) * (1.0 / CROP)
    pobuf[p] = pooled

    def send_po(k, _):
        q = (p + k) % 16
        push(pobuf.at[p], pobuf.at[p], ssem.at[PO], rsem.at[PO], plane_dev(q))
        return 0

    lax.fori_loop(1, 16, send_po, 0)

    def send_m2(k, _):
        q = (p + k) % 16
        push(mmbuf.at[q % 8], m2buf.at[p], ssem.at[M2], rsem.at[M2], plane_dev(q))
        return 0

    lax.fori_loop(1, 16, send_m2, 0)
    m2buf[p] = mmbuf[p % 8]

    lane = lax.broadcasted_iota(jnp.int32, (256, 256), 1)
    r_t = (lane // 2) % 8
    r_p = lane // 16
    item = 2 * (
        ((r_t // 2) * 2 + r_p // 8) * 16 + ((r_p // 4) % 2) * 8 + (r_p % 4) * 2 + r_t % 2
    ) + lane % 2
    hot_a = (pair_a[...] == item).astype(bf16)
    hot_b = (pair_b[...] == item).astype(bf16)
    lane16 = lax.broadcasted_iota(jnp.int32, (16, 256), 1)
    sub16 = lax.broadcasted_iota(jnp.int32, (16, 256), 0)
    own = (lane16 == sub16 + p * 16).astype(f32)
    first = dot(own.astype(bf16), hot_a, NT).astype(bf16)
    target = dot(first, hot_b)

    await_bytes(pobuf.at[pl.ds(0, 15)], rsem.at[PO])
    everyone = pobuf[...].reshape(256, SLICE)
    grbuf[t, pl.ds(0, 16), :] = dot(pooled, everyone, NT, HIGHEST)
    grbuf[t, pl.ds(16, 8), :] = dot(jnp.ones((8, SLICE), f32), everyone * everyone, NT, HIGHEST)

    def send_gr(k, _):
        push(grbuf.at[t], grbuf.at[t], ssem.at[GR], rsem.at[GR], tp_dev((t + k) % 8))
        return 0

    lax.fori_loop(1, 8, send_gr, 0)
    await_bytes(grbuf.at[pl.ds(0, 7)], rsem.at[GR])
    gram = grbuf[0]
    for m in range(1, 8):
        gram = gram + grbuf[m]
    inv_row = lax.rsqrt(gram[16:17] + embed_eps)
    inv_col = jnp.sum(own * inv_row, axis=1, keepdims=True)
    sims = gram[:16] * inv_col * inv_row * inv_tau
    exponents = jnp.where(own > 0.5, 0.0, jnp.exp(sims - inv_tau))
    totals = jnp.sum(exponents, axis=1, keepdims=True)
    tobuf[p] = jnp.broadcast_to(totals, (16, 128))

    def send_to(k, _):
        q = (p + k) % 16
        push(tobuf.at[p], tobuf.at[p], ssem.at[TO], rsem.at[TO], plane_dev(q))
        return 0

    lax.fori_loop(1, 16, send_to, 0)
    losses = jnp.log(totals) + inv_tau - jnp.sum(sims * target, axis=1, keepdims=True)
    loss_out[...] = jnp.broadcast_to(losses, (16, 128))
    await_bytes(tobuf.at[pl.ds(0, 15)], rsem.at[TO])
    columns = tobuf[...].reshape(256, 128)
    columns = jnp.concatenate([columns, columns], axis=1)
    eye = lax.broadcasted_iota(jnp.int32, (256, 256), 0) == lane
    column_totals = jnp.sum(jnp.where(eye, columns, 0.0), axis=0, keepdims=True)
    weights = exponents / totals + exponents / column_totals - 2.0 * target
    grad_embedding = dot(weights * inv_row, everyone, precision=HIGHEST) * inv_tau
    along = jnp.sum(weights * sims, axis=1, keepdims=True)
    grad_pooled = (grad_embedding - pooled * inv_col * along) * inv_col
    grad_frame = (grad_pooled * (1.0 / CROP)).astype(bf16)
    partial = dot(grad_frame, wo_slice, NT)
    for h in range(8):
        gmsend[h] = partial[:, h * 128 : (h + 1) * 128]
    gfbuf[p] = grad_frame

    def send_gm(k, _):
        m = (t + k) % 8
        push(gmsend.at[m], gmbuf.at[t], ssem.at[GM], rsem.at[GM], tp_dev(m))
        return 0

    lax.fori_loop(1, 8, send_gm, 0)
    gmbuf[t] = gmsend[t]

    def send_gf(k, _):
        q = (p + k) % 16
        push(gfbuf.at[p], gfbuf.at[p], ssem.at[GF], rsem.at[GF], plane_dev(q))
        return 0

    lax.fori_loop(1, 16, send_gf, 0)
    await_bytes(gmbuf.at[pl.ds(0, 7)], rsem.at[GM])
    gm = gmbuf[0]
    for m in range(1, 8):
        gm = gm + gmbuf[m]
    grad_mixed = gm.astype(bf16)
    gmsum = grad_mixed.astype(f32)
    sub_item = lax.broadcasted_iota(jnp.int32, (16, 128), 0)

    def backward(b, _):
        part = qkvbuf[b]
        q, k, v = part[:, :128], part[:, 128:256], part[:, 256:]
        prob = probs[b]
        mask = sub_item == b
        g_row = jnp.sum(jnp.where(mask, dot(grad_mixed, v, NT), 0.0), axis=0, keepdims=True)
        gm_row = jnp.sum(jnp.where(mask, gmsum, 0.0), axis=0, keepdims=True)
        centred = g_row - jnp.sum(prob * g_row, axis=-1, keepdims=True)
        dscores = (prob * centred * score_scale).astype(bf16)
        grad_q = dot(dscores, k)
        grad_k = dot(dscores, q, TN)
        grad_v = dot(prob.astype(bf16), jnp.broadcast_to(gm_row, (CROP, 128)).astype(bf16), TN)
        gp[b] = jnp.concatenate([grad_q, grad_k, grad_v], axis=1).astype(bf16)
        return 0

    lax.fori_loop(0, 16, backward, 0)

    def block(q):
        s = ((q // 4) % 2) * 8 + (q % 4) * 2 + q // 8
        cols = xbuf[:, :, pl.ds(pl.multiple_of(s * 128, 128), 128)].reshape(16 * CROP, 128)
        return dot(cols, gp[...].reshape(16 * CROP, QKV), TN).astype(bf16)

    def scatter(k, _):
        q = (p + k) % 16
        value = block(q)
        for i in range(3):
            rsend[q, i] = value[:, i * 128 : (i + 1) * 128]
        push(rsend.at[q], rbuf.at[p], ssem.at[RS], rsem.at[RS], plane_dev(q))
        return 0

    lax.fori_loop(1, 16, scatter, 0)
    value = block(p)
    for i in range(3):
        rbuf[p, i] = value[:, i * 128 : (i + 1) * 128]

    await_bytes(m2buf.at[pl.ds(0, 15)], rsem.at[M2])
    await_bytes(gfbuf.at[pl.ds(0, 15)], rsem.at[GF])
    o_tmp[...] = dot(
        m2buf[...].reshape(256, 128).astype(bf16), gfbuf[...].reshape(256, SLICE), TN
    )
    o_fin[...] = o_tmp[pl.ds(pl.multiple_of(yh * 64, 64), 64), :].astype(bf16)

    s_cols = pl.ds(pl.multiple_of(t * 128, 128), 128)
    o_cols = pl.ds(pl.multiple_of(t * SLICE, SLICE), SLICE)

    def each_target(fn):
        def step(j, _):
            @pl.when(jnp.logical_or(j != dp, c != yh))
            def _():
                fn(j)
            return 0
        lax.fori_loop(0, 8, step, 0)

    def send_o(j):
        push(o_fin, o_out.at[:, o_cols], f2_send.at[j], f2_recv.at[t], (j, base + yh))

    each_target(send_o)

    await_bytes(rbuf.at[pl.ds(0, 15)], rsem.at[RS])
    for i in range(3):
        total = rbuf[0, i].astype(f32)
        for q in range(1, 16):
            total = total + rbuf[q, i].astype(f32)
        s_fin[i] = total.astype(bf16)

    def send_s(j):
        push(s_fin, s_out.at[:, :, s_cols], f_send.at[j], f_recv.at[t], (j, base + yh))

    each_target(send_s)

    @pl.when(c == yh)
    def _():
        s_out[:, :, s_cols] = s_fin[...]
        o_out[:, o_cols] = o_fin[...]

    def collect(m, _):
        @pl.when(jnp.logical_or(m != t, c != yh))
        def _():
            await_bytes(s_fin, f_recv.at[m])
            await_bytes(o_fin, f2_recv.at[m])
        return 0

    lax.fori_loop(0, 8, collect, 0)

    def sent(j):
        await_bytes(s_fin, f_send.at[j])
        await_bytes(o_fin, f2_send.at[j])

    each_target(sent)
    await_bytes(xbuf.at[pl.ds(0, 14)], xssem)
    for sem, ref in (
        (W, wbuf), (WO, wobuf), (M2, m2buf), (PO, pobuf), (TO, tobuf), (GF, gfbuf), (RS, rbuf),
    ):
        await_bytes(ref.at[pl.ds(0, 15)], ssem.at[sem])
    for sem, ref in ((MC, mcbuf), (MM, mmbuf), (GR, grbuf), (GM, gmbuf)):
        await_bytes(ref.at[pl.ds(0, 7)], ssem.at[sem])


def run_kernel(*args):
    vmem = pl.BlockSpec(memory_space=pltpu.VMEM)
    return pl.pallas_call(
        kernel,
        out_shape=(
            jax.ShapeDtypeStruct((16, 128), f32),
            jax.ShapeDtypeStruct((3, 128, INNER), bf16),
            jax.ShapeDtypeStruct((64, D), bf16),
        ),
        in_specs=[vmem] * len(args),
        out_specs=(vmem, vmem, vmem),
        scratch_shapes=[
            pltpu.VMEM((16, CROP, D), bf16),
            pltpu.VMEM((16, 128, QKV), bf16),
            pltpu.VMEM((16, 64, SLICE), bf16),
            pltpu.VMEM((8, 2, SLICE), f32),
            pltpu.VMEM((16, CROP, QKV), bf16),
            pltpu.VMEM((16, CROP, CROP), f32),
            pltpu.VMEM((8, 16, 128), f32),
            pltpu.VMEM((16, 16, 128), f32),
            pltpu.VMEM((16, 16, SLICE), f32),
            pltpu.VMEM((8, 24, 256), f32),
            pltpu.VMEM((16, 16, 128), f32),
            pltpu.VMEM((16, 16, SLICE), bf16),
            pltpu.VMEM((8, 16, 128), f32),
            pltpu.VMEM((8, 16, 128), f32),
            pltpu.VMEM((16, CROP, QKV), bf16),
            pltpu.VMEM((16, 3, 128, 128), bf16),
            pltpu.VMEM((16, 3, 128, 128), bf16),
            pltpu.VMEM((3, 128, 128), bf16),
            pltpu.VMEM((128, SLICE), f32),
            pltpu.VMEM((64, SLICE), bf16),
            pltpu.VMEM((CROP, CROP), f32),
            pltpu.SemaphoreType.DMA((11,)),
            pltpu.SemaphoreType.DMA((11,)),
            pltpu.SemaphoreType.DMA,
            pltpu.SemaphoreType.DMA((16,)),
            pltpu.SemaphoreType.DMA((8,)),
            pltpu.SemaphoreType.DMA((8,)),
            pltpu.SemaphoreType.DMA((8,)),
            pltpu.SemaphoreType.DMA((8,)),
        ],
        compiler_params=pltpu.CompilerParams(
            collective_id=0, has_side_effects=True, vmem_limit_bytes=56 * 1024 * 1024
        ),
        name="encoder",
    )(*args)


def per_device(
    frames, crop_starts, pairing, bias_table,
    input_master, input_moment, input_square,
    output_master, output_moment, output_square,
    gain_master, gain_moment, gain_square,
):
    x = lax.axis_index("dp") // 2
    t = 2 * x + lax.axis_index("shard") % 2
    gain_w = gain_master.astype(bf16).astype(f32)
    input_w = input_master.astype(bf16).astype(f32)
    crops = jnp.stack(
        [lax.dynamic_slice_in_dim(frames[i], crop_starts[i], CROP, 0) for i in range(2)]
    )
    frames_f = crops.astype(f32)
    centred = frames_f - jnp.mean(frames_f, axis=-1, keepdims=True)
    normed = centred * lax.rsqrt(jnp.mean(centred * centred, axis=-1, keepdims=True) + norm_eps)
    xn = normed.astype(bf16)
    mc = jnp.mean(frames_f, axis=1).reshape(2, 8, SLICE).transpose(1, 0, 2)
    pieces = lax.dynamic_slice_in_dim(
        input_master.reshape(128, 3, HEADS, HEAD_DIM), 2 * x, 2, 2
    ).astype(bf16).astype(f32)
    wp = (pieces * gain_w[:, None, None, None]).astype(bf16)
    wp = wp.transpose(2, 0, 1, 3).reshape(2, 128, QKV)
    wo2 = lax.dynamic_slice_in_dim(output_master.reshape(64, 8, SLICE), 2 * x, 2, 1)
    wo2 = wo2.astype(bf16).transpose(1, 0, 2)
    bias = jnp.pad(bias_table, ((0, 0), (0, 1))).reshape(HEADS, 1, 2 * CROP)
    pair_b = pairing.reshape(128, 2)[:, ::-1].reshape(256, 1)
    losses, s_grad, o_grad = run_kernel(
        xn, mc, wp, wo2, bias, pairing.reshape(256, 1), pair_b
    )
    pair_losses = lax.dynamic_slice(losses, (2 * t, 0), (2, 1)).reshape(2)
    share = s_grad.astype(f32).transpose(1, 0, 2).reshape(128, 3 * INNER)
    gain_total = jnp.sum(share * input_w, axis=1)
    input_new = adam_update(
        input_master, input_moment, input_square, share * gain_w[:, None], weight_decay
    )
    output_new = adam_update(
        output_master, output_moment, output_square, o_grad.astype(f32), weight_decay
    )
    gain_new = adam_update(gain_master, gain_moment, gain_square, gain_total, 0.0)
    return (pair_losses, *input_new, *output_new, *gain_new)


def solution(mesh):
    one = P("shard")
    two = P("shard", None)
    items = P(("dp", "shard"))
    in_specs = (P(("dp", "shard"), None, None), items, P(), P()) + (two,) * 6 + (one,) * 3
    out_specs = (items,) + (two,) * 6 + (one,) * 3
    return jax.shard_map(
        per_device, mesh=mesh, in_specs=in_specs, out_specs=out_specs, check_vma=False
    )
```

time: 460 us -> 166 us (0.36)
  the two profiles are of different devices: /device:TPU:1 before, /device:TPU:112 now
where the time goes in v1:
time: 166 us
  Pallas kernels  125 us (75%)
  local copies, waits for them, and re-layouts  24.7 us (15%)
  other arithmetic  11.2 us (7%)
  between operations  4.72 us (3%)
    pallas_call x1, Pallas kernels, run_kernel(): pl.pallas_call(kernel, out_shape=(jax.ShapeDtypeStruct((16, 128), f32), j...  125 us
    unnamed x34, local copies, waits for them, and re-layouts  13.9 us
    sub x3, other arithmetic, adam_update(): master - learn_rate * (mean_hat / (jnp.sqrt(square_hat) + adam_eps) + dec...  7.18 us

profile of v1, /device:TPU:112, one launch (start us, length us, event | category | flops | bytes accessed | tf_op | source)
XLA Modules:
  0.0 165.9 jit_solution(5640598522155157302)
XLA Ops:
  0.7 2.7 %fusion.16 = (bf16[1,256,2048]{2,1,0:T(8,128)(2,1)S(1)}, bf16[1,256,2048]{2,1,0:T(8,128)(2,1)}) fusion(bf16[2,256,2048]{2,1,0:T(8,128)(2,1)} %param.13), kind=kLoop, calls=%fused_computation.39 | loop fusion | bytes 4194304 | tf_op jit(solution)/shard_map/slice | solution.py:488
  3.4 0.6 fusion.17
  7.8 1.3 constant_dynamic-slice_fusion.2
  9.4 0.6 convert_reduce_fusion
  9.9 1.3 fusion.3.xn
  11.2 0.6 broadcast_multiply_fusion
  11.9 1.9 %copy.37 = f32[128,3072]{0,1:T(8,128)S(1)} copy(f32[128,3072]{1,0:T(8,128)} %param.17) | data formatting | bytes 3145728 | tf_op args[4]
  13.9 0.8 copy.40.wp
  15.0 0.6 copy.57
  15.6 0.6 reshape.75.bias
  16.2 0.8 copy.41.pair_a
  17.3 0.8 reshape.85.pair_b
  18.0 125.3 %encoder.1 = (f32[16,128]{1,0:T(8,128)}, bf16[3,128,1024]{2,1,0:T(8,128)(2,1)}, bf16[64,2048]{1,0:T(8,128)(2,1)}) custom-call(bf16[2,128,2048]{2,1,0:T(8,128)(2,1)} %fusion.3.xn, f32[8,2,256]{2,1,0:T(2,128)} %bitcast.33, bf16[2,128,384]{2,1,0:T(8,128)(2,1)} %copy.40.wp, bf16[2,64,256]{2,1,0:T(8,128)(2,1)} %bitcast.32, f32[8,1,256]{2,1,0:T(1,128)} %reshape.75.bias, ...), custom_call_target="tpu_custom_call" | custom-call | tf_op jit(solution)/shard_map/encoder/pallas_call | solution.py:430
  143.3 1.3 fusion.10
  144.6 1.3 convert_bitcast_fusion
  145.9 1.6 copy.44
  147.5 3.1 %copy.45 = f32[128,3072]{0,1:T(8,128)} copy(f32[128,3072]{1,0:T(8,128)} %param.19) | data formatting | bytes 3145728 | tf_op args[6]
  150.7 1.6 copy.43
  152.3 5.3 %multiply_subtract_fusion = (f32[128,3072]{0,1:T(8,128)}, f32[128,3072]{0,1:T(8,128)S(1)}, f32[128,3072]{0,1:T(8,128)}, f32[128]{0:T(128)S(1)}) fusion(f32[128,3072]{0,1:T(8,128)S(1)} %copy.37, f32[128]{0:T(128)S(1)} %convert_convert_fusion, f32[128,3,1024]{0,2,1:T(8,128)} %copy.44, f32[128,3072]{0,1:T(8,128)} %copy.45, f32[128,3072]{0,1:T(8,128)} %copy.43), kind=kLoop, calls=%fused_computation.13 | loop fusion | flops 7470976 | bytes 11011072 | tf_op jit(solution)/shard_map/sub | solution.py:45
  157.6 3.1 %copy.49 = f32[128,3072]{1,0:T(8,128)} copy(f32[128,3072]{0,1:T(8,128)} %get-tuple-element.44) | data formatting | bytes 3145728
  160.7 1.6 copy.50
  162.3 1.6 copy.51
  164.0 1.4 multiply_subtract_fusion.1
  165.4 0.5 multiply_subtract_fusion.2
  (37 shorter events, 0.8 us)
Async XLA Ops:
  0.6 2.7 %copy-start.9 = (s32[2]{0:T(128)S(1)}, s32[2]{0:T(128)}, u32[]{:S(2)}) copy-start(s32[2]{0:T(128)} %param.14) | copy-start | bytes 28
  11.9 2.0 %copy-start.10 = (f32[128]{0:T(128)S(1)}, f32[128]{0:T(128)}, u32[]{:S(2)}) copy-start(f32[128]{0:T(128)} %param.23) | copy-start | bytes 1540
  11.9 2.9 %copy-start.1 = (f32[64,2048]{1,0:T(8,128)S(1)}, f32[64,2048]{1,0:T(8,128)}, u32[]{:S(2)}) copy-start(f32[64,2048]{1,0:T(8,128)} %param.20) | copy-start | bytes 1572868
  13.8 1.8 %copy-start.7 = (f32[8,255]{1,0:T(8,128)S(1)}, f32[8,255]{1,0:T(8,128)}, u32[]{:S(2)}) copy-start(f32[8,255]{1,0:T(8,128)} %param.16) | copy-start | bytes 24484
  13.8 2.4 %copy-start.8 = (s32[256]{0:T(256)S(1)}, s32[256]{0:T(256)}, u32[]{:S(2)}) copy-start(s32[256]{0:T(256)} %param.15) | copy-start | bytes 3076
  147.5 3.1 %copy-start.3 = (f32[128,3072]{1,0:T(8,128)S(1)}, f32[128,3072]{1,0:T(8,128)}, u32[]{:S(2)}) copy-start(f32[128,3072]{1,0:T(8,128)} %param.18) | copy-start | bytes 4718596
  157.6 3.1 %copy-start = (f32[128,3072]{0,1:T(8,128)S(1)}, f32[128,3072]{0,1:T(8,128)}, u32[]{:S(2)}) copy-start(f32[128,3072]{0,1:T(8,128)} %get-tuple-element.46) | copy-start | bytes 4718596
  162.3 1.6 copy-start.2
  162.3 1.6 copy-start.4
  162.3 1.6 copy-start.5
  162.3 1.6 copy-start.6
  164.0 1.4 copy-start.11
  164.0 1.4 copy-start.12

commit v2 on v1

v2 whole, which is shorter than its diff:
```python
import functools

import jax
import jax.numpy as jnp
from jax import lax
from jax.experimental import pallas as pl
from jax.experimental.pallas import tpu as pltpu
from jax.sharding import PartitionSpec as P

D = 2048
HEADS = 8
HEAD_DIM = 128
INNER = 1024
CROP = 128
QKV = 3 * HEAD_DIM
SLICE = D // 8

inv_tau = 20.0
norm_eps = 1e-05
embed_eps = 1e-06
beta_one = 0.9
beta_two = 0.999
adam_eps = 1e-08
learn_rate = 0.002
weight_decay = 0.1
adam_step = 1000
score_scale = HEAD_DIM ** (-0.5)

f32 = jnp.float32
bf16 = jnp.bfloat16
HIGHEST = lax.Precision.HIGHEST
NT = (((1,), (1,)), ((), ()))
TN = (((0,), (0,)), ((), ()))


def dot(a, b, dims=(((1,), (0,)), ((), ())), precision=None):
    return lax.dot_general(a, b, dims, precision=precision, preferred_element_type=f32)


def adam_update(master, moment, square, gradient, decay):
    moment_new = beta_one * moment + (1.0 - beta_one) * gradient
    square_new = beta_two * square + (1.0 - beta_two) * gradient * gradient
    mean_hat = moment_new / (1.0 - beta_one**adam_step)
    square_hat = square_new / (1.0 - beta_two**adam_step)
    master_new = master - learn_rate * (
        mean_hat / (jnp.sqrt(square_hat) + adam_eps) + decay * master
    )
    return (master_new, moment_new, square_new)


W, WO, MC, MM, EA, PO, GR, TO, LA, GM, RS = range(11)


def item_of(row):
    t, p = (row // 2) % 8, row // 16
    return 2 * (
        ((t // 2) * 2 + p // 8) * 16 + ((p // 4) % 2) * 8 + (p % 4) * 2 + t % 2
    ) + row % 2


def kernel(
    xn, mc, pairing, bias, input_master, output_master, gain,
    loss_out, s_out, o_out,
    wraw, woraw, wp, wo2, mcsend, target,
    xbuf, xt, wbuf, wobuf, mcbuf, qkvbuf, probs, arows, mmbuf, eabuf, easend, pobuf, grbuf,
    tobuf, labuf, gmsend, gmbuf, gp, rsend, rbuf, s_fin, o_tmp, o_fin, band, table,
    lsem, ssem, rsem, xssem, xrsem, q_send, q_recv, v_send, v_recv, o_send, o_recv,
):
    dp = lax.axis_index("dp")
    sh = lax.axis_index("shard")
    x, yh = dp // 2, dp % 2
    yl, z, c = sh // 8, (sh // 2) % 4, sh % 2
    base = yl * 8 + z * 2
    t = 2 * x + c
    p = yh * 8 + yl * 4 + z

    def tp_dev(m):
        return ((m // 2) * 2 + yh, base + m % 2)

    def plane_dev(q):
        return (x * 2 + q // 8, ((q // 4) % 2) * 8 + (q % 4) * 2 + c)

    def push(src, dst, send, recv, dev):
        pltpu.make_async_remote_copy(
            src_ref=src, dst_ref=dst, send_sem=send, recv_sem=recv,
            device_id=dev, device_id_type=pl.DeviceIdType.MESH,
        ).start()

    def await_bytes(ref, sem):
        pltpu.make_async_copy(ref, ref, sem).wait()

    loads = []
    for i in range(3):
        cols = pl.ds(pl.multiple_of(i * INNER + x * 256, 256), 256)
        loads.append(
            pltpu.make_async_copy(input_master.at[:, cols], wraw.at[i], lsem.at[i])
        )
    loads.append(
        pltpu.make_async_copy(
            output_master.at[:, pl.ds(pl.multiple_of(x * 512, 512), 512)], woraw, lsem.at[3]
        )
    )
    for load in loads:
        load.start()

    barrier = pltpu.get_barrier_semaphore()

    def greet(k, _):
        for dev in (
            (dp, (sh + k) % 16),
            plane_dev((p + k) % 16),
        ):
            pl.semaphore_signal(barrier, inc=1, device_id=dev, device_id_type=pl.DeviceIdType.MESH)
        j = (dp * 2 + c + k) % 16
        pl.semaphore_signal(
            barrier, inc=1, device_id=(j // 2, base + j % 2), device_id_type=pl.DeviceIdType.MESH
        )
        return 0

    lax.fori_loop(1, 16, greet, 0)

    right = ((x + 1) % 4) * 2 + c
    left = ((x + 3) % 4) * 2 + c
    far = ((x + 2) % 4) * 2 + c
    sib = x * 2 + 1 - c
    other = 1 - 2 * c

    def send_item(src, slot, member):
        push(src, xbuf.at[slot], xssem, xrsem.at[slot], tp_dev(member))

    pl.semaphore_wait(barrier, 45)
    send_item(xn.at[0], 2 * t, right)
    send_item(xn.at[1], 2 * t + 1, left)
    send_item(xn.at[0], 2 * t, sib)
    send_item(xn.at[1], 2 * t + 1, sib)
    send_item(xn.at[1], 2 * t + 1, right)
    send_item(xn.at[0], 2 * t, left)

    for load in loads:
        load.wait()
    square = lax.broadcasted_iota(jnp.int32, (128, 128), 0) == lax.broadcasted_iota(
        jnp.int32, (128, 128), 1
    )
    gain_row = gain[...].astype(bf16).astype(f32)
    gain_col = jnp.sum(jnp.where(square, gain_row, 0.0), axis=1, keepdims=True)
    for core in range(2):
        for i in range(3):
            piece = wraw[i, :, core * 128 : (core + 1) * 128].astype(bf16).astype(f32)
            wp[core, :, i * 128 : (i + 1) * 128] = (piece * gain_col).astype(bf16)
        wo2[core] = woraw[:, core * SLICE : (core + 1) * SLICE].astype(bf16)

    def send_w(k, _):
        s = (sh + k) % 16
        push(wp.at[s % 2], wbuf.at[sh], ssem.at[W], rsem.at[W], (dp, s))
        return 0

    lax.fori_loop(1, 16, send_w, 0)

    def send_wo(k, _):
        s = (sh + k) % 16
        push(wo2.at[s % 2], wobuf.at[sh], ssem.at[WO], rsem.at[WO], (dp, s))
        return 0

    lax.fori_loop(1, 16, send_wo, 0)

    for m in range(8):
        for i in range(2):
            mcsend[m, i : i + 1, :] = mc[i, m : m + 1, :]

    def send_mc(k, _):
        m = (t + k) % 8
        push(mcsend.at[m], mcbuf.at[t], ssem.at[MC], rsem.at[MC], tp_dev(m))
        return 0

    lax.fori_loop(1, 8, send_mc, 0)

    wbuf[sh] = wp[c]
    wobuf[sh] = wo2[c]
    mcbuf[t] = mcsend[t]
    xbuf[2 * t] = xn[0]
    xbuf[2 * t + 1] = xn[1]

    table[...] = jnp.zeros_like(table)
    table[:, : 2 * CROP - 1] = bias[...]
    row = jnp.broadcast_to(table[pl.ds(t, 1), :], (CROP, 2 * CROP))
    shifted = pltpu.roll(row, CROP + 1, 1, stride=1, stride_axis=0)
    band[...] = shifted[:, :CROP].T

    lane16 = lax.broadcasted_iota(jnp.int32, (16, 256), 1)
    sub16 = lax.broadcasted_iota(jnp.int32, (16, 256), 0)
    pair = jnp.broadcast_to(pairing[...], (16, 256))
    swapped = jnp.where(lane16 % 2 == 0, pltpu.roll(pair, 255, 1), pltpu.roll(pair, 1, 1))
    hot_a = (pair == item_of(sub16 + p * 16)).astype(f32).astype(bf16)
    rows256 = lax.broadcasted_iota(jnp.int32, (256, 256), 0)
    hot_b = (jnp.broadcast_to(swapped[:1], (256, 256)) == item_of(rows256)).astype(f32).astype(bf16)
    target[...] = dot(hot_a, hot_b, NT)

    def wait_item(slot):
        await_bytes(xbuf.at[slot], xrsem.at[slot])

    wait_item(2 * left)
    send_item(xbuf.at[2 * left], 2 * left, right)
    send_item(xbuf.at[2 * left], 2 * left, sib)
    wait_item(2 * right + 1)
    send_item(xbuf.at[2 * right + 1], 2 * right + 1, left)
    send_item(xbuf.at[2 * right + 1], 2 * right + 1, sib)
    wait_item(2 * sib)
    wait_item(2 * sib + 1)
    await_bytes(wbuf.at[pl.ds(0, 15)], rsem.at[W])

    half_mask = (
        lax.broadcasted_iota(jnp.int32, (16, 256), 0)
        == lax.broadcasted_iota(jnp.int32, (16, 256), 1) // 128
    )

    def forward(m):
        rows = xbuf[pl.ds(2 * m, 2)].reshape(2 * CROP, D)
        packed = dot(rows, wbuf[...].reshape(D, QKV)).astype(bf16)
        xt[:, pl.ds(pl.multiple_of(m * 256, 256), 256)] = rows.T
        qkvbuf[pl.ds(2 * m, 2)] = packed.reshape(2, CROP, QKV)
        mass = []
        for i in range(2):
            part = packed[i * CROP : (i + 1) * CROP]
            q, k, v = part[:, :128], part[:, 128:256], part[:, 256:]
            scores = dot(q, k, NT) * score_scale + band[...]
            raised = jnp.exp(scores - jnp.max(scores, axis=-1, keepdims=True))
            prob = raised / jnp.sum(raised, axis=-1, keepdims=True)
            probs[2 * m + i] = prob
            mixed = dot(prob.astype(bf16), v).astype(bf16).astype(f32)
            mmbuf[t, pl.ds(2 * m + i, 1), :] = jnp.sum(mixed, axis=0, keepdims=True)
            mass.append(jnp.sum(prob, axis=0, keepdims=True))
        both = jnp.where(half_mask, jnp.concatenate(mass, axis=1), 0.0).astype(bf16)
        weighed = dot(both, rows)
        for i in range(2):
            arows[pl.ds(2 * m + i, 1), :] = weighed[i : i + 1]

    def fwd_own(k, _):
        forward(t + k * other)
        return 0

    lax.fori_loop(0, 2, fwd_own, 0)

    wait_item(2 * left + 1)
    send_item(xbuf.at[2 * left + 1], 2 * left + 1, sib)
    wait_item(2 * right)
    send_item(xbuf.at[2 * right], 2 * right, sib)

    def fwd_near(k, _):
        member = ((x + 3 + 2 * (k % 2)) % 4) * 2 + c + (k // 2) * other

        @pl.when(k >= 2)
        def _():
            wait_item(2 * member)
            wait_item(2 * member + 1)

        forward(member)
        return 0

    lax.fori_loop(0, 4, fwd_near, 0)

    wait_item(2 * far)
    send_item(xbuf.at[2 * far], 2 * far, sib)
    wait_item(2 * far + 1)
    send_item(xbuf.at[2 * far + 1], 2 * far + 1, sib)

    def fwd_far(k, _):
        member = far + k * other

        @pl.when(k >= 1)
        def _():
            wait_item(2 * member)
            wait_item(2 * member + 1)

        forward(member)
        return 0

    lax.fori_loop(0, 2, fwd_far, 0)

    def send_mm(k, _):
        push(mmbuf.at[t], mmbuf.at[t], ssem.at[MM], rsem.at[MM], tp_dev((t + k) % 8))
        return 0

    lax.fori_loop(1, 8, send_mm, 0, unroll=True)
    await_bytes(wobuf.at[pl.ds(0, 15)], rsem.at[WO])
    await_bytes(mcbuf.at[pl.ds(0, 7)], rsem.at[MC])
    await_bytes(mmbuf.at[pl.ds(0, 7)], rsem.at[MM])

    wo_slice = wobuf[...].reshape(INNER, SLICE)
    summed = jnp.concatenate([mmbuf[h] for h in range(8)], axis=1)
    high = summed.astype(bf16)
    low = (summed - high.astype(f32)).astype(bf16)
    product = dot(jnp.concatenate([high, low], axis=0), wo_slice)
    means = jnp.concatenate([mcbuf[m] for m in range(8)], axis=0)
    pooled = means + (product[:16] + product[16:]) * (1.0 / CROP)
    pobuf[p] = pooled

    def send_po(k, _):
        q = (p + k) % 16
        push(pobuf.at[p], pobuf.at[p], ssem.at[PO], rsem.at[PO], plane_dev(q))
        return 0

    lax.fori_loop(1, 16, send_po, 0, unroll=True)

    own = (lane16 == sub16 + p * 16).astype(f32)
    await_bytes(pobuf.at[pl.ds(0, 15)], rsem.at[PO])
    everyone = pobuf[...].reshape(256, SLICE)
    grbuf[t, pl.ds(0, 16), :] = dot(pooled, everyone, NT, HIGHEST)
    grbuf[t, pl.ds(16, 8), :] = dot(jnp.ones((8, SLICE), f32), everyone * everyone, NT, HIGHEST)

    def send_gr(k, _):
        push(grbuf.at[t], grbuf.at[t], ssem.at[GR], rsem.at[GR], tp_dev((t + k) % 8))
        return 0

    lax.fori_loop(1, 8, send_gr, 0, unroll=True)

    for s in range(16):
        q = (s % 2) * 8 + s // 2
        easend[q, :, :128] = arows[:, s * 128 : (s + 1) * 128].astype(bf16)
        easend[q, :, 128:] = mmbuf[s // 2].astype(bf16)
    eabuf[p] = easend[p]
    await_bytes(grbuf.at[pl.ds(0, 7)], rsem.at[GR])
    gram = grbuf[0]
    for m in range(1, 8):
        gram = gram + grbuf[m]
    inv_row = lax.rsqrt(gram[16:17] + embed_eps)
    inv_col = jnp.sum(own * inv_row, axis=1, keepdims=True)
    sims = gram[:16] * inv_col * inv_row * inv_tau
    exponents = jnp.where(own > 0.5, 0.0, jnp.exp(sims - inv_tau))
    totals = jnp.sum(exponents, axis=1, keepdims=True)
    tobuf[p] = jnp.broadcast_to(totals, (16, 128))

    def send_to(k, _):
        q = (p + k) % 16
        push(tobuf.at[p], tobuf.at[p], ssem.at[TO], rsem.at[TO], plane_dev(q))
        return 0

    lax.fori_loop(1, 16, send_to, 0, unroll=True)
    losses = jnp.log(totals) + inv_tau - jnp.sum(sims * target[...], axis=1, keepdims=True)
    loss_out[...] = jnp.broadcast_to(losses, (16, 128))
    await_bytes(tobuf.at[pl.ds(0, 15)], rsem.at[TO])
    columns = tobuf[...].reshape(256, 128)
    columns = jnp.concatenate([columns, columns], axis=1)
    eye = lax.broadcasted_iota(jnp.int32, (256, 256), 0) == (
        lax.broadcasted_iota(jnp.int32, (256, 256), 1)
    )
    column_totals = jnp.sum(jnp.where(eye, columns, 0.0), axis=0, keepdims=True)
    weights = exponents / totals + exponents / column_totals - 2.0 * target[...]
    grad_embedding = dot(weights * inv_row, everyone, precision=HIGHEST) * inv_tau
    along = jnp.sum(weights * sims, axis=1, keepdims=True)
    grad_pooled = (grad_embedding - pooled * inv_col * along) * inv_col
    grad_frame = (grad_pooled * (1.0 / CROP)).astype(bf16)
    partial = dot(grad_frame, wo_slice, NT)
    for h in range(8):
        gmsend[h] = partial[:, h * 128 : (h + 1) * 128]
    labuf[p, :, :SLICE] = grad_frame

    def send_gm(k, _):
        m = (t + k) % 8
        push(gmsend.at[m], gmbuf.at[t], ssem.at[GM], rsem.at[GM], tp_dev(m))
        return 0

    lax.fori_loop(1, 8, send_gm, 0, unroll=True)
    gmbuf[t] = gmsend[t]

    def send_ea(k, _):
        q = (p + k) % 16
        push(easend.at[q], eabuf.at[p], ssem.at[EA], rsem.at[EA], plane_dev(q))
        return 0

    lax.fori_loop(1, 16, send_ea, 0)
    await_bytes(gmbuf.at[pl.ds(0, 7)], rsem.at[GM])
    gm = gmbuf[0]
    for m in range(1, 8):
        gm = gm + gmbuf[m]
    grad_mixed = gm.astype(bf16)
    labuf[p, :, SLICE:] = grad_mixed

    def send_la(k, _):
        q = (p + k) % 16
        push(labuf.at[p], labuf.at[p], ssem.at[LA], rsem.at[LA], plane_dev(q))
        return 0

    lax.fori_loop(1, 16, send_la, 0)
    sub_item = lax.broadcasted_iota(jnp.int32, (16, 128), 0)

    def backward(step, _):
        for i in range(4):
            b = step * 4 + i
            part = qkvbuf[b]
            q, k, v = part[:, :128], part[:, 128:256], part[:, 256:]
            prob = probs[b]
            all_rows = dot(grad_mixed, v, NT)
            g_row = jnp.sum(jnp.where(sub_item == b, all_rows, 0.0), axis=0, keepdims=True)
            centred = g_row - jnp.sum(prob * g_row, axis=-1, keepdims=True)
            dscores = (prob * centred * score_scale).astype(bf16)
            grad_q = dot(dscores, k)
            grad_k = dot(dscores, q, TN)
            gp[b] = jnp.concatenate([grad_q, grad_k], axis=1).astype(bf16)
        return 0

    lax.fori_loop(0, 4, backward, 0)

    def scatter(k, _):
        pair_at = (p + k) % 8
        rows = pl.ds(pl.multiple_of(pair_at * 256, 256), 256)
        value = dot(xt[rows, :], gp[...].reshape(16 * CROP, 256)).astype(bf16)
        for half in range(2):
            q = half * 8 + pair_at
            block = value[half * 128 : (half + 1) * 128]

            @pl.when(q != p)
            def _():
                for i in range(2):
                    rsend[q, i] = block[:, i * 128 : (i + 1) * 128]
                push(rsend.at[q], rbuf.at[p], ssem.at[RS], rsem.at[RS], plane_dev(q))

            @pl.when(q == p)
            def _():
                for i in range(2):
                    rbuf[p, i] = block[:, i * 128 : (i + 1) * 128]
        return 0

    lax.fori_loop(1, 9, scatter, 0)

    await_bytes(eabuf.at[pl.ds(0, 15)], rsem.at[EA])
    await_bytes(labuf.at[pl.ds(0, 15)], rsem.at[LA])
    early = eabuf[...].reshape(256, 256)
    late = labuf[...].reshape(256, SLICE + 128)
    o_tmp[...] = dot(early[:, 128:], late[:, :SLICE], TN)
    s_fin[2] = dot(early[:, :128], late[:, SLICE:], TN).astype(bf16)
    o_fin[...] = o_tmp[pl.ds(pl.multiple_of(yh * 64, 64), 64), :].astype(bf16)

    s_cols = pl.ds(pl.multiple_of(t * 128, 128), 128)
    o_cols = pl.ds(pl.multiple_of(t * SLICE, SLICE), SLICE)

    def each_target(fn):
        def step(j, _):
            @pl.when(jnp.logical_or(j != dp, c != yh))
            def _():
                fn(j)
            return 0
        lax.fori_loop(0, 8, step, 0)

    def send_early(j):
        dev = (j, base + yh)
        push(s_fin.at[2], s_out.at[2, :, s_cols], v_send.at[j], v_recv.at[t], dev)
        push(o_fin, o_out.at[:, o_cols], o_send.at[j], o_recv.at[t], dev)

    each_target(send_early)

    await_bytes(rbuf.at[pl.ds(0, 15)], rsem.at[RS])
    for i in range(2):
        total = rbuf[0, i].astype(f32)
        for q in range(1, 16):
            total = total + rbuf[q, i].astype(f32)
        s_fin[i] = total.astype(bf16)

    def send_s(j):
        push(
            s_fin.at[pl.ds(0, 2)], s_out.at[pl.ds(0, 2), :, s_cols],
            q_send.at[j], q_recv.at[t], (j, base + yh),
        )

    each_target(send_s)

    @pl.when(c == yh)
    def _():
        s_out[:, :, s_cols] = s_fin[...]
        o_out[:, o_cols] = o_fin[...]

    def collect(m, _):
        @pl.when(jnp.logical_or(m != t, c != yh))
        def _():
            await_bytes(s_fin.at[2], v_recv.at[m])
            await_bytes(o_fin, o_recv.at[m])
            await_bytes(s_fin.at[pl.ds(0, 2)], q_recv.at[m])
        return 0

    lax.fori_loop(0, 8, collect, 0)

    def sent(j):
        await_bytes(s_fin.at[2], v_send.at[j])
        await_bytes(o_fin, o_send.at[j])
        await_bytes(s_fin.at[pl.ds(0, 2)], q_send.at[j])

    each_target(sent)
    await_bytes(xbuf.at[pl.ds(0, 14)], xssem)
    for sem, ref in (
        (W, wbuf), (WO, wobuf), (EA, eabuf), (PO, pobuf), (TO, tobuf), (LA, labuf), (RS, rbuf),
    ):
        await_bytes(ref.at[pl.ds(0, 15)], ssem.at[sem])
    for sem, ref in ((MC, mcbuf), (MM, mmbuf), (GR, grbuf), (GM, gmbuf)):
        await_bytes(ref.at[pl.ds(0, 7)], ssem.at[sem])


def norm_kernel(starts, frames, xn, mc, wide):
    def widen(r, _):
        rows = pl.ds(pl.multiple_of(r * 32, 32), 32)
        wide[rows, :] = frames[0, rows, :].astype(f32)
        return 0

    lax.fori_loop(0, 8, widen, 0)
    wide[pl.ds(2 * CROP, 8), :] = jnp.zeros((8, D), f32)
    begin = starts[pl.program_id(0)]
    base, odd = (begin // 8) * 8, begin % 8

    def chunk(r, total):
        near = wide[pl.ds(pl.multiple_of(base + r * 16, 8), 24), :]
        rows = pltpu.roll(near, 24 - odd, 0)[:16]
        centred = rows - jnp.mean(rows, axis=-1, keepdims=True)
        scale = lax.rsqrt(jnp.mean(centred * centred, axis=-1, keepdims=True) + norm_eps)
        xn[0, pl.ds(pl.multiple_of(r * 16, 16), 16), :] = (centred * scale).astype(bf16)
        return total + rows[:8] + rows[8:]

    total = lax.fori_loop(0, CROP // 16, chunk, jnp.zeros((8, D), f32))
    mean = jnp.sum(total, axis=0, keepdims=True) * (1.0 / CROP)
    for m in range(8):
        mc[0, m : m + 1, :] = mean[:, m * SLICE : (m + 1) * SLICE]


def run_norm(frames, starts):
    return pl.pallas_call(
        norm_kernel,
        grid=(2,),
        out_shape=(
            jax.ShapeDtypeStruct((2, CROP, D), bf16),
            jax.ShapeDtypeStruct((2, 8, SLICE), f32),
        ),
        in_specs=[
            pl.BlockSpec(memory_space=pltpu.SMEM),
            pl.BlockSpec((1, 2 * CROP, D), lambda i: (i, 0, 0)),
        ],
        out_specs=(
            pl.BlockSpec((1, CROP, D), lambda i: (i, 0, 0)),
            pl.BlockSpec((1, 8, SLICE), lambda i: (i, 0, 0)),
        ),
        scratch_shapes=[pltpu.VMEM((2 * CROP + 8, D), f32)],
        compiler_params=pltpu.CompilerParams(vmem_limit_bytes=24 * 1024 * 1024),
        name="norm",
    )(starts, frames)


def run_kernel(*args):
    vmem = pl.BlockSpec(memory_space=pltpu.VMEM)
    hbm = pl.BlockSpec(memory_space=pl.ANY)
    return pl.pallas_call(
        kernel,
        out_shape=(
            jax.ShapeDtypeStruct((16, 128), f32),
            jax.ShapeDtypeStruct((3, 128, INNER), bf16),
            jax.ShapeDtypeStruct((64, D), bf16),
        ),
        in_specs=[vmem, vmem, vmem, vmem, hbm, hbm, vmem],
        out_specs=(vmem, vmem, vmem),
        scratch_shapes=[
            pltpu.VMEM((3, 128, 256), f32),
            pltpu.VMEM((64, 512), f32),
            pltpu.VMEM((2, 128, QKV), bf16),
            pltpu.VMEM((2, 64, SLICE), bf16),
            pltpu.VMEM((8, 2, SLICE), f32),
            pltpu.VMEM((16, 256), f32),
            pltpu.VMEM((16, CROP, D), bf16),
            pltpu.VMEM((D, 16 * CROP), bf16),
            pltpu.VMEM((16, 128, QKV), bf16),
            pltpu.VMEM((16, 64, SLICE), bf16),
            pltpu.VMEM((8, 2, SLICE), f32),
            pltpu.VMEM((16, CROP, QKV), bf16),
            pltpu.VMEM((16, CROP, CROP), f32),
            pltpu.VMEM((16, D), f32),
            pltpu.VMEM((8, 16, 128), f32),
            pltpu.VMEM((16, 16, 256), bf16),
            pltpu.VMEM((16, 16, 256), bf16),
            pltpu.VMEM((16, 16, SLICE), f32),
            pltpu.VMEM((8, 24, 256), f32),
            pltpu.VMEM((16, 16, 128), f32),
            pltpu.VMEM((16, 16, SLICE + 128), bf16),
            pltpu.VMEM((8, 16, 128), f32),
            pltpu.VMEM((8, 16, 128), f32),
            pltpu.VMEM((16, CROP, 256), bf16),
            pltpu.VMEM((16, 2, 128, 128), bf16),
            pltpu.VMEM((16, 2, 128, 128), bf16),
            pltpu.VMEM((3, 128, 128), bf16),
            pltpu.VMEM((128, SLICE), f32),
            pltpu.VMEM((64, SLICE), bf16),
            pltpu.VMEM((CROP, CROP), f32),
            pltpu.VMEM((HEADS, 2 * CROP), f32),
            pltpu.SemaphoreType.DMA((4,)),
            pltpu.SemaphoreType.DMA((11,)),
            pltpu.SemaphoreType.DMA((11,)),
            pltpu.SemaphoreType.DMA,
            pltpu.SemaphoreType.DMA((16,)),
        ]
        + [pltpu.SemaphoreType.DMA((8,))] * 6,
        compiler_params=pltpu.CompilerParams(
            collective_id=0, has_side_effects=True, vmem_limit_bytes=52 * 1024 * 1024
        ),
        name="encoder",
    )(*args)


STEPS = 4


def adam_kernel(
    share, o_grad, gain, gain_m, gain_s, in_w, in_m, in_s, out_w, out_m, out_s,
    new_in_w, new_in_m, new_in_s, new_out_w, new_out_m, new_out_s, new_gw, new_gm, new_gs,
    column,
):
    step = pl.program_id(0)
    rows = 128 // STEPS
    gain_row = gain[...].astype(bf16).astype(f32)
    lane = lax.broadcasted_iota(jnp.int32, (rows, 128), 1)
    sub = lax.broadcasted_iota(jnp.int32, (rows, 128), 0)
    gain_col = jnp.sum(jnp.where(lane == sub + step * rows, gain_row, 0.0), axis=1, keepdims=True)

    def part(j, total):
        i, cols = j // 4, pl.ds(pl.multiple_of(j * 256, 256), 256)
        inner = pl.ds(pl.multiple_of((j % 4) * 256, 256), 256)
        master = in_w[:, cols]
        piece = share[i, :, inner].astype(f32)
        new = adam_update(master, in_m[:, cols], in_s[:, cols], piece * gain_col, weight_decay)
        new_in_w[:, cols], new_in_m[:, cols], new_in_s[:, cols] = new
        terms = piece * master.astype(bf16).astype(f32)
        return total + terms[:, :128] + terms[:, 128:]

    total = lax.fori_loop(0, 12, part, jnp.zeros((rows, 128), f32))

    def out_part(j, _):
        cols = pl.ds(pl.multiple_of(j * 512, 512), 512)
        new = adam_update(
            out_w[:, cols], out_m[:, cols], out_s[:, cols], o_grad[:, cols].astype(f32), weight_decay
        )
        new_out_w[:, cols], new_out_m[:, cols], new_out_s[:, cols] = new
        return 0

    lax.fori_loop(0, 4, out_part, 0)
    column[pl.ds(pl.multiple_of(step * rows, rows), rows), :] = jnp.broadcast_to(
        jnp.sum(total, axis=1, keepdims=True), (rows, 128)
    )

    @pl.when(step == STEPS - 1)
    def _():
        square = lax.broadcasted_iota(jnp.int32, (128, 128), 0) == lax.broadcasted_iota(
            jnp.int32, (128, 128), 1
        )
        grad = jnp.sum(jnp.where(square, column[...], 0.0), axis=0, keepdims=True)
        new_gw[...], new_gm[...], new_gs[...] = adam_update(
            gain[...], gain_m[...], gain_s[...], grad, 0.0
        )


def run_adam(share, o_grad, gains, inputs, outputs):
    one = pl.BlockSpec((1, 128), lambda i: (0, 0))
    big = pl.BlockSpec((128 // STEPS, 3 * INNER), lambda i: (i, 0))
    mid = pl.BlockSpec((64 // STEPS, D), lambda i: (i, 0))
    shares = pl.BlockSpec((3, 128 // STEPS, INNER), lambda i: (0, i, 0))
    return pl.pallas_call(
        adam_kernel,
        grid=(STEPS,),
        out_shape=[jax.ShapeDtypeStruct((128, 3 * INNER), f32)] * 3
        + [jax.ShapeDtypeStruct((64, D), f32)] * 3
        + [jax.ShapeDtypeStruct((1, 128), f32)] * 3,
        in_specs=[shares, mid] + [one] * 3 + [big] * 3 + [mid] * 3,
        out_specs=[big] * 3 + [mid] * 3 + [one] * 3,
        scratch_shapes=[pltpu.VMEM((128, 128), f32)],
        compiler_params=pltpu.CompilerParams(vmem_limit_bytes=24 * 1024 * 1024),
        name="adam",
    )(share, o_grad, *gains, *inputs, *outputs)


def per_device(
    frames, crop_starts, pairing, bias_table,
    input_master, input_moment, input_square,
    output_master, output_moment, output_square,
    gain_master, gain_moment, gain_square,
):
    t = 2 * (lax.axis_index("dp") // 2) + lax.axis_index("shard") % 2
    gains = [g.reshape(1, 128) for g in (gain_master, gain_moment, gain_square)]
    losses, s_grad, o_grad = run_kernel(
        *run_norm(frames, crop_starts), pairing.reshape(1, 256), bias_table,
        input_master, output_master, gains[0],
    )
    pair_losses = lax.dynamic_slice(losses, (2 * t, 0), (2, 1)).reshape(2)
    new = run_adam(
        s_grad, o_grad, gains,
        (input_master, input_moment, input_square),
        (output_master, output_moment, output_square),
    )
    return (pair_losses, *new[:6], *(g.reshape(128) for g in new[6:]))


def solution(mesh):
    one = P("shard")
    two = P("shard", None)
    items = P(("dp", "shard"))
    in_specs = (P(("dp", "shard"), None, None), items, P(), P()) + (two,) * 6 + (one,) * 3
    out_specs = (items,) + (two,) * 6 + (one,) * 3
    return jax.shard_map(
        per_device, mesh=mesh, in_specs=in_specs, out_specs=out_specs, check_vma=False
    )
```

time: 166 us -> 122 us (0.73)
  the two profiles are of different devices: /device:TPU:112 before, /device:TPU:1 now
where the time goes in v2:
time: 122 us
  Pallas kernels  115 us (94%)
  local copies, waits for them, and re-layouts  5.96 us (5%)
    pallas_call x1, Pallas kernels, run_kernel(): pl.pallas_call(kernel, out_shape=(jax.ShapeDtypeStruct((16, 128), f32), j...  105 us
    unnamed x28, local copies, waits for them, and re-layouts  5.33 us
    pallas_call x1, Pallas kernels, run_adam(): pl.pallas_call(adam_kernel, grid=(STEPS,), out_shape=[jax.ShapeDtypeStruc...  5.11 us
    pallas_call x1, Pallas kernels, run_norm(): pl.pallas_call(norm_kernel, grid=(2,), out_shape=(jax.ShapeDtypeStruct((2...  4.66 us

profile of v2, /device:TPU:1, one launch (start us, length us, event | category | flops | bytes accessed | tf_op | source)
XLA Modules:
  0.0 121.8 jit_solution(261900279270694149)
XLA Ops:
  0.6 0.0 copy-start.9
  0.7 0.0 copy-start.8
  0.7 0.0 copy-start.10
  0.7 0.0 copy-start.1
  0.7 1.6 %copy-done.1 = bf16[2,256,2048]{2,1,0:T(8,128)(2,1)S(1)} copy-done((bf16[2,256,2048]{2,1,0:T(8,128)(2,1)S(1)}, bf16[2,256,2048]{2,1,0:T(8,128)(2,1)}, u32[]{:S(2)}) %copy-start.1) | copy-done | bytes 2097176
  2.3 0.7 copy-done.11
  3.0 4.7 %norm.1 = (bf16[2,128,2048]{2,1,0:T(8,128)(2,1)S(1)}, f32[2,8,256]{2,1,0:T(8,128)S(1)}) custom-call(s32[2]{0:T(128)S(1)} %copy-done.11, bf16[2,256,2048]{2,1,0:T(8,128)(2,1)S(1)} %copy-done.1), custom_call_target="tpu_custom_call" | custom-call | tf_op jit(solution)/shard_map/norm/pallas_call | solution.py:522
  7.6 0.0 copy-start.5
  7.6 1.0 copy-done.5
  8.6 0.0 copy-done.9
  8.6 0.0 copy-done.8
  8.6 0.0 copy-done.10
  8.6 0.0 copy-done.2
  8.6 0.0 copy-start
  8.6 0.0 copy-start.3
  8.6 0.0 copy-start.12
  8.6 0.0 copy-start.13
  8.7 105.2 %encoder.1 = (f32[16,128]{1,0:T(8,128)S(1)}, bf16[3,128,1024]{2,1,0:T(8,128)(2,1)S(1)}, bf16[64,2048]{1,0:T(8,128)(2,1)S(1)}) custom-call(bf16[2,128,2048]{2,1,0:T(8,128)(2,1)} %copy-done.5, f32[2,8,256]{2,1,0:T(8,128)S(1)} %get-tuple-element.25.mc, s32[1,256]{1,0:T(1,128)S(1)} %bitcast.9, f32[8,255]{1,0:T(8,128)S(1)} %copy-done.8, f32[128,3072]{1,0:T(8,128)} %in_w.1, ...), custom_call_target="tpu_custom_call" | custom-call | tf_op jit(solution)/shard_map/encoder/pallas_call | solution.py:546
  113.9 0.6 dynamic-slice_reduce_fusion
  114.5 0.0 copy-done
  114.6 0.0 copy-start.6
  114.6 1.0 copy-done.6
  115.6 1.0 copy-done.7
  116.7 5.1 %adam.1 = (f32[128,3072]{1,0:T(8,128)}, f32[128,3072]{1,0:T(8,128)}, f32[128,3072]{1,0:T(8,128)}, f32[64,2048]{1,0:T(8,128)}, f32[64,2048]{1,0:T(8,128)}, /*inde...) custom-call(bf16[3,128,1024]{2,1,0:T(8,128)(2,1)S(1)} %get-tuple-element.27.share, ...), custom_call_target="tpu_custom_call" | custom-call | tf_op jit(solution)/shard_map/adam/pallas_call | solution.py:657
  (8 shorter events, 0.0 us)
Async XLA Ops:
  0.6 8.0 %copy-start.9 = (f32[128]{0:T(128)S(1)}, f32[128]{0:T(128)}, u32[]{:S(2)}) copy-start(f32[128]{0:T(128)} %param.23) | copy-start | bytes 1540
  0.7 7.9 %copy-start.8 = (f32[8,255]{1,0:T(8,128)S(1)}, f32[8,255]{1,0:T(8,128)}, u32[]{:S(2)}) copy-start(f32[8,255]{1,0:T(8,128)} %bias.1) | copy-start | bytes 24484
  0.7 7.9 %copy-start.10 = (s32[256]{0:T(256)S(1)}, s32[256]{0:T(256)}, u32[]{:S(2)}) copy-start(s32[256]{0:T(256)} %param.15) | copy-start | bytes 3076
  0.7 1.6 %copy-start.1 = (bf16[2,256,2048]{2,1,0:T(8,128)(2,1)S(1)}, bf16[2,256,2048]{2,1,0:T(8,128)(2,1)}, u32[]{:S(2)}) copy-start(bf16[2,256,2048]{2,1,0:T(8,128)(2,1)} %frames.1) | copy-start | bytes 6291460
  2.3 0.7 copy-start.11
  2.9 5.7 %copy-start.2 = (f32[64,2048]{1,0:T(8,128)S(1)}, f32[64,2048]{1,0:T(8,128)}, u32[]{:S(2)}) copy-start(f32[64,2048]{1,0:T(8,128)} %out_w.1) | copy-start | bytes 1572868
  3.0 111.6 %copy-start.4 = (f32[128,3072]{1,0:T(8,128)S(1)}, f32[128,3072]{1,0:T(8,128)}, u32[]{:S(2)}) copy-start(f32[128,3072]{1,0:T(8,128)} %in_s.1) | copy-start | bytes 4718596
  7.6 1.0 copy-start.5
  8.6 105.9 %copy-start = (f32[128,3072]{1,0:T(8,128)S(1)}, f32[128,3072]{1,0:T(8,128)}, u32[]{:S(2)}) copy-start(f32[128,3072]{1,0:T(8,128)} %in_w.1) | copy-start | bytes 4718596
  8.6 105.9 %copy-start.3 = (f32[128,3072]{1,0:T(8,128)S(1)}, f32[128,3072]{1,0:T(8,128)}, u32[]{:S(2)}) copy-start(f32[128,3072]{1,0:T(8,128)} %in_m.1) | copy-start | bytes 4718596
  8.6 105.9 %copy-start.12 = (f32[128]{0:T(128)S(1)}, f32[128]{0:T(128)}, u32[]{:S(2)}) copy-start(f32[128]{0:T(128)} %param.24) | copy-start | bytes 1540
  8.6 105.9 %copy-start.13 = (f32[128]{0:T(128)S(1)}, f32[128]{0:T(128)}, u32[]{:S(2)}) copy-start(f32[128]{0:T(128)} %param.25) | copy-start | bytes 1540
  114.6 1.0 copy-start.6
  115.6 1.0 copy-start.7

commit v3 on v2

--- a/solution.py
+++ b/solution.py
@@ -28,13 +28,24 @@
 
 f32 = jnp.float32
 bf16 = jnp.bfloat16
-HIGHEST = lax.Precision.HIGHEST
 NT = (((1,), (1,)), ((), ()))
 TN = (((0,), (0,)), ((), ()))
 
 
-def dot(a, b, dims=(((1,), (0,)), ((), ())), precision=None):
-    return lax.dot_general(a, b, dims, precision=precision, preferred_element_type=f32)
+def dot(a, b, dims=(((1,), (0,)), ((), ()))):
+    return lax.dot_general(a, b, dims, preferred_element_type=f32)
+
+
+def split(a):
+    high = a.astype(bf16)
+    return high, (a - high.astype(f32)).astype(bf16)
+
+
+def dot3(a, b, dims=(((1,), (0,)), ((), ()))):
+    rows = a.shape[0]
+    high, low = split(a)
+    both = dot(jnp.concatenate([high, low], axis=0), b[0], dims)
+    return both[:rows] + both[rows:] + dot(high, b[1], dims)
 
 
 def adam_update(master, moment, square, gradient, decay):
@@ -48,7 +59,7 @@
     return (master_new, moment_new, square_new)
 
 
-W, WO, MC, MM, EA, PO, GR, TO, LA, GM, RS = range(11)
+W, WO, MC, MM, EA, PO, GR, TO, LA, GM, RZ, RY, BQ, BK = range(14)
 
 
 def item_of(row):
@@ -63,8 +74,8 @@
     loss_out, s_out, o_out,
     wraw, woraw, wp, wo2, mcsend, target,
     xbuf, xt, wbuf, wobuf, mcbuf, qkvbuf, probs, arows, mmbuf, eabuf, easend, pobuf, grbuf,
-    tobuf, labuf, gmsend, gmbuf, gp, rsend, rbuf, s_fin, o_tmp, o_fin, band, table,
-    lsem, ssem, rsem, xssem, xrsem, q_send, q_recv, v_send, v_recv, o_send, o_recv,
+    tobuf, labuf, gmsend, gmbuf, gp, zsend, ysend, zrecv, yrecv, mid, qrecv, krecv, s_fin, o_tmp, o_fin, band, table,
+    lsem, ssem, rsem, xssem, xrsem, q_send, q_recv, k_send, k_recv, v_send, v_recv, o_send, o_recv,
 ):
     dp = lax.axis_index("dp")
     sh = lax.axis_index("shard")
@@ -73,12 +84,16 @@
     base = yl * 8 + z * 2
     t = 2 * x + c
     p = yh * 8 + yl * 4 + z
+    y = yh * 2 + yl
 
     def tp_dev(m):
         return ((m // 2) * 2 + yh, base + m % 2)
 
     def plane_dev(q):
         return (x * 2 + q // 8, ((q // 4) % 2) * 8 + (q % 4) * 2 + c)
+
+    def at(y, z2):
+        return (x * 2 + y // 2, (y % 2) * 8 + z2 * 2 + c)
 
     def push(src, dst, send, recv, dev):
         pltpu.make_async_remote_copy(
@@ -287,9 +302,7 @@
 
     wo_slice = wobuf[...].reshape(INNER, SLICE)
     summed = jnp.concatenate([mmbuf[h] for h in range(8)], axis=1)
-    high = summed.astype(bf16)
-    low = (summed - high.astype(f32)).astype(bf16)
-    product = dot(jnp.concatenate([high, low], axis=0), wo_slice)
+    product = dot(jnp.concatenate(split(summed), axis=0), wo_slice)
     means = jnp.concatenate([mcbuf[m] for m in range(8)], axis=0)
     pooled = means + (product[:16] + product[16:]) * (1.0 / CROP)
     pobuf[p] = pooled
@@ -302,22 +315,30 @@
     lax.fori_loop(1, 16, send_po, 0, unroll=True)
 
     own = (lane16 == sub16 + p * 16).astype(f32)
-    await_bytes(pobuf.at[pl.ds(0, 15)], rsem.at[PO])
-    everyone = pobuf[...].reshape(256, SLICE)
-    grbuf[t, pl.ds(0, 16), :] = dot(pooled, everyone, NT, HIGHEST)
-    grbuf[t, pl.ds(16, 8), :] = dot(jnp.ones((8, SLICE), f32), everyone * everyone, NT, HIGHEST)
-
-    def send_gr(k, _):
-        push(grbuf.at[t], grbuf.at[t], ssem.at[GR], rsem.at[GR], tp_dev((t + k) % 8))
-        return 0
-
-    lax.fori_loop(1, 8, send_gr, 0, unroll=True)
-
     for s in range(16):
         q = (s % 2) * 8 + s // 2
         easend[q, :, :128] = arows[:, s * 128 : (s + 1) * 128].astype(bf16)
         easend[q, :, 128:] = mmbuf[s // 2].astype(bf16)
     eabuf[p] = easend[p]
+
+    def send_ea(k, _):
+        q = (p + k) % 16
+        push(easend.at[q], eabuf.at[p], ssem.at[EA], rsem.at[EA], plane_dev(q))
+        return 0
+
+    lax.fori_loop(1, 16, send_ea, 0)
+    await_bytes(pobuf.at[pl.ds(0, 15)], rsem.at[PO])
+    everyone = pobuf[...].reshape(256, SLICE)
+    parts = split(everyone)
+    grbuf[t, pl.ds(0, 16), :] = dot3(pooled, parts, NT)
+    squares = jnp.concatenate(split(everyone * everyone), axis=1)
+    grbuf[t, pl.ds(16, 8), :] = dot(jnp.ones((8, 2 * SLICE), bf16), squares, NT)
+
+    def send_gr(k, _):
+        push(grbuf.at[t], grbuf.at[t], ssem.at[GR], rsem.at[GR], tp_dev((t + k) % 8))
+        return 0
+
+    lax.fori_loop(1, 8, send_gr, 0, unroll=True)
     await_bytes(grbuf.at[pl.ds(0, 7)], rsem.at[GR])
     gram = grbuf[0]
     for m in range(1, 8):
@@ -327,7 +348,7 @@
     sims = gram[:16] * inv_col * inv_row * inv_tau
     exponents = jnp.where(own > 0.5, 0.0, jnp.exp(sims - inv_tau))
     totals = jnp.sum(exponents, axis=1, keepdims=True)
-    tobuf[p] = jnp.broadcast_to(totals, (16, 128))
+    tobuf[p] = jnp.sum(own * totals, axis=0, keepdims=True)
 
     def send_to(k, _):
         q = (p + k) % 16
@@ -338,14 +359,9 @@
     losses = jnp.log(totals) + inv_tau - jnp.sum(sims * target[...], axis=1, keepdims=True)
     loss_out[...] = jnp.broadcast_to(losses, (16, 128))
     await_bytes(tobuf.at[pl.ds(0, 15)], rsem.at[TO])
-    columns = tobuf[...].reshape(256, 128)
-    columns = jnp.concatenate([columns, columns], axis=1)
-    eye = lax.broadcasted_iota(jnp.int32, (256, 256), 0) == (
-        lax.broadcasted_iota(jnp.int32, (256, 256), 1)
-    )
-    column_totals = jnp.sum(jnp.where(eye, columns, 0.0), axis=0, keepdims=True)
+    column_totals = jnp.sum(tobuf[...], axis=0)
     weights = exponents / totals + exponents / column_totals - 2.0 * target[...]
-    grad_embedding = dot(weights * inv_row, everyone, precision=HIGHEST) * inv_tau
+    grad_embedding = dot3(weights * inv_row, parts) * inv_tau
     along = jnp.sum(weights * sims, axis=1, keepdims=True)
     grad_pooled = (grad_embedding - pooled * inv_col * along) * inv_col
     grad_frame = (grad_pooled * (1.0 / CROP)).astype(bf16)
@@ -362,25 +378,12 @@
     lax.fori_loop(1, 8, send_gm, 0, unroll=True)
     gmbuf[t] = gmsend[t]
 
-    def send_ea(k, _):
-        q = (p + k) % 16
-        push(easend.at[q], eabuf.at[p], ssem.at[EA], rsem.at[EA], plane_dev(q))
-        return 0
-
-    lax.fori_loop(1, 16, send_ea, 0)
     await_bytes(gmbuf.at[pl.ds(0, 7)], rsem.at[GM])
     gm = gmbuf[0]
     for m in range(1, 8):
         gm = gm + gmbuf[m]
     grad_mixed = gm.astype(bf16)
     labuf[p, :, SLICE:] = grad_mixed
-
-    def send_la(k, _):
-        q = (p + k) % 16
-        push(labuf.at[p], labuf.at[p], ssem.at[LA], rsem.at[LA], plane_dev(q))
-        return 0
-
-    lax.fori_loop(1, 16, send_la, 0)
     sub_item = lax.broadcasted_iota(jnp.int32, (16, 128), 0)
 
     def backward(step, _):
@@ -401,26 +404,59 @@
     lax.fori_loop(0, 4, backward, 0)
 
     def scatter(k, _):
-        pair_at = (p + k) % 8
-        rows = pl.ds(pl.multiple_of(pair_at * 256, 256), 256)
-        value = dot(xt[rows, :], gp[...].reshape(16 * CROP, 256)).astype(bf16)
-        for half in range(2):
-            q = half * 8 + pair_at
-            block = value[half * 128 : (half + 1) * 128]
+        z2 = (z + k) % 4
+        for yl2 in range(2):
+            rows = pl.ds(pl.multiple_of((yl2 * 4 + z2) * 256, 256), 256)
+            value = dot(xt[rows, :], gp[...].reshape(16 * CROP, 256)).astype(bf16)
+            for half in range(2):
+                y2 = half * 2 + yl2
+                block = value[half * 128 : (half + 1) * 128]
+                zsend[z2, y2] = block[:, :128]
+                ysend[y2, z2] = block[:, 128:]
+
+                @pl.when(y2 != y)
+                def _():
+                    push(ysend.at[y2, z2], yrecv.at[y, z2], ssem.at[RY], rsem.at[RY], at(y2, z))
+
+        @pl.when(z2 != z)
+        def _():
+            push(zsend.at[z2], zrecv.at[z], ssem.at[RZ], rsem.at[RZ], at(y, z2))
+
+        def send_la(j, _):
+            q = (p + j) % 16
 
             @pl.when(q != p)
             def _():
-                for i in range(2):
-                    rsend[q, i] = block[:, i * 128 : (i + 1) * 128]
-                push(rsend.at[q], rbuf.at[p], ssem.at[RS], rsem.at[RS], plane_dev(q))
-
-            @pl.when(q == p)
-            def _():
-                for i in range(2):
-                    rbuf[p, i] = block[:, i * 128 : (i + 1) * 128]
-        return 0
-
-    lax.fori_loop(1, 9, scatter, 0)
+                push(labuf.at[p], labuf.at[p], ssem.at[LA], rsem.at[LA], plane_dev(q))
+            return 0
+
+        lax.fori_loop(4 * k - 3, 4 * k + 1, send_la, 0)
+        return 0
+
+    lax.fori_loop(1, 5, scatter, 0)
+    zrecv[z] = zsend[z]
+    yrecv[y] = ysend[y]
+
+    def add_up(ref, *index):
+        total = ref[(0, *index)].astype(f32)
+        for q in range(1, 4):
+            total = total + ref[(q, *index)].astype(f32)
+        return total.astype(bf16)
+
+    await_bytes(zrecv.at[pl.ds(0, 3)], rsem.at[RZ])
+    for i in range(4):
+        mid[0, i] = add_up(zrecv, i)
+    for j in range(1, 4):
+        y2 = (y + j) % 4
+        push(mid.at[0, y2], qrecv.at[y], ssem.at[BQ], rsem.at[BQ], at(y2, z))
+    qrecv[y] = mid[0, y]
+    await_bytes(yrecv.at[pl.ds(0, 3)], rsem.at[RY])
+    for i in range(4):
+        mid[1, i] = add_up(yrecv, i)
+    for j in range(1, 4):
+        z2 = (z + j) % 4
+        push(mid.at[1, z2], krecv.at[z], ssem.at[BK], rsem.at[BK], at(y, z2))
+    krecv[z] = mid[1, z]
 
     await_bytes(eabuf.at[pl.ds(0, 15)], rsem.at[EA])
     await_bytes(labuf.at[pl.ds(0, 15)], rsem.at[LA])
@@ -448,20 +484,20 @@
 
     each_target(send_early)
 
-    await_bytes(rbuf.at[pl.ds(0, 15)], rsem.at[RS])
-    for i in range(2):
-        total = rbuf[0, i].astype(f32)
-        for q in range(1, 16):
-            total = total + rbuf[q, i].astype(f32)
-        s_fin[i] = total.astype(bf16)
-
-    def send_s(j):
-        push(
-            s_fin.at[pl.ds(0, 2)], s_out.at[pl.ds(0, 2), :, s_cols],
-            q_send.at[j], q_recv.at[t], (j, base + yh),
-        )
-
-    each_target(send_s)
+    def send_part(i, sends, recvs):
+        def send(j):
+            push(
+                s_fin.at[i], s_out.at[i, :, s_cols], sends.at[j], recvs.at[t], (j, base + yh)
+            )
+
+        each_target(send)
+
+    await_bytes(qrecv.at[pl.ds(0, 3)], rsem.at[BQ])
+    s_fin[0] = add_up(qrecv)
+    send_part(0, q_send, q_recv)
+    await_bytes(krecv.at[pl.ds(0, 3)], rsem.at[BK])
+    s_fin[1] = add_up(krecv)
+    send_part(1, k_send, k_recv)
 
     @pl.when(c == yh)
     def _():
@@ -473,7 +509,8 @@
         def _():
             await_bytes(s_fin.at[2], v_recv.at[m])
             await_bytes(o_fin, o_recv.at[m])
-            await_bytes(s_fin.at[pl.ds(0, 2)], q_recv.at[m])
+            await_bytes(s_fin.at[0], q_recv.at[m])
+            await_bytes(s_fin.at[1], k_recv.at[m])
         return 0
 
     lax.fori_loop(0, 8, collect, 0)
@@ -481,14 +518,17 @@
     def sent(j):
         await_bytes(s_fin.at[2], v_send.at[j])
         await_bytes(o_fin, o_send.at[j])
-        await_bytes(s_fin.at[pl.ds(0, 2)], q_send.at[j])
+        await_bytes(s_fin.at[0], q_send.at[j])
+        await_bytes(s_fin.at[1], k_send.at[j])
 
     each_target(sent)
     await_bytes(xbuf.at[pl.ds(0, 14)], xssem)
     for sem, ref in (
-        (W, wbuf), (WO, wobuf), (EA, eabuf), (PO, pobuf), (TO, tobuf), (LA, labuf), (RS, rbuf),
+        (W, wbuf), (WO, wobuf), (EA, eabuf), (PO, pobuf), (TO, tobuf), (LA, labuf),
     ):
         await_bytes(ref.at[pl.ds(0, 15)], ssem.at[sem])
+    for sem, ref in ((RZ, zrecv), (RY, yrecv), (BQ, qrecv), (BK, krecv)):
+        await_bytes(ref.at[pl.ds(0, 3)], ssem.at[sem])
     for sem, ref in ((MC, mcbuf), (MM, mmbuf), (GR, grbuf), (GM, gmbuf)):
         await_bytes(ref.at[pl.ds(0, 7)], ssem.at[sem])
 
@@ -572,27 +612,32 @@
             pltpu.VMEM((16, 16, 256), bf16),
             pltpu.VMEM((16, 16, SLICE), f32),
             pltpu.VMEM((8, 24, 256), f32),
-            pltpu.VMEM((16, 16, 128), f32),
+            pltpu.VMEM((16, 1, 256), f32),
             pltpu.VMEM((16, 16, SLICE + 128), bf16),
             pltpu.VMEM((8, 16, 128), f32),
             pltpu.VMEM((8, 16, 128), f32),
             pltpu.VMEM((16, CROP, 256), bf16),
-            pltpu.VMEM((16, 2, 128, 128), bf16),
-            pltpu.VMEM((16, 2, 128, 128), bf16),
+            pltpu.VMEM((4, 4, 128, 128), bf16),
+            pltpu.VMEM((4, 4, 128, 128), bf16),
+            pltpu.VMEM((4, 4, 128, 128), bf16),
+            pltpu.VMEM((4, 4, 128, 128), bf16),
+            pltpu.VMEM((2, 4, 128, 128), bf16),
+            pltpu.VMEM((4, 128, 128), bf16),
+            pltpu.VMEM((4, 128, 128), bf16),
             pltpu.VMEM((3, 128, 128), bf16),
             pltpu.VMEM((128, SLICE), f32),
             pltpu.VMEM((64, SLICE), bf16),
             pltpu.VMEM((CROP, CROP), f32),
             pltpu.VMEM((HEADS, 2 * CROP), f32),
             pltpu.SemaphoreType.DMA((4,)),
-            pltpu.SemaphoreType.DMA((11,)),
-            pltpu.SemaphoreType.DMA((11,)),
+            pltpu.SemaphoreType.DMA((14,)),
+            pltpu.SemaphoreType.DMA((14,)),
             pltpu.SemaphoreType.DMA,
             pltpu.SemaphoreType.DMA((16,)),
         ]
-        + [pltpu.SemaphoreType.DMA((8,))] * 6,
+        + [pltpu.SemaphoreType.DMA((8,))] * 8,
         compiler_params=pltpu.CompilerParams(
-            collective_id=0, has_side_effects=True, vmem_limit_bytes=52 * 1024 * 1024
+            collective_id=0, has_side_effects=True, vmem_limit_bytes=40 * 1024 * 1024
         ),
         name="encoder",
     )(*args)

time: 122 us -> 118 us (0.967)
  Pallas kernels: 115 us -> 112 us
    pallas_call x1, Pallas kernels: 105 us -> 102 us  [run_kernel(): pl.pallas_call(kernel, out_shape=(jax.ShapeDtypeStruct((16, 128), f32), j...]
    unnamed x28 -> x26, local copies, waits for them, and re-layouts: 5.33 us -> 4.47 us
where the time goes in v3:
time: 118 us
  Pallas kernels  112 us (95%)
  local copies, waits for them, and re-layouts  5.11 us (4%)
    pallas_call x1, Pallas kernels, run_kernel(): pl.pallas_call(kernel, out_shape=(jax.ShapeDtypeStruct((16, 128), f32), j...  102 us
    pallas_call x1, Pallas kernels, run_adam(): pl.pallas_call(adam_kernel, grid=(STEPS,), out_shape=[jax.ShapeDtypeStruc...  5.11 us
    pallas_call x1, Pallas kernels, run_norm(): pl.pallas_call(norm_kernel, grid=(2,), out_shape=(jax.ShapeDtypeStruct((2...  4.68 us
    unnamed x26, local copies, waits for them, and re-layouts  4.47 us

profile of v3, /device:TPU:1, one launch (start us, length us, event | category | flops | bytes accessed | tf_op | source)
XLA Modules:
  0.0 118.0 jit_solution(291151327146587280)
XLA Ops:
  0.6 0.0 copy-start
  0.7 0.0 copy-start.1
  0.7 1.7 %copy-done.1 = bf16[2,256,2048]{2,1,0:T(8,128)(2,1)S(1)} copy-done((bf16[2,256,2048]{2,1,0:T(8,128)(2,1)S(1)}, bf16[2,256,2048]{2,1,0:T(8,128)(2,1)}, u32[]{:S(2)}) %copy-start.1) | copy-done | bytes 2097176
  2.4 0.7 copy-done.10
  3.1 4.7 %norm.1 = (bf16[2,128,2048]{2,1,0:T(8,128)(2,1)S(1)}, f32[2,8,256]{2,1,0:T(8,128)S(1)}) custom-call(s32[2]{0:T(128)S(1)} %copy-done.10, bf16[2,256,2048]{2,1,0:T(8,128)(2,1)S(1)} %copy-done.1), custom_call_target="tpu_custom_call" | custom-call | tf_op jit(solution)/shard_map/norm/pallas_call | solution.py:562
  7.7 0.0 copy-done
  7.7 0.0 copy-done.2
  7.8 0.0 copy-done.7
  7.8 0.0 copy-done.8
  7.8 0.0 copy-done.9
  7.8 0.0 copy-start.3
  7.8 0.0 copy-start.4
  7.8 0.0 copy-start.11
  7.8 0.0 copy-start.12
  7.8 102.3 %encoder.1 = (f32[16,128]{1,0:T(8,128)S(1)}, bf16[3,128,1024]{2,1,0:T(8,128)(2,1)S(1)}, bf16[64,2048]{1,0:T(8,128)(2,1)S(1)}) custom-call(bf16[2,128,2048]{2,1,0:T(8,128)(2,1)S(1)} %get-tuple-element.24.xn, f32[2,8,256]{2,1,0:T(8,128)S(1)} %get-tuple-element.25.mc, s32[1,256]{1,0:T(1,128)S(1)} %bitcast.9, f32[8,255]{1,0:T(8,128)S(1)} %copy-done.7, ...), custom_call_target="tpu_custom_call" | custom-call | tf_op jit(solution)/shard_map/encoder/pallas_call | solution.py:586
  110.1 0.6 dynamic-slice_reduce_fusion
  110.8 0.0 copy-done.3
  110.8 0.0 copy-done.4
  110.8 0.0 copy-done.11
  110.8 0.0 copy-done.12
  110.8 0.0 copy-start.5
  110.8 1.0 copy-done.5
  111.8 1.0 copy-done.6
  112.9 5.1 %adam.1 = (f32[128,3072]{1,0:T(8,128)}, f32[128,3072]{1,0:T(8,128)}, f32[128,3072]{1,0:T(8,128)}, f32[64,2048]{1,0:T(8,128)}, f32[64,2048]{1,0:T(8,128)}, /*inde...) custom-call(bf16[3,128,1024]{2,1,0:T(8,128)(2,1)S(1)} %get-tuple-element.27.share, ...), custom_call_target="tpu_custom_call" | custom-call | tf_op jit(solution)/shard_map/adam/pallas_call | solution.py:702
  (6 shorter events, 0.0 us)
Async XLA Ops:
  0.6 7.1 %copy-start = (f32[128,3072]{1,0:T(8,128)S(1)}, f32[128,3072]{1,0:T(8,128)}, u32[]{:S(2)}) copy-start(f32[128,3072]{1,0:T(8,128)} %in_w.1) | copy-start | bytes 4718596
  0.7 1.7 %copy-start.1 = (bf16[2,256,2048]{2,1,0:T(8,128)(2,1)S(1)}, bf16[2,256,2048]{2,1,0:T(8,128)(2,1)}, u32[]{:S(2)}) copy-start(bf16[2,256,2048]{2,1,0:T(8,128)(2,1)} %frames.1) | copy-start | bytes 6291460
  2.4 0.7 copy-start.10
  3.0 4.7 %copy-start.2 = (f32[64,2048]{1,0:T(8,128)S(1)}, f32[64,2048]{1,0:T(8,128)}, u32[]{:S(2)}) copy-start(f32[64,2048]{1,0:T(8,128)} %out_w.1) | copy-start | bytes 1572868
  3.0 4.7 %copy-start.7 = (f32[8,255]{1,0:T(8,128)S(1)}, f32[8,255]{1,0:T(8,128)}, u32[]{:S(2)}) copy-start(f32[8,255]{1,0:T(8,128)} %bias.1) | copy-start | bytes 24484
  3.0 4.7 %copy-start.8 = (f32[128]{0:T(128)S(1)}, f32[128]{0:T(128)}, u32[]{:S(2)}) copy-start(f32[128]{0:T(128)} %param.23) | copy-start | bytes 1540
  3.0 4.7 %copy-start.9 = (s32[256]{0:T(256)S(1)}, s32[256]{0:T(256)}, u32[]{:S(2)}) copy-start(s32[256]{0:T(256)} %param.15) | copy-start | bytes 3076
  7.8 103.0 %copy-start.3 = (f32[128,3072]{1,0:T(8,128)S(1)}, f32[128,3072]{1,0:T(8,128)}, u32[]{:S(2)}) copy-start(f32[128,3072]{1,0:T(8,128)} %in_m.1) | copy-start | bytes 4718596
  7.8 103.0 %copy-start.4 = (f32[128,3072]{1,0:T(8,128)S(1)}, f32[128,3072]{1,0:T(8,128)}, u32[]{:S(2)}) copy-start(f32[128,3072]{1,0:T(8,128)} %in_s.1) | copy-start | bytes 4718596
  7.8 103.0 %copy-start.11 = (f32[128]{0:T(128)S(1)}, f32[128]{0:T(128)}, u32[]{:S(2)}) copy-start(f32[128]{0:T(128)} %param.24) | copy-start | bytes 1540
  7.8 103.0 %copy-start.12 = (f32[128]{0:T(128)S(1)}, f32[128]{0:T(128)}, u32[]{:S(2)}) copy-start(f32[128]{0:T(128)} %param.25) | copy-start | bytes 1540
  110.8 1.0 copy-start.5
  111.8 1.0 copy-start.6

commit v4 on v3

--- a/solution.py
+++ b/solution.py
@@ -51,15 +51,21 @@
 def adam_update(master, moment, square, gradient, decay):
     moment_new = beta_one * moment + (1.0 - beta_one) * gradient
     square_new = beta_two * square + (1.0 - beta_two) * gradient * gradient
-    mean_hat = moment_new / (1.0 - beta_one**adam_step)
-    square_hat = square_new / (1.0 - beta_two**adam_step)
-    master_new = master - learn_rate * (
-        mean_hat / (jnp.sqrt(square_hat) + adam_eps) + decay * master
-    )
-    return (master_new, moment_new, square_new)
+    mean_scale = learn_rate / (1.0 - beta_one**adam_step)
+    square_scale = 1.0 / (1.0 - beta_two**adam_step)
+    step = moment_new * mean_scale / (jnp.sqrt(square_new * square_scale) + adam_eps)
+    return (master * (1.0 - learn_rate * decay) - step, moment_new, square_new)
 
 
 W, WO, MC, MM, EA, PO, GR, TO, LA, GM, RZ, RY, BQ, BK = range(14)
+
+
+def div(a, b):
+    return lax.div(a, jnp.int32(b))
+
+
+def rem(a, b):
+    return lax.rem(a, jnp.int32(b))
 
 
 def item_of(row):
@@ -74,26 +80,27 @@
     loss_out, s_out, o_out,
     wraw, woraw, wp, wo2, mcsend, target,
     xbuf, xt, wbuf, wobuf, mcbuf, qkvbuf, probs, arows, mmbuf, eabuf, easend, pobuf, grbuf,
-    tobuf, labuf, gmsend, gmbuf, gp, zsend, ysend, zrecv, yrecv, mid, qrecv, krecv, s_fin, o_tmp, o_fin, band, table,
-    lsem, ssem, rsem, xssem, xrsem, q_send, q_recv, k_send, k_recv, v_send, v_recv, o_send, o_recv,
+    tobuf, labuf, gmsend, gmbuf, gp, zsend, ysend, zrecv, yrecv, zmid, ymid, qrecv, krecv, s_fin, o_tmp, o_fin, band, table,
+    lsem, ssem, rsem, xssem, xrsem, f_send, f_recv,
 ):
     dp = lax.axis_index("dp")
     sh = lax.axis_index("shard")
-    x, yh = dp // 2, dp % 2
-    yl, z, c = sh // 8, (sh // 2) % 4, sh % 2
+    x, yh = div(dp, 2), rem(dp, 2)
+    yl, z, c = div(sh, 8), rem(div(sh, 2), 4), rem(sh, 2)
     base = yl * 8 + z * 2
     t = 2 * x + c
     p = yh * 8 + yl * 4 + z
     y = yh * 2 + yl
 
     def tp_dev(m):
-        return ((m // 2) * 2 + yh, base + m % 2)
+        return (div(m, 2) * 2 + yh, base + rem(m, 2))
 
     def plane_dev(q):
-        return (x * 2 + q // 8, ((q // 4) % 2) * 8 + (q % 4) * 2 + c)
-
-    def at(y, z2):
-        return (x * 2 + y // 2, (y % 2) * 8 + z2 * 2 + c)
+        return (x * 2 + div(q, 8), rem(div(q, 4), 2) * 8 + rem(q, 4) * 2 + c)
+
+    def at(y2, z2):
+        y2 = jnp.int32(y2)
+        return (x * 2 + div(y2, 2), rem(y2, 2) * 8 + z2 * 2 + c)
 
     def push(src, dst, send, recv, dev):
         pltpu.make_async_remote_copy(
@@ -120,30 +127,33 @@
 
     barrier = pltpu.get_barrier_semaphore()
 
-    def greet(k, _):
-        for dev in (
-            (dp, (sh + k) % 16),
-            plane_dev((p + k) % 16),
-        ):
-            pl.semaphore_signal(barrier, inc=1, device_id=dev, device_id_type=pl.DeviceIdType.MESH)
-        j = (dp * 2 + c + k) % 16
-        pl.semaphore_signal(
-            barrier, inc=1, device_id=(j // 2, base + j % 2), device_id_type=pl.DeviceIdType.MESH
-        )
-        return 0
-
-    lax.fori_loop(1, 16, greet, 0)
-
-    right = ((x + 1) % 4) * 2 + c
-    left = ((x + 3) % 4) * 2 + c
-    far = ((x + 2) % 4) * 2 + c
+    def greet(dev):
+        pl.semaphore_signal(barrier, inc=1, device_id=dev, device_id_type=pl.DeviceIdType.MESH)
+
+    for k in range(1, 16):
+        greet((dp, rem(sh + k, 16)))
+    for k in range(8):
+        greet((x * 2 + 1 - yh, div(jnp.int32(k), 4) * 8 + (k % 4) * 2 + c))
+    for k in range(1, 8):
+        j = rem(dp + k, 8)
+        greet((j, base + 1 - c))
+        if k % 2 == 0:
+            greet((j, base + c))
+        else:
+            @pl.when(div(j, 2) != x)
+            def _():
+                greet((j, base + c))
+
+    right = rem(x + 1, 4) * 2 + c
+    left = rem(x + 3, 4) * 2 + c
+    far = rem(x + 2, 4) * 2 + c
     sib = x * 2 + 1 - c
     other = 1 - 2 * c
 
     def send_item(src, slot, member):
         push(src, xbuf.at[slot], xssem, xrsem.at[slot], tp_dev(member))
 
-    pl.semaphore_wait(barrier, 45)
+    pl.semaphore_wait(barrier, 36)
     send_item(xn.at[0], 2 * t, right)
     send_item(xn.at[1], 2 * t + 1, left)
     send_item(xn.at[0], 2 * t, sib)
@@ -165,29 +175,29 @@
         wo2[core] = woraw[:, core * SLICE : (core + 1) * SLICE].astype(bf16)
 
     def send_w(k, _):
-        s = (sh + k) % 16
-        push(wp.at[s % 2], wbuf.at[sh], ssem.at[W], rsem.at[W], (dp, s))
-        return 0
-
-    lax.fori_loop(1, 16, send_w, 0)
+        s = rem(sh + k, 16)
+        push(wp.at[rem(s, 2)], wbuf.at[sh], ssem.at[W], rsem.at[W], (dp, s))
+        return 0
+
+    lax.fori_loop(1, 16, send_w, 0, unroll=True)
 
     def send_wo(k, _):
-        s = (sh + k) % 16
-        push(wo2.at[s % 2], wobuf.at[sh], ssem.at[WO], rsem.at[WO], (dp, s))
-        return 0
-
-    lax.fori_loop(1, 16, send_wo, 0)
+        s = rem(sh + k, 16)
+        push(wo2.at[rem(s, 2)], wobuf.at[sh], ssem.at[WO], rsem.at[WO], (dp, s))
+        return 0
+
+    lax.fori_loop(1, 16, send_wo, 0, unroll=True)
 
     for m in range(8):
         for i in range(2):
             mcsend[m, i : i + 1, :] = mc[i, m : m + 1, :]
 
     def send_mc(k, _):
-        m = (t + k) % 8
+        m = rem(t + k, 8)
         push(mcsend.at[m], mcbuf.at[t], ssem.at[MC], rsem.at[MC], tp_dev(m))
         return 0
 
-    lax.fori_loop(1, 8, send_mc, 0)
+    lax.fori_loop(1, 8, send_mc, 0, unroll=True)
 
     wbuf[sh] = wp[c]
     wobuf[sh] = wo2[c]
@@ -261,7 +271,7 @@
     send_item(xbuf.at[2 * right], 2 * right, sib)
 
     def fwd_near(k, _):
-        member = ((x + 3 + 2 * (k % 2)) % 4) * 2 + c + (k // 2) * other
+        member = rem(x + 3 + 2 * rem(k, 2), 4) * 2 + c + div(k, 2) * other
 
         @pl.when(k >= 2)
         def _():
@@ -292,7 +302,7 @@
     lax.fori_loop(0, 2, fwd_far, 0)
 
     def send_mm(k, _):
-        push(mmbuf.at[t], mmbuf.at[t], ssem.at[MM], rsem.at[MM], tp_dev((t + k) % 8))
+        push(mmbuf.at[t], mmbuf.at[t], ssem.at[MM], rsem.at[MM], tp_dev(rem(t + k, 8)))
         return 0
 
     lax.fori_loop(1, 8, send_mm, 0, unroll=True)
@@ -308,7 +318,7 @@
     pobuf[p] = pooled
 
     def send_po(k, _):
-        q = (p + k) % 16
+        q = rem(p + k, 16)
         push(pobuf.at[p], pobuf.at[p], ssem.at[PO], rsem.at[PO], plane_dev(q))
         return 0
 
@@ -322,11 +332,11 @@
     eabuf[p] = easend[p]
 
     def send_ea(k, _):
-        q = (p + k) % 16
+        q = rem(p + k, 16)
         push(easend.at[q], eabuf.at[p], ssem.at[EA], rsem.at[EA], plane_dev(q))
         return 0
 
-    lax.fori_loop(1, 16, send_ea, 0)
+    lax.fori_loop(1, 16, send_ea, 0, unroll=True)
     await_bytes(pobuf.at[pl.ds(0, 15)], rsem.at[PO])
     everyone = pobuf[...].reshape(256, SLICE)
     parts = split(everyone)
@@ -335,7 +345,7 @@
     grbuf[t, pl.ds(16, 8), :] = dot(jnp.ones((8, 2 * SLICE), bf16), squares, NT)
 
     def send_gr(k, _):
-        push(grbuf.at[t], grbuf.at[t], ssem.at[GR], rsem.at[GR], tp_dev((t + k) % 8))
+        push(grbuf.at[t], grbuf.at[t], ssem.at[GR], rsem.at[GR], tp_dev(rem(t + k, 8)))
         return 0
 
     lax.fori_loop(1, 8, send_gr, 0, unroll=True)
@@ -351,7 +361,7 @@
     tobuf[p] = jnp.sum(own * totals, axis=0, keepdims=True)
 
     def send_to(k, _):
-        q = (p + k) % 16
+        q = rem(p + k, 16)
         push(tobuf.at[p], tobuf.at[p], ssem.at[TO], rsem.at[TO], plane_dev(q))
         return 0
 
@@ -371,7 +381,7 @@
     labuf[p, :, :SLICE] = grad_frame
 
     def send_gm(k, _):
-        m = (t + k) % 8
+        m = rem(t + k, 8)
         push(gmsend.at[m], gmbuf.at[t], ssem.at[GM], rsem.at[GM], tp_dev(m))
         return 0
 
@@ -387,8 +397,8 @@
     sub_item = lax.broadcasted_iota(jnp.int32, (16, 128), 0)
 
     def backward(step, _):
-        for i in range(4):
-            b = step * 4 + i
+        for i in range(8):
+            b = step * 8 + i
             part = qkvbuf[b]
             q, k, v = part[:, :128], part[:, 128:256], part[:, 256:]
             prob = probs[b]
@@ -399,20 +409,28 @@
             grad_q = dot(dscores, k)
             grad_k = dot(dscores, q, TN)
             gp[b] = jnp.concatenate([grad_q, grad_k], axis=1).astype(bf16)
-        return 0
-
-    lax.fori_loop(0, 4, backward, 0)
+
+        def send_la(j, _):
+            q = rem(p + j, 16)
+            push(labuf.at[p], labuf.at[p], ssem.at[LA], rsem.at[LA], plane_dev(q))
+            return 0
+
+        lax.fori_loop(1 + 8 * step, 9 + 7 * step, send_la, 0)
+        return 0
+
+    lax.fori_loop(0, 2, backward, 0)
 
     def scatter(k, _):
-        z2 = (z + k) % 4
+        z2 = rem(z + k, 4)
         for yl2 in range(2):
             rows = pl.ds(pl.multiple_of((yl2 * 4 + z2) * 256, 256), 256)
             value = dot(xt[rows, :], gp[...].reshape(16 * CROP, 256)).astype(bf16)
             for half in range(2):
                 y2 = half * 2 + yl2
                 block = value[half * 128 : (half + 1) * 128]
-                zsend[z2, y2] = block[:, :128]
-                ysend[y2, z2] = block[:, 128:]
+                zsend[z2, y2, :128] = block[:, :128]
+                zsend[z2, y2, 128:] = block[:64, 128:]
+                ysend[y2, z2] = block[64:, 128:]
 
                 @pl.when(y2 != y)
                 def _():
@@ -422,15 +440,6 @@
         def _():
             push(zsend.at[z2], zrecv.at[z], ssem.at[RZ], rsem.at[RZ], at(y, z2))
 
-        def send_la(j, _):
-            q = (p + j) % 16
-
-            @pl.when(q != p)
-            def _():
-                push(labuf.at[p], labuf.at[p], ssem.at[LA], rsem.at[LA], plane_dev(q))
-            return 0
-
-        lax.fori_loop(4 * k - 3, 4 * k + 1, send_la, 0)
         return 0
 
     lax.fori_loop(1, 5, scatter, 0)
@@ -443,20 +452,13 @@
             total = total + ref[(q, *index)].astype(f32)
         return total.astype(bf16)
 
-    await_bytes(zrecv.at[pl.ds(0, 3)], rsem.at[RZ])
-    for i in range(4):
-        mid[0, i] = add_up(zrecv, i)
-    for j in range(1, 4):
-        y2 = (y + j) % 4
-        push(mid.at[0, y2], qrecv.at[y], ssem.at[BQ], rsem.at[BQ], at(y2, z))
-    qrecv[y] = mid[0, y]
     await_bytes(yrecv.at[pl.ds(0, 3)], rsem.at[RY])
     for i in range(4):
-        mid[1, i] = add_up(yrecv, i)
+        ymid[i] = add_up(yrecv, i)
     for j in range(1, 4):
-        z2 = (z + j) % 4
-        push(mid.at[1, z2], krecv.at[z], ssem.at[BK], rsem.at[BK], at(y, z2))
-    krecv[z] = mid[1, z]
+        z2 = rem(z + j, 4)
+        push(ymid.at[z2], krecv.at[z], ssem.at[BK], rsem.at[BK], at(y, z2))
+    krecv[z] = ymid[z]
 
     await_bytes(eabuf.at[pl.ds(0, 15)], rsem.at[EA])
     await_bytes(labuf.at[pl.ds(0, 15)], rsem.at[LA])
@@ -470,58 +472,72 @@
     o_cols = pl.ds(pl.multiple_of(t * SLICE, SLICE), SLICE)
 
     def each_target(fn):
-        def step(j, _):
-            @pl.when(jnp.logical_or(j != dp, c != yh))
-            def _():
-                fn(j)
-            return 0
-        lax.fori_loop(0, 8, step, 0)
+        for k in range(1, 8):
+            fn(rem(dp + k, 8))
+
+        @pl.when(c != yh)
+        def _():
+            fn(dp)
 
     def send_early(j):
         dev = (j, base + yh)
-        push(s_fin.at[2], s_out.at[2, :, s_cols], v_send.at[j], v_recv.at[t], dev)
-        push(o_fin, o_out.at[:, o_cols], o_send.at[j], o_recv.at[t], dev)
+        push(s_fin.at[2], s_out.at[2, :, s_cols], f_send.at[2], f_recv.at[2], dev)
+        push(o_fin, o_out.at[:, o_cols], f_send.at[3], f_recv.at[3], dev)
 
     each_target(send_early)
 
-    def send_part(i, sends, recvs):
+    await_bytes(zrecv.at[pl.ds(0, 3)], rsem.at[RZ])
+    for i in range(4):
+        zmid[i] = add_up(zrecv, i)
+    for j in range(1, 4):
+        y2 = rem(y + j, 4)
+        push(zmid.at[y2], qrecv.at[y], ssem.at[BQ], rsem.at[BQ], at(y2, z))
+    qrecv[y] = zmid[y]
+
+    def send_part(i, rows, sem):
         def send(j):
             push(
-                s_fin.at[i], s_out.at[i, :, s_cols], sends.at[j], recvs.at[t], (j, base + yh)
+                s_fin.at[i, rows], s_out.at[i, rows, s_cols], f_send.at[sem], f_recv.at[sem],
+                (j, base + yh),
             )
 
         each_target(send)
 
+    all_rows, first_half, last_half = pl.ds(0, 128), pl.ds(0, 64), pl.ds(64, 64)
+    await_bytes(krecv.at[pl.ds(0, 3)], rsem.at[BK])
+    s_fin[1, 64:] = add_up(krecv)
+    send_part(1, last_half, 4)
     await_bytes(qrecv.at[pl.ds(0, 3)], rsem.at[BQ])
-    s_fin[0] = add_up(qrecv)
-    send_part(0, q_send, q_recv)
-    await_bytes(krecv.at[pl.ds(0, 3)], rsem.at[BK])
-    s_fin[1] = add_up(krecv)
-    send_part(1, k_send, k_recv)
+    added = add_up(qrecv)
+    s_fin[0] = added[:128]
+    s_fin[1, :64] = added[128:]
+    send_part(0, all_rows, 0)
+    send_part(1, first_half, 1)
 
     @pl.when(c == yh)
     def _():
         s_out[:, :, s_cols] = s_fin[...]
         o_out[:, o_cols] = o_fin[...]
 
-    def collect(m, _):
-        @pl.when(jnp.logical_or(m != t, c != yh))
+    def await_all(sems):
+        def await_parts(members):
+            cols = pl.ds(0, members * 128)
+            await_bytes(s_out.at[0, :, cols], sems.at[0])
+            await_bytes(s_out.at[1, first_half, cols], sems.at[1])
+            await_bytes(s_out.at[2, :, cols], sems.at[2])
+            await_bytes(o_out.at[:, pl.ds(0, members * SLICE)], sems.at[3])
+            await_bytes(s_out.at[1, last_half, cols], sems.at[4])
+
+        @pl.when(c == yh)
         def _():
-            await_bytes(s_fin.at[2], v_recv.at[m])
-            await_bytes(o_fin, o_recv.at[m])
-            await_bytes(s_fin.at[0], q_recv.at[m])
-            await_bytes(s_fin.at[1], k_recv.at[m])
-        return 0
-
-    lax.fori_loop(0, 8, collect, 0)
-
-    def sent(j):
-        await_bytes(s_fin.at[2], v_send.at[j])
-        await_bytes(o_fin, o_send.at[j])
-        await_bytes(s_fin.at[0], q_send.at[j])
-        await_bytes(s_fin.at[1], k_send.at[j])
-
-    each_target(sent)
+            await_parts(7)
+
+        @pl.when(c != yh)
+        def _():
+            await_parts(8)
+
+    await_all(f_recv)
+    await_all(f_send)
     await_bytes(xbuf.at[pl.ds(0, 14)], xssem)
     for sem, ref in (
         (W, wbuf), (WO, wobuf), (EA, eabuf), (PO, pobuf), (TO, tobuf), (LA, labuf),
@@ -533,48 +549,52 @@
         await_bytes(ref.at[pl.ds(0, 7)], ssem.at[sem])
 
 
-def norm_kernel(starts, frames, xn, mc, wide):
-    def widen(r, _):
-        rows = pl.ds(pl.multiple_of(r * 32, 32), 32)
-        wide[rows, :] = frames[0, rows, :].astype(f32)
-        return 0
-
-    lax.fori_loop(0, 8, widen, 0)
-    wide[pl.ds(2 * CROP, 8), :] = jnp.zeros((8, D), f32)
-    begin = starts[pl.program_id(0)]
-    base, odd = (begin // 8) * 8, begin % 8
-
-    def chunk(r, total):
-        near = wide[pl.ds(pl.multiple_of(base + r * 16, 8), 24), :]
-        rows = pltpu.roll(near, 24 - odd, 0)[:16]
-        centred = rows - jnp.mean(rows, axis=-1, keepdims=True)
-        scale = lax.rsqrt(jnp.mean(centred * centred, axis=-1, keepdims=True) + norm_eps)
-        xn[0, pl.ds(pl.multiple_of(r * 16, 16), 16), :] = (centred * scale).astype(bf16)
-        return total + rows[:8] + rows[8:]
-
-    total = lax.fori_loop(0, CROP // 16, chunk, jnp.zeros((8, D), f32))
-    mean = jnp.sum(total, axis=0, keepdims=True) * (1.0 / CROP)
-    for m in range(8):
-        mc[0, m : m + 1, :] = mean[:, m * SLICE : (m + 1) * SLICE]
+def norm_kernel(starts, frames, xn, mc, raw, sems):
+    begin = [starts[i] for i in range(2)]
+    base = [(b // 16) * 16 for b in begin]
+    base = [jnp.minimum(b, CROP - 16) for b in base]
+    loads = [
+        pltpu.make_async_copy(
+            frames.at[i, pl.ds(pl.multiple_of(base[i], 16), CROP + 16)], raw.at[i], sems.at[i]
+        )
+        for i in range(2)
+    ]
+    for load in loads:
+        load.start()
+    for i in range(2):
+        loads[i].wait()
+        odd = begin[i] - base[i]
+
+        def chunk(r, total):
+            near = raw[i, pl.ds(pl.multiple_of(r * 16, 16), 32), :].astype(f32)
+            rows = pltpu.roll(near, (32 - odd) % 32, 0)[:16]
+            centred = rows - jnp.mean(rows, axis=-1, keepdims=True)
+            scale = lax.rsqrt(jnp.mean(centred * centred, axis=-1, keepdims=True) + norm_eps)
+            xn[i, pl.ds(pl.multiple_of(r * 16, 16), 16), :] = (centred * scale).astype(bf16)
+            return total + rows[:8] + rows[8:]
+
+        total = lax.fori_loop(0, CROP // 16, chunk, jnp.zeros((8, D), f32), unroll=4)
+        mean = jnp.sum(total, axis=0, keepdims=True) * (1.0 / CROP)
+        for m in range(8):
+            mc[i, m : m + 1, :] = mean[:, m * SLICE : (m + 1) * SLICE]
 
 
 def run_norm(frames, starts):
+    vmem = pl.BlockSpec(memory_space=pltpu.VMEM)
     return pl.pallas_call(
         norm_kernel,
-        grid=(2,),
         out_shape=(
             jax.ShapeDtypeStruct((2, CROP, D), bf16),
             jax.ShapeDtypeStruct((2, 8, SLICE), f32),
         ),
         in_specs=[
-            pl.BlockSpec(memory_space=pltpu.SMEM),
-            pl.BlockSpec((1, 2 * CROP, D), lambda i: (i, 0, 0)),
+            pl.BlockSpec(memory_space=pltpu.SMEM), pl.BlockSpec(memory_space=pltpu.HBM),
         ],
-        out_specs=(
-            pl.BlockSpec((1, CROP, D), lambda i: (i, 0, 0)),
-            pl.BlockSpec((1, 8, SLICE), lambda i: (i, 0, 0)),
-        ),
-        scratch_shapes=[pltpu.VMEM((2 * CROP + 8, D), f32)],
+        out_specs=(vmem, vmem),
+        scratch_shapes=[
+            pltpu.VMEM((2, CROP + 16, D), bf16),
+            pltpu.SemaphoreType.DMA((2,)),
+        ],
         compiler_params=pltpu.CompilerParams(vmem_limit_bytes=24 * 1024 * 1024),
         name="norm",
     )(starts, frames)
@@ -582,7 +602,7 @@
 
 def run_kernel(*args):
     vmem = pl.BlockSpec(memory_space=pltpu.VMEM)
-    hbm = pl.BlockSpec(memory_space=pl.ANY)
+    hbm = pl.BlockSpec(memory_space=pltpu.HBM)
     return pl.pallas_call(
         kernel,
         out_shape=(
@@ -617,13 +637,14 @@
             pltpu.VMEM((8, 16, 128), f32),
             pltpu.VMEM((8, 16, 128), f32),
             pltpu.VMEM((16, CROP, 256), bf16),
-            pltpu.VMEM((4, 4, 128, 128), bf16),
-            pltpu.VMEM((4, 4, 128, 128), bf16),
-            pltpu.VMEM((4, 4, 128, 128), bf16),
-            pltpu.VMEM((4, 4, 128, 128), bf16),
-            pltpu.VMEM((2, 4, 128, 128), bf16),
-            pltpu.VMEM((4, 128, 128), bf16),
-            pltpu.VMEM((4, 128, 128), bf16),
+            pltpu.VMEM((4, 4, 192, 128), bf16),
+            pltpu.VMEM((4, 4, 64, 128), bf16),
+            pltpu.VMEM((4, 4, 192, 128), bf16),
+            pltpu.VMEM((4, 4, 64, 128), bf16),
+            pltpu.VMEM((4, 192, 128), bf16),
+            pltpu.VMEM((4, 64, 128), bf16),
+            pltpu.VMEM((4, 192, 128), bf16),
+            pltpu.VMEM((4, 64, 128), bf16),
             pltpu.VMEM((3, 128, 128), bf16),
             pltpu.VMEM((128, SLICE), f32),
             pltpu.VMEM((64, SLICE), bf16),
@@ -635,7 +656,7 @@
             pltpu.SemaphoreType.DMA,
             pltpu.SemaphoreType.DMA((16,)),
         ]
-        + [pltpu.SemaphoreType.DMA((8,))] * 8,
+        + [pltpu.SemaphoreType.DMA((5,))] * 2,
         compiler_params=pltpu.CompilerParams(
             collective_id=0, has_side_effects=True, vmem_limit_bytes=40 * 1024 * 1024
         ),
@@ -647,70 +668,116 @@
 
 
 def adam_kernel(
-    share, o_grad, gain, gain_m, gain_s, in_w, in_m, in_s, out_w, out_m, out_s,
-    new_in_w, new_in_m, new_in_s, new_out_w, new_out_m, new_out_s, new_gw, new_gm, new_gs,
-    column,
+    share, o_grad, losses, gain, gain_m, gain_s, in_w, in_m, in_s, out_w, out_m, out_s,
+    pair_losses, new_in_w, new_in_m, new_in_s, new_out_w, new_out_m, new_out_s, new_gw, new_gm, new_gs,
+    column, state, square_in, in_new, out_new, lsems, ssems, isems, osems,
 ):
-    step = pl.program_id(0)
+    loads = [
+        pltpu.make_async_copy(ref, state.at[i], lsems.at[i])
+        for i, ref in enumerate((out_w, out_m, out_s))
+    ]
+    chunks = [
+        pltpu.make_async_copy(
+            in_s.at[pl.ds(i * 32, 32)], square_in.at[pl.ds(i * 32, 32)], ssems.at[i]
+        )
+        for i in range(STEPS)
+    ]
+    for load in chunks + loads:
+        load.start()
+    t = 2 * (lax.axis_index("dp") // 2) + lax.axis_index("shard") % 2
+    item = lax.broadcasted_iota(jnp.int32, (16, 128), 0)
+    lane = lax.broadcasted_iota(jnp.int32, (16, 128), 1)
+    for i in range(2):
+        mine = jnp.logical_and(item == 2 * t + i, lane == 0)
+        pair_losses[i] = jnp.sum(jnp.where(mine, losses[...], 0.0))
+    square = lax.broadcasted_iota(jnp.int32, (128, 128), 0) == lax.broadcasted_iota(
+        jnp.int32, (128, 128), 1
+    )
+    gain_row = gain[...].astype(bf16).astype(f32)
+    column[...] = jnp.broadcast_to(
+        jnp.sum(jnp.where(square, gain_row, 0.0), axis=1, keepdims=True), (128, 128)
+    )
     rows = 128 // STEPS
-    gain_row = gain[...].astype(bf16).astype(f32)
-    lane = lax.broadcasted_iota(jnp.int32, (rows, 128), 1)
-    sub = lax.broadcasted_iota(jnp.int32, (rows, 128), 0)
-    gain_col = jnp.sum(jnp.where(lane == sub + step * rows, gain_row, 0.0), axis=1, keepdims=True)
-
-    def part(j, total):
-        i, cols = j // 4, pl.ds(pl.multiple_of(j * 256, 256), 256)
-        inner = pl.ds(pl.multiple_of((j % 4) * 256, 256), 256)
-        master = in_w[:, cols]
-        piece = share[i, :, inner].astype(f32)
-        new = adam_update(master, in_m[:, cols], in_s[:, cols], piece * gain_col, weight_decay)
-        new_in_w[:, cols], new_in_m[:, cols], new_in_s[:, cols] = new
-        terms = piece * master.astype(bf16).astype(f32)
-        return total + terms[:, :128] + terms[:, 128:]
-
-    total = lax.fori_loop(0, 12, part, jnp.zeros((rows, 128), f32))
-
-    def out_part(j, _):
-        cols = pl.ds(pl.multiple_of(j * 512, 512), 512)
-        new = adam_update(
-            out_w[:, cols], out_m[:, cols], out_s[:, cols], o_grad[:, cols].astype(f32), weight_decay
-        )
-        new_out_w[:, cols], new_out_m[:, cols], new_out_s[:, cols] = new
-        return 0
-
-    lax.fori_loop(0, 4, out_part, 0)
-    column[pl.ds(pl.multiple_of(step * rows, rows), rows), :] = jnp.broadcast_to(
-        jnp.sum(total, axis=1, keepdims=True), (rows, 128)
+    stores = []
+    for step in range(STEPS):
+        at_rows = pl.ds(step * rows, rows)
+        chunks[step].wait()
+        gain_col = column[at_rows, :][:, :1]
+
+        def part(j, total):
+            i, cols = j // 2, pl.ds(pl.multiple_of(j * 512, 512), 512)
+            inner = pl.ds(pl.multiple_of((j % 2) * 512, 512), 512)
+            master = in_w[at_rows, cols]
+            piece = share[i, at_rows, inner].astype(f32)
+            new = adam_update(
+                master, in_m[at_rows, cols], square_in[at_rows, cols], piece * gain_col, weight_decay
+            )
+            for n in range(3):
+                in_new[n, at_rows, cols] = new[n]
+            terms = piece * master.astype(bf16).astype(f32)
+            return total + sum(terms[:, n * 128 : (n + 1) * 128] for n in range(4))
+
+        total = lax.fori_loop(0, 6, part, jnp.zeros((rows, 128), f32), unroll=2)
+        column[at_rows, :] = jnp.broadcast_to(jnp.sum(total, axis=1, keepdims=True), (rows, 128))
+        for n, ref in enumerate((new_in_w, new_in_m, new_in_s)):
+            stores.append(
+                pltpu.make_async_copy(in_new.at[n, at_rows], ref.at[at_rows], isems.at[n, step])
+            )
+            stores[-1].start()
+    for load in loads:
+        load.wait()
+    for step in range(2):
+        at_rows = pl.ds(step * 32, 32)
+
+        def out_part(j, _):
+            cols = pl.ds(pl.multiple_of(j * 512, 512), 512)
+            new = adam_update(
+                state[0, at_rows, cols], state[1, at_rows, cols], state[2, at_rows, cols],
+                o_grad[at_rows, cols].astype(f32), weight_decay,
+            )
+            for n in range(3):
+                out_new[n, at_rows, cols] = new[n]
+            return 0
+
+        lax.fori_loop(0, 4, out_part, 0, unroll=2)
+        for n, ref in enumerate((new_out_w, new_out_m, new_out_s)):
+            stores.append(
+                pltpu.make_async_copy(out_new.at[n, at_rows], ref.at[at_rows], osems.at[n, step])
+            )
+            stores[-1].start()
+    grad = jnp.sum(jnp.where(square, column[...], 0.0), axis=0, keepdims=True)
+    new_gw[...], new_gm[...], new_gs[...] = adam_update(
+        gain[...], gain_m[...], gain_s[...], grad, 0.0
     )
-
-    @pl.when(step == STEPS - 1)
-    def _():
-        square = lax.broadcasted_iota(jnp.int32, (128, 128), 0) == lax.broadcasted_iota(
-            jnp.int32, (128, 128), 1
-        )
-        grad = jnp.sum(jnp.where(square, column[...], 0.0), axis=0, keepdims=True)
-        new_gw[...], new_gm[...], new_gs[...] = adam_update(
-            gain[...], gain_m[...], gain_s[...], grad, 0.0
-        )
-
-
-def run_adam(share, o_grad, gains, inputs, outputs):
-    one = pl.BlockSpec((1, 128), lambda i: (0, 0))
-    big = pl.BlockSpec((128 // STEPS, 3 * INNER), lambda i: (i, 0))
-    mid = pl.BlockSpec((64 // STEPS, D), lambda i: (i, 0))
-    shares = pl.BlockSpec((3, 128 // STEPS, INNER), lambda i: (0, i, 0))
+    for store in stores:
+        store.wait()
+
+
+def run_adam(share, o_grad, losses, gains, inputs, outputs):
+    vmem = pl.BlockSpec(memory_space=pltpu.VMEM)
+    hbm = pl.BlockSpec(memory_space=pltpu.HBM)
     return pl.pallas_call(
         adam_kernel,
-        grid=(STEPS,),
-        out_shape=[jax.ShapeDtypeStruct((128, 3 * INNER), f32)] * 3
+        out_shape=[jax.ShapeDtypeStruct((2,), f32)]
+        + [jax.ShapeDtypeStruct((128, 3 * INNER), f32)] * 3
         + [jax.ShapeDtypeStruct((64, D), f32)] * 3
         + [jax.ShapeDtypeStruct((1, 128), f32)] * 3,
-        in_specs=[shares, mid] + [one] * 3 + [big] * 3 + [mid] * 3,
-        out_specs=[big] * 3 + [mid] * 3 + [one] * 3,
-        scratch_shapes=[pltpu.VMEM((128, 128), f32)],
-        compiler_params=pltpu.CompilerParams(vmem_limit_bytes=24 * 1024 * 1024),
+        in_specs=[vmem] * 8 + [hbm] * 4,
+        out_specs=[pl.BlockSpec(memory_space=pltpu.SMEM)] + [hbm] * 6 + [vmem] * 3,
+        scratch_shapes=[
+            pltpu.VMEM((128, 128), f32),
+            pltpu.VMEM((3, 64, D), f32),
+            pltpu.VMEM((128, 3 * INNER), f32),
+            pltpu.VMEM((3, 128, 3 * INNER), f32),
+            pltpu.VMEM((3, 64, D), f32),
+            pltpu.SemaphoreType.DMA((3,)),
+            pltpu.SemaphoreType.DMA((STEPS,)),
+            pltpu.SemaphoreType.DMA((3, STEPS)),
+            pltpu.SemaphoreType.DMA((3, 2)),
+        ],
+        compiler_params=pltpu.CompilerParams(vmem_limit_bytes=48 * 1024 * 1024),
         name="adam",
-    )(share, o_grad, *gains, *inputs, *outputs)
+    )(share, o_grad, losses, *gains, *inputs, *outputs)
 
 
 def per_device(
@@ -719,19 +786,17 @@
     output_master, output_moment, output_square,
     gain_master, gain_moment, gain_square,
 ):
-    t = 2 * (lax.axis_index("dp") // 2) + lax.axis_index("shard") % 2
     gains = [g.reshape(1, 128) for g in (gain_master, gain_moment, gain_square)]
     losses, s_grad, o_grad = run_kernel(
         *run_norm(frames, crop_starts), pairing.reshape(1, 256), bias_table,
         input_master, output_master, gains[0],
     )
-    pair_losses = lax.dynamic_slice(losses, (2 * t, 0), (2, 1)).reshape(2)
     new = run_adam(
-        s_grad, o_grad, gains,
+        s_grad, o_grad, losses, gains,
         (input_master, input_moment, input_square),
         (output_master, output_moment, output_square),
     )
-    return (pair_losses, *new[:6], *(g.reshape(128) for g in new[6:]))
+    return (*new[:7], *(g.reshape(128) for g in new[7:]))
 
 
 def solution(mesh):

time: 118 us -> 114 us (0.966)
  local copies, waits for them, and re-layouts: 5.11 us -> 2.44 us
  Pallas kernels: 112 us -> 110 us
    unnamed x26 -> x24, local copies, waits for them, and re-layouts: 4.47 us -> 2.44 us
    pallas_call x2, Pallas kernels: 9.79 us -> 7.98 us  [the longest x1 5.61 us: run_adam(): pl.pallas_call(adam_kernel, out_shape=[jax.ShapeDtypeStruct((2,), f32)] +...]
where the time goes in v4:
time: 114 us; the launch traced here: 113 us
  Pallas kernels  110 us (96%)
  local copies, waits for them, and re-layouts  2.44 us (2%)
    pallas_call x1, Pallas kernels, run_kernel(): pl.pallas_call(kernel, out_shape=(jax.ShapeDtypeStruct((16, 128), f32), j...  102 us
    pallas_call x1, Pallas kernels, run_adam(): pl.pallas_call(adam_kernel, out_shape=[jax.ShapeDtypeStruct((2,), f32)] +...  5.61 us
    unnamed x24, local copies, waits for them, and re-layouts  2.44 us
    pallas_call x1, Pallas kernels, run_norm(): pl.pallas_call(norm_kernel, out_shape=(jax.ShapeDtypeStruct((2, CROP, D),...  2.37 us

profile of v4, /device:TPU:1, one launch (start us, length us, event | category | flops | bytes accessed | tf_op | source)
XLA Modules:
  0.0 113.4 jit_solution(5988762600694885293)
XLA Ops:
  0.6 0.0 copy-start.1
  0.7 0.0 copy-start
  0.7 0.0 copy-start.2
  0.7 1.7 %copy-done.2 = bf16[2,256,2048]{2,1,0:T(8,128)(2,1)S(1)} copy-done((bf16[2,256,2048]{2,1,0:T(8,128)(2,1)S(1)}, bf16[2,256,2048]{2,1,0:T(8,128)(2,1)}, u32[]{:S(2)}) %copy-start.2) | copy-done | bytes 2097176
  2.4 0.0 copy-start.9
  2.4 0.7 copy-done.9
  3.1 2.4 %norm.1 = (bf16[2,128,2048]{2,1,0:T(8,128)(2,1)S(1)}, f32[2,8,256]{2,1,0:T(8,128)S(1)}) custom-call(s32[2]{0:T(128)S(1)} %copy-done.9, bf16[2,256,2048]{2,1,0:T(8,128)(2,1)S(1)} %copy-done.2), custom_call_target="tpu_custom_call" | custom-call | tf_op jit(solution)/shard_map/norm/pallas_call | solution.py:584
  5.4 0.0 copy-done.1
  5.5 0.0 copy-done
  5.5 0.0 copy-done.6
  5.5 0.0 copy-done.7
  5.5 0.0 copy-done.8
  5.5 0.0 copy-start.3
  5.5 0.0 copy-start.4
  5.5 0.0 copy-start.5
  5.5 0.0 copy-start.10
  5.5 0.0 copy-start.11
  5.6 102.1 %encoder.1 = (f32[16,128]{1,0:T(8,128)S(1)}, bf16[3,128,1024]{2,1,0:T(8,128)(2,1)S(1)}, bf16[64,2048]{1,0:T(8,128)(2,1)S(1)}) custom-call(bf16[2,128,2048]{2,1,0:T(8,128)(2,1)S(1)} %get-tuple-element.25.xn, f32[2,8,256]{2,1,0:T(8,128)S(1)} %get-tuple-element.26.mc, s32[1,256]{1,0:T(1,128)S(1)} %bitcast.9, f32[8,255]{1,0:T(8,128)S(1)} %copy-done.6, ...), custom_call_target="tpu_custom_call" | custom-call | tf_op jit(solution)/shard_map/encoder/pallas_call | solution.py:606
  107.7 0.0 copy-done.3
  107.7 0.0 copy-done.4
  107.7 0.0 copy-done.5
  107.7 0.0 copy-done.10
  107.8 0.0 copy-done.11
  107.8 5.6 %adam.1 = (f32[2]{0:T(128)}, f32[128,3072]{1,0:T(8,128)}, f32[128,3072]{1,0:T(8,128)}, f32[128,3072]{1,0:T(8,128)}, f32[64,2048]{1,0:T(8,128)}, /*index=5*/f32[6...) custom-call(bf16[3,128,1024]{2,1,0:T(8,128)(2,1)S(1)} %get-tuple-element.27.share, ...), custom_call_target="tpu_custom_call" | custom-call | tf_op jit(solution)/shard_map/adam/pallas_call | solution.py:759
  (3 shorter events, 0.0 us)
Async XLA Ops:
  0.6 4.8 %copy-start.1 = (f32[64,2048]{1,0:T(8,128)S(1)}, f32[64,2048]{1,0:T(8,128)}, u32[]{:S(2)}) copy-start(f32[64,2048]{1,0:T(8,128)} %out_w.1) | copy-start | bytes 1572868
  0.7 4.8 %copy-start = (f32[128,3072]{1,0:T(8,128)S(1)}, f32[128,3072]{1,0:T(8,128)}, u32[]{:S(2)}) copy-start(f32[128,3072]{1,0:T(8,128)} %in_w.1) | copy-start | bytes 4718596
  0.7 1.7 %copy-start.2 = (bf16[2,256,2048]{2,1,0:T(8,128)(2,1)S(1)}, bf16[2,256,2048]{2,1,0:T(8,128)(2,1)}, u32[]{:S(2)}) copy-start(bf16[2,256,2048]{2,1,0:T(8,128)(2,1)} %frames.1) | copy-start | bytes 6291460
  2.4 0.7 copy-start.9
  3.1 2.4 %copy-start.6 = (f32[8,255]{1,0:T(8,128)S(1)}, f32[8,255]{1,0:T(8,128)}, u32[]{:S(2)}) copy-start(f32[8,255]{1,0:T(8,128)} %bias.1) | copy-start | bytes 24484
  3.1 2.4 %copy-start.7 = (f32[128]{0:T(128)S(1)}, f32[128]{0:T(128)}, u32[]{:S(2)}) copy-start(f32[128]{0:T(128)} %param.23) | copy-start | bytes 1540
  3.1 2.4 %copy-start.8 = (s32[256]{0:T(256)S(1)}, s32[256]{0:T(256)}, u32[]{:S(2)}) copy-start(s32[256]{0:T(256)} %param.15) | copy-start | bytes 3076
  5.5 102.2 %copy-start.3 = (f32[128,3072]{1,0:T(8,128)S(1)}, f32[128,3072]{1,0:T(8,128)}, u32[]{:S(2)}) copy-start(f32[128,3072]{1,0:T(8,128)} %in_m.1) | copy-start | bytes 4718596
  5.5 102.2 %copy-start.4 = (f32[64,2048]{1,0:T(8,128)S(1)}, f32[64,2048]{1,0:T(8,128)}, u32[]{:S(2)}) copy-start(f32[64,2048]{1,0:T(8,128)} %out_m.1) | copy-start | bytes 1572868
  5.5 102.2 %copy-start.5 = (f32[64,2048]{1,0:T(8,128)S(1)}, f32[64,2048]{1,0:T(8,128)}, u32[]{:S(2)}) copy-start(f32[64,2048]{1,0:T(8,128)} %out_s.1) | copy-start | bytes 1572868
  5.5 102.2 %copy-start.10 = (f32[128]{0:T(128)S(1)}, f32[128]{0:T(128)}, u32[]{:S(2)}) copy-start(f32[128]{0:T(128)} %param.24) | copy-start | bytes 1540
  5.5 102.2 %copy-start.11 = (f32[128]{0:T(128)S(1)}, f32[128]{0:T(128)}, u32[]{:S(2)}) copy-start(f32[128]{0:T(128)} %param.25) | copy-start | bytes 1540

commit v5 on v4

--- a/solution.py
+++ b/solution.py
@@ -57,7 +57,7 @@
     return (master * (1.0 - learn_rate * decay) - step, moment_new, square_new)
 
 
-W, WO, MC, MM, EA, PO, GR, TO, LA, GM, RZ, RY, BQ, BK = range(14)
+W, WO, MC, MM, EA, PO, GR, TO, LA, GM, RZ, RY, BQ, BK, SS = range(15)
 
 
 def div(a, b):
@@ -79,7 +79,7 @@
     xn, mc, pairing, bias, input_master, output_master, gain,
     loss_out, s_out, o_out,
     wraw, woraw, wp, wo2, mcsend, target,
-    xbuf, xt, wbuf, wobuf, mcbuf, qkvbuf, probs, arows, mmbuf, eabuf, easend, pobuf, grbuf,
+    xbuf, xt, wbuf, wobuf, mcbuf, qkvbuf, probs, arows, mmbuf, eabuf, easend, pobuf, grbuf, ssbuf,
     tobuf, labuf, gmsend, gmbuf, gp, zsend, ysend, zrecv, yrecv, zmid, ymid, qrecv, krecv, s_fin, o_tmp, o_fin, band, table,
     lsem, ssem, rsem, xssem, xrsem, f_send, f_recv,
 ):
@@ -340,22 +340,25 @@
     await_bytes(pobuf.at[pl.ds(0, 15)], rsem.at[PO])
     everyone = pobuf[...].reshape(256, SLICE)
     parts = split(everyone)
-    grbuf[t, pl.ds(0, 16), :] = dot3(pooled, parts, NT)
+    grbuf[t] = dot3(pooled, parts, NT)
     squares = jnp.concatenate(split(everyone * everyone), axis=1)
-    grbuf[t, pl.ds(16, 8), :] = dot(jnp.ones((8, 2 * SLICE), bf16), squares, NT)
+    ssbuf[t] = dot(jnp.ones((8, 2 * SLICE), bf16), squares, NT)[:1]
 
     def send_gr(k, _):
-        push(grbuf.at[t], grbuf.at[t], ssem.at[GR], rsem.at[GR], tp_dev(rem(t + k, 8)))
+        dev = tp_dev(rem(t + k, 8))
+        push(grbuf.at[t], grbuf.at[t], ssem.at[GR], rsem.at[GR], dev)
+        push(ssbuf.at[t], ssbuf.at[t], ssem.at[SS], rsem.at[SS], dev)
         return 0
 
     lax.fori_loop(1, 8, send_gr, 0, unroll=True)
     await_bytes(grbuf.at[pl.ds(0, 7)], rsem.at[GR])
+    await_bytes(ssbuf.at[pl.ds(0, 7)], rsem.at[SS])
     gram = grbuf[0]
     for m in range(1, 8):
         gram = gram + grbuf[m]
-    inv_row = lax.rsqrt(gram[16:17] + embed_eps)
+    inv_row = lax.rsqrt(jnp.sum(ssbuf[...], axis=0) + embed_eps)
     inv_col = jnp.sum(own * inv_row, axis=1, keepdims=True)
-    sims = gram[:16] * inv_col * inv_row * inv_tau
+    sims = gram * inv_col * inv_row * inv_tau
     exponents = jnp.where(own > 0.5, 0.0, jnp.exp(sims - inv_tau))
     totals = jnp.sum(exponents, axis=1, keepdims=True)
     tobuf[p] = jnp.sum(own * totals, axis=0, keepdims=True)
@@ -429,8 +432,8 @@
                 y2 = half * 2 + yl2
                 block = value[half * 128 : (half + 1) * 128]
                 zsend[z2, y2, :128] = block[:, :128]
-                zsend[z2, y2, 128:] = block[:64, 128:]
-                ysend[y2, z2] = block[64:, 128:]
+                zsend[z2, y2, 128:] = block[:16, 128:]
+                ysend[y2, z2] = block[16:, 128:]
 
                 @pl.when(y2 != y)
                 def _():
@@ -503,14 +506,14 @@
 
         each_target(send)
 
-    all_rows, first_half, last_half = pl.ds(0, 128), pl.ds(0, 64), pl.ds(64, 64)
+    all_rows, first_half, last_half = pl.ds(0, 128), pl.ds(0, 16), pl.ds(16, 112)
     await_bytes(krecv.at[pl.ds(0, 3)], rsem.at[BK])
-    s_fin[1, 64:] = add_up(krecv)
+    s_fin[1, 16:] = add_up(krecv)
     send_part(1, last_half, 4)
     await_bytes(qrecv.at[pl.ds(0, 3)], rsem.at[BQ])
     added = add_up(qrecv)
     s_fin[0] = added[:128]
-    s_fin[1, :64] = added[128:]
+    s_fin[1, :16] = added[128:]
     send_part(0, all_rows, 0)
     send_part(1, first_half, 1)
 
@@ -545,7 +548,7 @@
         await_bytes(ref.at[pl.ds(0, 15)], ssem.at[sem])
     for sem, ref in ((RZ, zrecv), (RY, yrecv), (BQ, qrecv), (BK, krecv)):
         await_bytes(ref.at[pl.ds(0, 3)], ssem.at[sem])
-    for sem, ref in ((MC, mcbuf), (MM, mmbuf), (GR, grbuf), (GM, gmbuf)):
+    for sem, ref in ((MC, mcbuf), (MM, mmbuf), (GR, grbuf), (SS, ssbuf), (GM, gmbuf)):
         await_bytes(ref.at[pl.ds(0, 7)], ssem.at[sem])
 
 
@@ -631,28 +634,29 @@
             pltpu.VMEM((16, 16, 256), bf16),
             pltpu.VMEM((16, 16, 256), bf16),
             pltpu.VMEM((16, 16, SLICE), f32),
-            pltpu.VMEM((8, 24, 256), f32),
+            pltpu.VMEM((8, 16, 256), f32),
+            pltpu.VMEM((8, 1, 256), f32),
             pltpu.VMEM((16, 1, 256), f32),
             pltpu.VMEM((16, 16, SLICE + 128), bf16),
             pltpu.VMEM((8, 16, 128), f32),
             pltpu.VMEM((8, 16, 128), f32),
             pltpu.VMEM((16, CROP, 256), bf16),
-            pltpu.VMEM((4, 4, 192, 128), bf16),
-            pltpu.VMEM((4, 4, 64, 128), bf16),
-            pltpu.VMEM((4, 4, 192, 128), bf16),
-            pltpu.VMEM((4, 4, 64, 128), bf16),
-            pltpu.VMEM((4, 192, 128), bf16),
-            pltpu.VMEM((4, 64, 128), bf16),
-            pltpu.VMEM((4, 192, 128), bf16),
-            pltpu.VMEM((4, 64, 128), bf16),
+            pltpu.VMEM((4, 4, 144, 128), bf16),
+            pltpu.VMEM((4, 4, 112, 128), bf16),
+            pltpu.VMEM((4, 4, 144, 128), bf16),
+            pltpu.VMEM((4, 4, 112, 128), bf16),
+            pltpu.VMEM((4, 144, 128), bf16),
+            pltpu.VMEM((4, 112, 128), bf16),
+            pltpu.VMEM((4, 144, 128), bf16),
+            pltpu.VMEM((4, 112, 128), bf16),
             pltpu.VMEM((3, 128, 128), bf16),
             pltpu.VMEM((128, SLICE), f32),
             pltpu.VMEM((64, SLICE), bf16),
             pltpu.VMEM((CROP, CROP), f32),
             pltpu.VMEM((HEADS, 2 * CROP), f32),
             pltpu.SemaphoreType.DMA((4,)),
-            pltpu.SemaphoreType.DMA((14,)),
-            pltpu.SemaphoreType.DMA((14,)),
+            pltpu.SemaphoreType.DMA((15,)),
+            pltpu.SemaphoreType.DMA((15,)),
             pltpu.SemaphoreType.DMA,
             pltpu.SemaphoreType.DMA((16,)),
         ]
@@ -660,6 +664,9 @@
         compiler_params=pltpu.CompilerParams(
             collective_id=0, has_side_effects=True, vmem_limit_bytes=40 * 1024 * 1024
         ),
+        cost_estimate=pl.CostEstimate(
+            flops=15_000_000_000, bytes_accessed=300_000_000, transcendentals=300_000
+        ),
         name="encoder",
     )(*args)
 
@@ -670,20 +677,8 @@
 def adam_kernel(
     share, o_grad, losses, gain, gain_m, gain_s, in_w, in_m, in_s, out_w, out_m, out_s,
     pair_losses, new_in_w, new_in_m, new_in_s, new_out_w, new_out_m, new_out_s, new_gw, new_gm, new_gs,
-    column, state, square_in, in_new, out_new, lsems, ssems, isems, osems,
+    column, in_new, out_new, isems, osems,
 ):
-    loads = [
-        pltpu.make_async_copy(ref, state.at[i], lsems.at[i])
-        for i, ref in enumerate((out_w, out_m, out_s))
-    ]
-    chunks = [
-        pltpu.make_async_copy(
-            in_s.at[pl.ds(i * 32, 32)], square_in.at[pl.ds(i * 32, 32)], ssems.at[i]
-        )
-        for i in range(STEPS)
-    ]
-    for load in chunks + loads:
-        load.start()
     t = 2 * (lax.axis_index("dp") // 2) + lax.axis_index("shard") % 2
     item = lax.broadcasted_iota(jnp.int32, (16, 128), 0)
     lane = lax.broadcasted_iota(jnp.int32, (16, 128), 1)
@@ -701,7 +696,6 @@
     stores = []
     for step in range(STEPS):
         at_rows = pl.ds(step * rows, rows)
-        chunks[step].wait()
         gain_col = column[at_rows, :][:, :1]
 
         def part(j, total):
@@ -710,7 +704,7 @@
             master = in_w[at_rows, cols]
             piece = share[i, at_rows, inner].astype(f32)
             new = adam_update(
-                master, in_m[at_rows, cols], square_in[at_rows, cols], piece * gain_col, weight_decay
+                master, in_m[at_rows, cols], in_s[at_rows, cols], piece * gain_col, weight_decay
             )
             for n in range(3):
                 in_new[n, at_rows, cols] = new[n]
@@ -724,15 +718,13 @@
                 pltpu.make_async_copy(in_new.at[n, at_rows], ref.at[at_rows], isems.at[n, step])
             )
             stores[-1].start()
-    for load in loads:
-        load.wait()
     for step in range(2):
         at_rows = pl.ds(step * 32, 32)
 
         def out_part(j, _):
             cols = pl.ds(pl.multiple_of(j * 512, 512), 512)
             new = adam_update(
-                state[0, at_rows, cols], state[1, at_rows, cols], state[2, at_rows, cols],
+                out_w[at_rows, cols], out_m[at_rows, cols], out_s[at_rows, cols],
                 o_grad[at_rows, cols].astype(f32), weight_decay,
             )
             for n in range(3):
@@ -762,20 +754,16 @@
         + [jax.ShapeDtypeStruct((128, 3 * INNER), f32)] * 3
         + [jax.ShapeDtypeStruct((64, D), f32)] * 3
         + [jax.ShapeDtypeStruct((1, 128), f32)] * 3,
-        in_specs=[vmem] * 8 + [hbm] * 4,
+        in_specs=[vmem] * 12,
         out_specs=[pl.BlockSpec(memory_space=pltpu.SMEM)] + [hbm] * 6 + [vmem] * 3,
         scratch_shapes=[
             pltpu.VMEM((128, 128), f32),
-            pltpu.VMEM((3, 64, D), f32),
-            pltpu.VMEM((128, 3 * INNER), f32),
             pltpu.VMEM((3, 128, 3 * INNER), f32),
             pltpu.VMEM((3, 64, D), f32),
-            pltpu.SemaphoreType.DMA((3,)),
-            pltpu.SemaphoreType.DMA((STEPS,)),
             pltpu.SemaphoreType.DMA((3, STEPS)),
             pltpu.SemaphoreType.DMA((3, 2)),
         ],
-        compiler_params=pltpu.CompilerParams(vmem_limit_bytes=48 * 1024 * 1024),
+        compiler_params=pltpu.CompilerParams(vmem_limit_bytes=24 * 1024 * 1024),
         name="adam",
     )(share, o_grad, losses, *gains, *inputs, *outputs)
 

time: 114 us -> 114 us (level)
    unnamed x24 -> x26, local copies, waits for them, and re-layouts: 2.44 us -> 2.99 us
where the time goes in v5:
time: 114 us; the launch traced here: 113 us
  Pallas kernels  110 us (96%)
  local copies, waits for them, and re-layouts  2.99 us (3%)
    pallas_call x1, Pallas kernels, run_kernel(): pl.pallas_call(kernel, out_shape=(jax.ShapeDtypeStruct((16, 128), f32), j...  102 us
    pallas_call x1, Pallas kernels, run_adam(): pl.pallas_call(adam_kernel, out_shape=[jax.ShapeDtypeStruct((2,), f32)] +...  4.75 us
    unnamed x26, local copies, waits for them, and re-layouts  2.99 us
    pallas_call x1, Pallas kernels, run_norm(): pl.pallas_call(norm_kernel, out_shape=(jax.ShapeDtypeStruct((2, CROP, D),...  2.37 us

profile of v5, /device:TPU:1, one launch (start us, length us, event | category | flops | bytes accessed | tf_op | source)
XLA Modules:
  0.0 113.3 jit_solution(5841561228889426367)
XLA Ops:
  0.6 0.0 copy-start.8
  0.7 0.0 copy-start.12
  0.7 0.0 copy-start
  0.7 1.6 %copy-done = bf16[2,256,2048]{2,1,0:T(8,128)(2,1)S(1)} copy-done((bf16[2,256,2048]{2,1,0:T(8,128)(2,1)S(1)}, bf16[2,256,2048]{2,1,0:T(8,128)(2,1)}, u32[]{:S(2)}) %copy-start) | copy-done | bytes 2097176
  2.3 0.0 copy-start.7
  2.3 0.7 copy-done.7
  2.9 0.0 copy-start.1
  2.9 2.4 %norm.1 = (bf16[2,128,2048]{2,1,0:T(8,128)(2,1)S(1)}, f32[2,8,256]{2,1,0:T(8,128)S(1)}) custom-call(s32[2]{0:T(128)S(1)} %copy-done.7, bf16[2,256,2048]{2,1,0:T(8,128)(2,1)S(1)} %copy-done), custom_call_target="tpu_custom_call" | custom-call | tf_op jit(solution)/shard_map/norm/pallas_call | solution.py:587
  5.3 0.0 copy-done.8
  5.3 0.0 copy-done.12
  5.3 0.0 copy-done.1
  5.3 0.0 copy-done.4
  5.3 0.0 copy-start.11
  5.4 0.7 copy-done.11
  6.1 0.0 copy-start.9
  6.1 0.0 copy-start.10
  6.1 102.4 %encoder.1 = (f32[16,128]{1,0:T(8,128)S(1)}, bf16[3,128,1024]{2,1,0:T(8,128)(2,1)S(1)}, bf16[64,2048]{1,0:T(8,128)(2,1)S(1)}) custom-call(bf16[2,128,2048]{2,1,0:T(8,128)(2,1)S(1)} %get-tuple-element.25.xn, f32[2,8,256]{2,1,0:T(8,128)S(1)} %get-tuple-element.26.mc, s32[1,256]{1,0:T(1,128)S(1)} %bitcast.11, f32[8,255]{1,0:T(8,128)S(1)} %copy-done.11, ...), custom_call_target="tpu_custom_call" | custom-call | flops 15000000512 | bytes 300000000 | tf_op jit(solution)/shard_map/encoder/pallas_call | solution.py:609
  108.5 0.0 copy-done.2
  108.5 0.0 copy-done.3
  108.5 0.0 copy-done.5
  108.5 0.0 copy-done.6
  108.6 0.0 copy-done.9
  108.6 0.0 copy-done.10
  108.6 4.8 %adam.1 = (f32[2]{0:T(128)}, f32[128,3072]{1,0:T(8,128)}, f32[128,3072]{1,0:T(8,128)}, f32[128,3072]{1,0:T(8,128)}, f32[64,2048]{1,0:T(8,128)}, /*index=5*/f32[6...) custom-call(bf16[3,128,1024]{2,1,0:T(8,128)(2,1)S(1)} %get-tuple-element.27.share, ...), custom_call_target="tpu_custom_call" | custom-call | tf_op jit(solution)/shard_map/adam/pallas_call | solution.py:751
  (5 shorter events, 0.0 us)
Async XLA Ops:
  0.6 4.7 %copy-start.8 = (f32[128]{0:T(128)S(1)}, f32[128]{0:T(128)}, u32[]{:S(2)}) copy-start(f32[128]{0:T(128)} %param.23) | copy-start | bytes 1540
  0.7 4.7 %copy-start.12 = (s32[256]{0:T(256)S(1)}, s32[256]{0:T(256)}, u32[]{:S(2)}) copy-start(s32[256]{0:T(256)} %param.15) | copy-start | bytes 3076
  0.7 1.6 %copy-start = (bf16[2,256,2048]{2,1,0:T(8,128)(2,1)S(1)}, bf16[2,256,2048]{2,1,0:T(8,128)(2,1)}, u32[]{:S(2)}) copy-start(bf16[2,256,2048]{2,1,0:T(8,128)(2,1)} %frames.1) | copy-start | bytes 6291460
  2.3 0.7 copy-start.7
  2.9 2.4 %copy-start.1 = (f32[128,3072]{1,0:T(8,128)S(1)}, f32[128,3072]{1,0:T(8,128)}, u32[]{:S(2)}) copy-start(f32[128,3072]{1,0:T(8,128)} %in_w.1) | copy-start | bytes 4718596
  2.9 2.4 %copy-start.4 = (f32[64,2048]{1,0:T(8,128)S(1)}, f32[64,2048]{1,0:T(8,128)}, u32[]{:S(2)}) copy-start(f32[64,2048]{1,0:T(8,128)} %out_w.1) | copy-start | bytes 1572868
  5.3 0.7 copy-start.11
  6.1 102.5 %copy-start.2 = (f32[128,3072]{1,0:T(8,128)S(1)}, f32[128,3072]{1,0:T(8,128)}, u32[]{:S(2)}) copy-start(f32[128,3072]{1,0:T(8,128)} %in_m.1) | copy-start | bytes 4718596
  6.1 102.5 %copy-start.3 = (f32[128,3072]{1,0:T(8,128)S(1)}, f32[128,3072]{1,0:T(8,128)}, u32[]{:S(2)}) copy-start(f32[128,3072]{1,0:T(8,128)} %in_s.1) | copy-start | bytes 4718596
  6.1 102.5 %copy-start.5 = (f32[64,2048]{1,0:T(8,128)S(1)}, f32[64,2048]{1,0:T(8,128)}, u32[]{:S(2)}) copy-start(f32[64,2048]{1,0:T(8,128)} %out_m.1) | copy-start | bytes 1572868
  6.1 102.5 %copy-start.6 = (f32[64,2048]{1,0:T(8,128)S(1)}, f32[64,2048]{1,0:T(8,128)}, u32[]{:S(2)}) copy-start(f32[64,2048]{1,0:T(8,128)} %out_s.1) | copy-start | bytes 1572868
  6.1 102.5 %copy-start.9 = (f32[128]{0:T(128)S(1)}, f32[128]{0:T(128)}, u32[]{:S(2)}) copy-start(f32[128]{0:T(128)} %param.24) | copy-start | bytes 1540
  6.1 102.5 %copy-start.10 = (f32[128]{0:T(128)S(1)}, f32[128]{0:T(128)}, u32[]{:S(2)}) copy-start(f32[128]{0:T(128)} %param.25) | copy-start | bytes 1540

commit v6 on v5

--- a/solution.py
+++ b/solution.py
@@ -400,8 +400,8 @@
     sub_item = lax.broadcasted_iota(jnp.int32, (16, 128), 0)
 
     def backward(step, _):
-        for i in range(8):
-            b = step * 8 + i
+        for i in range(16):
+            b = step * 16 + i
             part = qkvbuf[b]
             q, k, v = part[:, :128], part[:, 128:256], part[:, 256:]
             prob = probs[b]
@@ -418,10 +418,10 @@
             push(labuf.at[p], labuf.at[p], ssem.at[LA], rsem.at[LA], plane_dev(q))
             return 0
 
-        lax.fori_loop(1 + 8 * step, 9 + 7 * step, send_la, 0)
-        return 0
-
-    lax.fori_loop(0, 2, backward, 0)
+        lax.fori_loop(1, 16, send_la, 0)
+        return 0
+
+    lax.fori_loop(0, 1, backward, 0)
 
     def scatter(k, _):
         z2 = rem(z + k, 4)
@@ -576,7 +576,7 @@
             xn[i, pl.ds(pl.multiple_of(r * 16, 16), 16), :] = (centred * scale).astype(bf16)
             return total + rows[:8] + rows[8:]
 
-        total = lax.fori_loop(0, CROP // 16, chunk, jnp.zeros((8, D), f32), unroll=4)
+        total = lax.fori_loop(0, CROP // 16, chunk, jnp.zeros((8, D), f32), unroll=8)
         mean = jnp.sum(total, axis=0, keepdims=True) * (1.0 / CROP)
         for m in range(8):
             mc[i, m : m + 1, :] = mean[:, m * SLICE : (m + 1) * SLICE]
@@ -671,7 +671,7 @@
     )(*args)
 
 
-STEPS = 4
+STEPS = 8
 
 
 def adam_kernel(
@@ -699,8 +699,8 @@
         gain_col = column[at_rows, :][:, :1]
 
         def part(j, total):
-            i, cols = j // 2, pl.ds(pl.multiple_of(j * 512, 512), 512)
-            inner = pl.ds(pl.multiple_of((j % 2) * 512, 512), 512)
+            i, cols = j, pl.ds(pl.multiple_of(j * 1024, 1024), 1024)
+            inner = pl.ds(0, 1024)
             master = in_w[at_rows, cols]
             piece = share[i, at_rows, inner].astype(f32)
             new = adam_update(
@@ -709,9 +709,9 @@
             for n in range(3):
                 in_new[n, at_rows, cols] = new[n]
             terms = piece * master.astype(bf16).astype(f32)
-            return total + sum(terms[:, n * 128 : (n + 1) * 128] for n in range(4))
-
-        total = lax.fori_loop(0, 6, part, jnp.zeros((rows, 128), f32), unroll=2)
+            return total + sum(terms[:, n * 128 : (n + 1) * 128] for n in range(8))
+
+        total = lax.fori_loop(0, 3, part, jnp.zeros((rows, 128), f32), unroll=3)
         column[at_rows, :] = jnp.broadcast_to(jnp.sum(total, axis=1, keepdims=True), (rows, 128))
         for n, ref in enumerate((new_in_w, new_in_m, new_in_s)):
             stores.append(
@@ -731,7 +731,7 @@
                 out_new[n, at_rows, cols] = new[n]
             return 0
 
-        lax.fori_loop(0, 4, out_part, 0, unroll=2)
+        lax.fori_loop(0, 4, out_part, 0, unroll=4)
         for n, ref in enumerate((new_out_w, new_out_m, new_out_s)):
             stores.append(
                 pltpu.make_async_copy(out_new.at[n, at_rows], ref.at[at_rows], osems.at[n, step])

time: 114 us -> 111 us (0.974)
  Pallas kernels: 110 us -> 107 us
where the time goes in v6:
time: 111 us
  Pallas kernels  107 us (96%)
  local copies, waits for them, and re-layouts  2.99 us (3%)
    pallas_call x1, Pallas kernels, run_kernel(): pl.pallas_call(kernel, out_shape=(jax.ShapeDtypeStruct((16, 128), f32), j...  101 us
    pallas_call x1, Pallas kernels, run_adam(): pl.pallas_call(adam_kernel, out_shape=[jax.ShapeDtypeStruct((2,), f32)] +...  4.03 us
    unnamed x26, local copies, waits for them, and re-layouts  2.99 us

profile of v6, /device:TPU:1, one launch (start us, length us, event | category | flops | bytes accessed | tf_op | source)
XLA Modules:
  0.0 111.1 jit_solution(16196390444700607193)
XLA Ops:
  0.6 0.0 copy-start.8
  0.7 0.0 copy-start.12
  0.7 0.0 copy-start
  0.7 1.6 %copy-done = bf16[2,256,2048]{2,1,0:T(8,128)(2,1)S(1)} copy-done((bf16[2,256,2048]{2,1,0:T(8,128)(2,1)S(1)}, bf16[2,256,2048]{2,1,0:T(8,128)(2,1)}, u32[]{:S(2)}) %copy-start) | copy-done | bytes 2097176
  2.3 0.0 copy-start.7
  2.3 0.7 copy-done.7
  2.9 0.0 copy-start.1
  2.9 2.0 %norm.1 = (bf16[2,128,2048]{2,1,0:T(8,128)(2,1)S(1)}, f32[2,8,256]{2,1,0:T(8,128)S(1)}) custom-call(s32[2]{0:T(128)S(1)} %copy-done.7, bf16[2,256,2048]{2,1,0:T(8,128)(2,1)S(1)} %copy-done), custom_call_target="tpu_custom_call" | custom-call | tf_op jit(solution)/shard_map/norm/pallas_call | solution.py:587
  4.9 0.0 copy-done.8
  4.9 0.0 copy-done.12
  4.9 0.0 copy-done.1
  4.9 0.0 copy-done.4
  4.9 0.0 copy-start.11
  4.9 0.7 copy-done.11
  5.6 0.0 copy-start.9
  5.7 0.0 copy-start.10
  5.7 101.4 %encoder.1 = (f32[16,128]{1,0:T(8,128)S(1)}, bf16[3,128,1024]{2,1,0:T(8,128)(2,1)S(1)}, bf16[64,2048]{1,0:T(8,128)(2,1)S(1)}) custom-call(bf16[2,128,2048]{2,1,0:T(8,128)(2,1)S(1)} %get-tuple-element.25.xn, f32[2,8,256]{2,1,0:T(8,128)S(1)} %get-tuple-element.26.mc, s32[1,256]{1,0:T(1,128)S(1)} %bitcast.11, f32[8,255]{1,0:T(8,128)S(1)} %copy-done.11, ...), custom_call_target="tpu_custom_call" | custom-call | flops 15000000512 | bytes 300000000 | tf_op jit(solution)/shard_map/encoder/pallas_call | solution.py:609
  107.0 0.0 copy-done.2
  107.1 0.0 copy-done.3
  107.1 0.0 copy-done.5
  107.1 0.0 copy-done.6
  107.1 0.0 copy-done.9
  107.1 0.0 copy-done.10
  107.1 4.0 %adam.1 = (f32[2]{0:T(128)}, f32[128,3072]{1,0:T(8,128)}, f32[128,3072]{1,0:T(8,128)}, f32[128,3072]{1,0:T(8,128)}, f32[64,2048]{1,0:T(8,128)}, /*index=5*/f32[6...) custom-call(bf16[3,128,1024]{2,1,0:T(8,128)(2,1)S(1)} %get-tuple-element.27.share, ...), custom_call_target="tpu_custom_call" | custom-call | tf_op jit(solution)/shard_map/adam/pallas_call | solution.py:751
  (5 shorter events, 0.0 us)
Async XLA Ops:
  0.6 4.2 %copy-start.8 = (f32[128]{0:T(128)S(1)}, f32[128]{0:T(128)}, u32[]{:S(2)}) copy-start(f32[128]{0:T(128)} %param.23) | copy-start | bytes 1540
  0.7 4.2 %copy-start.12 = (s32[256]{0:T(256)S(1)}, s32[256]{0:T(256)}, u32[]{:S(2)}) copy-start(s32[256]{0:T(256)} %param.15) | copy-start | bytes 3076
  0.7 1.6 %copy-start = (bf16[2,256,2048]{2,1,0:T(8,128)(2,1)S(1)}, bf16[2,256,2048]{2,1,0:T(8,128)(2,1)}, u32[]{:S(2)}) copy-start(bf16[2,256,2048]{2,1,0:T(8,128)(2,1)} %frames.1) | copy-start | bytes 6291460
  2.3 0.7 copy-start.7
  2.9 2.0 %copy-start.1 = (f32[128,3072]{1,0:T(8,128)S(1)}, f32[128,3072]{1,0:T(8,128)}, u32[]{:S(2)}) copy-start(f32[128,3072]{1,0:T(8,128)} %in_w.1) | copy-start | bytes 4718596
  2.9 2.0 %copy-start.4 = (f32[64,2048]{1,0:T(8,128)S(1)}, f32[64,2048]{1,0:T(8,128)}, u32[]{:S(2)}) copy-start(f32[64,2048]{1,0:T(8,128)} %out_w.1) | copy-start | bytes 1572868
  4.9 0.7 copy-start.11
  5.6 101.4 %copy-start.2 = (f32[128,3072]{1,0:T(8,128)S(1)}, f32[128,3072]{1,0:T(8,128)}, u32[]{:S(2)}) copy-start(f32[128,3072]{1,0:T(8,128)} %in_m.1) | copy-start | bytes 4718596
  5.6 101.4 %copy-start.3 = (f32[128,3072]{1,0:T(8,128)S(1)}, f32[128,3072]{1,0:T(8,128)}, u32[]{:S(2)}) copy-start(f32[128,3072]{1,0:T(8,128)} %in_s.1) | copy-start | bytes 4718596
  5.6 101.4 %copy-start.5 = (f32[64,2048]{1,0:T(8,128)S(1)}, f32[64,2048]{1,0:T(8,128)}, u32[]{:S(2)}) copy-start(f32[64,2048]{1,0:T(8,128)} %out_m.1) | copy-start | bytes 1572868
  5.6 101.4 %copy-start.6 = (f32[64,2048]{1,0:T(8,128)S(1)}, f32[64,2048]{1,0:T(8,128)}, u32[]{:S(2)}) copy-start(f32[64,2048]{1,0:T(8,128)} %out_s.1) | copy-start | bytes 1572868
  5.6 101.4 %copy-start.9 = (f32[128]{0:T(128)S(1)}, f32[128]{0:T(128)}, u32[]{:S(2)}) copy-start(f32[128]{0:T(128)} %param.24) | copy-start | bytes 1540
  5.7 101.4 %copy-start.10 = (f32[128]{0:T(128)S(1)}, f32[128]{0:T(128)}, u32[]{:S(2)}) copy-start(f32[128]{0:T(128)} %param.25) | copy-start | bytes 1540

commit v7 on v6

--- a/solution.py
+++ b/solution.py
@@ -331,12 +331,6 @@
         easend[q, :, 128:] = mmbuf[s // 2].astype(bf16)
     eabuf[p] = easend[p]
 
-    def send_ea(k, _):
-        q = rem(p + k, 16)
-        push(easend.at[q], eabuf.at[p], ssem.at[EA], rsem.at[EA], plane_dev(q))
-        return 0
-
-    lax.fori_loop(1, 16, send_ea, 0, unroll=True)
     await_bytes(pobuf.at[pl.ds(0, 15)], rsem.at[PO])
     everyone = pobuf[...].reshape(256, SLICE)
     parts = split(everyone)
@@ -351,6 +345,12 @@
         return 0
 
     lax.fori_loop(1, 8, send_gr, 0, unroll=True)
+    def send_ea(k, _):
+        q = rem(p + k, 16)
+        push(easend.at[q], eabuf.at[p], ssem.at[EA], rsem.at[EA], plane_dev(q))
+        return 0
+
+    lax.fori_loop(1, 16, send_ea, 0, unroll=True)
     await_bytes(grbuf.at[pl.ds(0, 7)], rsem.at[GR])
     await_bytes(ssbuf.at[pl.ds(0, 7)], rsem.at[SS])
     gram = grbuf[0]

time: 111 us -> 111 us (level)
  no operation moved by 1% of the time
where the time goes in v7:
time: 111 us
  Pallas kernels  107 us (96%)
  local copies, waits for them, and re-layouts  2.99 us (3%)
    pallas_call x1, Pallas kernels, run_kernel(): pl.pallas_call(kernel, out_shape=(jax.ShapeDtypeStruct((16, 128), f32), j...  101 us
    pallas_call x1, Pallas kernels, run_adam(): pl.pallas_call(adam_kernel, out_shape=[jax.ShapeDtypeStruct((2,), f32)] +...  4.03 us
    unnamed x26, local copies, waits for them, and re-layouts  2.99 us

profile of v7, /device:TPU:1, one launch (start us, length us, event | category | flops | bytes accessed | tf_op | source)
XLA Modules:
  0.0 110.7 jit_solution(1004378904950563153)
XLA Ops:
  0.6 0.0 copy-start.8
  0.7 0.0 copy-start.12
  0.7 0.0 copy-start
  0.7 1.6 %copy-done = bf16[2,256,2048]{2,1,0:T(8,128)(2,1)S(1)} copy-done((bf16[2,256,2048]{2,1,0:T(8,128)(2,1)S(1)}, bf16[2,256,2048]{2,1,0:T(8,128)(2,1)}, u32[]{:S(2)}) %copy-start) | copy-done | bytes 2097176
  2.3 0.0 copy-start.7
  2.3 0.7 copy-done.7
  2.9 0.0 copy-start.1
  2.9 2.0 %norm.1 = (bf16[2,128,2048]{2,1,0:T(8,128)(2,1)S(1)}, f32[2,8,256]{2,1,0:T(8,128)S(1)}) custom-call(s32[2]{0:T(128)S(1)} %copy-done.7, bf16[2,256,2048]{2,1,0:T(8,128)(2,1)S(1)} %copy-done), custom_call_target="tpu_custom_call" | custom-call | tf_op jit(solution)/shard_map/norm/pallas_call | solution.py:587
  4.9 0.0 copy-done.8
  4.9 0.0 copy-done.12
  4.9 0.0 copy-done.1
  4.9 0.0 copy-done.4
  4.9 0.0 copy-start.11
  4.9 0.7 copy-done.11
  5.6 0.0 copy-start.9
  5.7 0.0 copy-start.10
  5.7 100.9 %encoder.1 = (f32[16,128]{1,0:T(8,128)S(1)}, bf16[3,128,1024]{2,1,0:T(8,128)(2,1)S(1)}, bf16[64,2048]{1,0:T(8,128)(2,1)S(1)}) custom-call(bf16[2,128,2048]{2,1,0:T(8,128)(2,1)S(1)} %get-tuple-element.25.xn, f32[2,8,256]{2,1,0:T(8,128)S(1)} %get-tuple-element.26.mc, s32[1,256]{1,0:T(1,128)S(1)} %bitcast.11, f32[8,255]{1,0:T(8,128)S(1)} %copy-done.11, ...), custom_call_target="tpu_custom_call" | custom-call | flops 15000000512 | bytes 300000000 | tf_op jit(solution)/shard_map/encoder/pallas_call | solution.py:609
  106.6 0.0 copy-done.2
  106.6 0.0 copy-done.3
  106.6 0.0 copy-done.5
  106.6 0.0 copy-done.6
  106.7 0.0 copy-done.9
  106.7 0.0 copy-done.10
  106.7 4.0 %adam.1 = (f32[2]{0:T(128)}, f32[128,3072]{1,0:T(8,128)}, f32[128,3072]{1,0:T(8,128)}, f32[128,3072]{1,0:T(8,128)}, f32[64,2048]{1,0:T(8,128)}, /*index=5*/f32[6...) custom-call(bf16[3,128,1024]{2,1,0:T(8,128)(2,1)S(1)} %get-tuple-element.27.share, ...), custom_call_target="tpu_custom_call" | custom-call | tf_op jit(solution)/shard_map/adam/pallas_call | solution.py:751
  (5 shorter events, 0.0 us)
Async XLA Ops:
  0.6 4.2 %copy-start.8 = (f32[128]{0:T(128)S(1)}, f32[128]{0:T(128)}, u32[]{:S(2)}) copy-start(f32[128]{0:T(128)} %param.23) | copy-start | bytes 1540
  0.7 4.2 %copy-start.12 = (s32[256]{0:T(256)S(1)}, s32[256]{0:T(256)}, u32[]{:S(2)}) copy-start(s32[256]{0:T(256)} %param.15) | copy-start | bytes 3076
  0.7 1.6 %copy-start = (bf16[2,256,2048]{2,1,0:T(8,128)(2,1)S(1)}, bf16[2,256,2048]{2,1,0:T(8,128)(2,1)}, u32[]{:S(2)}) copy-start(bf16[2,256,2048]{2,1,0:T(8,128)(2,1)} %frames.1) | copy-start | bytes 6291460
  2.3 0.7 copy-start.7
  2.9 2.0 %copy-start.1 = (f32[128,3072]{1,0:T(8,128)S(1)}, f32[128,3072]{1,0:T(8,128)}, u32[]{:S(2)}) copy-start(f32[128,3072]{1,0:T(8,128)} %in_w.1) | copy-start | bytes 4718596
  2.9 2.0 %copy-start.4 = (f32[64,2048]{1,0:T(8,128)S(1)}, f32[64,2048]{1,0:T(8,128)}, u32[]{:S(2)}) copy-start(f32[64,2048]{1,0:T(8,128)} %out_w.1) | copy-start | bytes 1572868
  4.9 0.7 copy-start.11
  5.6 101.0 %copy-start.2 = (f32[128,3072]{1,0:T(8,128)S(1)}, f32[128,3072]{1,0:T(8,128)}, u32[]{:S(2)}) copy-start(f32[128,3072]{1,0:T(8,128)} %in_m.1) | copy-start | bytes 4718596
  5.6 101.0 %copy-start.3 = (f32[128,3072]{1,0:T(8,128)S(1)}, f32[128,3072]{1,0:T(8,128)}, u32[]{:S(2)}) copy-start(f32[128,3072]{1,0:T(8,128)} %in_s.1) | copy-start | bytes 4718596
  5.6 101.0 %copy-start.5 = (f32[64,2048]{1,0:T(8,128)S(1)}, f32[64,2048]{1,0:T(8,128)}, u32[]{:S(2)}) copy-start(f32[64,2048]{1,0:T(8,128)} %out_m.1) | copy-start | bytes 1572868
  5.6 101.0 %copy-start.6 = (f32[64,2048]{1,0:T(8,128)S(1)}, f32[64,2048]{1,0:T(8,128)}, u32[]{:S(2)}) copy-start(f32[64,2048]{1,0:T(8,128)} %out_s.1) | copy-start | bytes 1572868
  5.6 101.0 %copy-start.9 = (f32[128]{0:T(128)S(1)}, f32[128]{0:T(128)}, u32[]{:S(2)}) copy-start(f32[128]{0:T(128)} %param.24) | copy-start | bytes 1540
  5.7 101.0 %copy-start.10 = (f32[128]{0:T(128)S(1)}, f32[128]{0:T(128)}, u32[]{:S(2)}) copy-start(f32[128]{0:T(128)} %param.25) | copy-start | bytes 1540

commit v8 on v7

--- a/solution.py
+++ b/solution.py
@@ -397,6 +397,14 @@
         gm = gm + gmbuf[m]
     grad_mixed = gm.astype(bf16)
     labuf[p, :, SLICE:] = grad_mixed
+
+    def send_la(k, _):
+        push(
+            labuf.at[p], labuf.at[p], ssem.at[LA], rsem.at[LA], plane_dev(rem(p + k, 16))
+        )
+        return 0
+
+    lax.fori_loop(1, 16, send_la, 0, unroll=True)
     sub_item = lax.broadcasted_iota(jnp.int32, (16, 128), 0)
 
     def backward(step, _):
@@ -412,13 +420,6 @@
             grad_q = dot(dscores, k)
             grad_k = dot(dscores, q, TN)
             gp[b] = jnp.concatenate([grad_q, grad_k], axis=1).astype(bf16)
-
-        def send_la(j, _):
-            q = rem(p + j, 16)
-            push(labuf.at[p], labuf.at[p], ssem.at[LA], rsem.at[LA], plane_dev(q))
-            return 0
-
-        lax.fori_loop(1, 16, send_la, 0)
         return 0
 
     lax.fori_loop(0, 1, backward, 0)

time: 111 us -> 110 us (level)
  no operation moved by 1% of the time
where the time goes in v8:
time: 110 us
  Pallas kernels  106 us (96%)
  local copies, waits for them, and re-layouts  2.99 us (3%)
    pallas_call x1, Pallas kernels, run_kernel(): pl.pallas_call(kernel, out_shape=(jax.ShapeDtypeStruct((16, 128), f32), j...  100 us
    pallas_call x1, Pallas kernels, run_adam(): pl.pallas_call(adam_kernel, out_shape=[jax.ShapeDtypeStruct((2,), f32)] +...  4.03 us
    unnamed x26, local copies, waits for them, and re-layouts  2.99 us

profile of v8, /device:TPU:1, one launch (start us, length us, event | category | flops | bytes accessed | tf_op | source)
XLA Modules:
  0.0 110.2 jit_solution(4755269736233459616)
XLA Ops:
  0.6 0.0 copy-start.8
  0.7 0.0 copy-start.12
  0.7 0.0 copy-start
  0.7 1.6 %copy-done = bf16[2,256,2048]{2,1,0:T(8,128)(2,1)S(1)} copy-done((bf16[2,256,2048]{2,1,0:T(8,128)(2,1)S(1)}, bf16[2,256,2048]{2,1,0:T(8,128)(2,1)}, u32[]{:S(2)}) %copy-start) | copy-done | bytes 2097176
  2.3 0.0 copy-start.7
  2.3 0.7 copy-done.7
  2.9 0.0 copy-start.1
  2.9 2.0 %norm.1 = (bf16[2,128,2048]{2,1,0:T(8,128)(2,1)S(1)}, f32[2,8,256]{2,1,0:T(8,128)S(1)}) custom-call(s32[2]{0:T(128)S(1)} %copy-done.7, bf16[2,256,2048]{2,1,0:T(8,128)(2,1)S(1)} %copy-done), custom_call_target="tpu_custom_call" | custom-call | tf_op jit(solution)/shard_map/norm/pallas_call | solution.py:588
  4.9 0.0 copy-done.8
  4.9 0.0 copy-done.12
  4.9 0.0 copy-done.1
  4.9 0.0 copy-done.4
  4.9 0.0 copy-start.11
  4.9 0.7 copy-done.11
  5.6 0.0 copy-start.9
  5.7 0.0 copy-start.10
  5.7 100.5 %encoder.1 = (f32[16,128]{1,0:T(8,128)S(1)}, bf16[3,128,1024]{2,1,0:T(8,128)(2,1)S(1)}, bf16[64,2048]{1,0:T(8,128)(2,1)S(1)}) custom-call(bf16[2,128,2048]{2,1,0:T(8,128)(2,1)S(1)} %get-tuple-element.25.xn, f32[2,8,256]{2,1,0:T(8,128)S(1)} %get-tuple-element.26.mc, s32[1,256]{1,0:T(1,128)S(1)} %bitcast.11, f32[8,255]{1,0:T(8,128)S(1)} %copy-done.11, ...), custom_call_target="tpu_custom_call" | custom-call | flops 15000000512 | bytes 300000000 | tf_op jit(solution)/shard_map/encoder/pallas_call | solution.py:610
  106.1 0.0 copy-done.2
  106.2 0.0 copy-done.3
  106.2 0.0 copy-done.5
  106.2 0.0 copy-done.6
  106.2 0.0 copy-done.9
  106.2 0.0 copy-done.10
  106.2 4.0 %adam.1 = (f32[2]{0:T(128)}, f32[128,3072]{1,0:T(8,128)}, f32[128,3072]{1,0:T(8,128)}, f32[128,3072]{1,0:T(8,128)}, f32[64,2048]{1,0:T(8,128)}, /*index=5*/f32[6...) custom-call(bf16[3,128,1024]{2,1,0:T(8,128)(2,1)S(1)} %get-tuple-element.27.share, ...), custom_call_target="tpu_custom_call" | custom-call | tf_op jit(solution)/shard_map/adam/pallas_call | solution.py:752
  (5 shorter events, 0.0 us)
Async XLA Ops:
  0.6 4.2 %copy-start.8 = (f32[128]{0:T(128)S(1)}, f32[128]{0:T(128)}, u32[]{:S(2)}) copy-start(f32[128]{0:T(128)} %param.23) | copy-start | bytes 1540
  0.7 4.2 %copy-start.12 = (s32[256]{0:T(256)S(1)}, s32[256]{0:T(256)}, u32[]{:S(2)}) copy-start(s32[256]{0:T(256)} %param.15) | copy-start | bytes 3076
  0.7 1.6 %copy-start = (bf16[2,256,2048]{2,1,0:T(8,128)(2,1)S(1)}, bf16[2,256,2048]{2,1,0:T(8,128)(2,1)}, u32[]{:S(2)}) copy-start(bf16[2,256,2048]{2,1,0:T(8,128)(2,1)} %frames.1) | copy-start | bytes 6291460
  2.3 0.7 copy-start.7
  2.9 2.0 %copy-start.1 = (f32[128,3072]{1,0:T(8,128)S(1)}, f32[128,3072]{1,0:T(8,128)}, u32[]{:S(2)}) copy-start(f32[128,3072]{1,0:T(8,128)} %in_w.1) | copy-start | bytes 4718596
  2.9 2.0 %copy-start.4 = (f32[64,2048]{1,0:T(8,128)S(1)}, f32[64,2048]{1,0:T(8,128)}, u32[]{:S(2)}) copy-start(f32[64,2048]{1,0:T(8,128)} %out_w.1) | copy-start | bytes 1572868
  4.9 0.7 copy-start.11
  5.6 100.5 %copy-start.2 = (f32[128,3072]{1,0:T(8,128)S(1)}, f32[128,3072]{1,0:T(8,128)}, u32[]{:S(2)}) copy-start(f32[128,3072]{1,0:T(8,128)} %in_m.1) | copy-start | bytes 4718596
  5.6 100.5 %copy-start.3 = (f32[128,3072]{1,0:T(8,128)S(1)}, f32[128,3072]{1,0:T(8,128)}, u32[]{:S(2)}) copy-start(f32[128,3072]{1,0:T(8,128)} %in_s.1) | copy-start | bytes 4718596
  5.6 100.5 %copy-start.5 = (f32[64,2048]{1,0:T(8,128)S(1)}, f32[64,2048]{1,0:T(8,128)}, u32[]{:S(2)}) copy-start(f32[64,2048]{1,0:T(8,128)} %out_m.1) | copy-start | bytes 1572868
  5.6 100.5 %copy-start.6 = (f32[64,2048]{1,0:T(8,128)S(1)}, f32[64,2048]{1,0:T(8,128)}, u32[]{:S(2)}) copy-start(f32[64,2048]{1,0:T(8,128)} %out_s.1) | copy-start | bytes 1572868
  5.6 100.5 %copy-start.9 = (f32[128]{0:T(128)S(1)}, f32[128]{0:T(128)}, u32[]{:S(2)}) copy-start(f32[128]{0:T(128)} %param.24) | copy-start | bytes 1540
  5.7 100.5 %copy-start.10 = (f32[128]{0:T(128)S(1)}, f32[128]{0:T(128)}, u32[]{:S(2)}) copy-start(f32[128]{0:T(128)} %param.25) | copy-start | bytes 1540
